TPU v7x, 32 devices: a whole 2x2x4 slice. The times are simulated.
32 devices in a mesh: wide: 16 (over z, y, core), narrow: 2 (over x).
Axes of the slice: x: 2, y: 2, z: 4, core: 2. Of those that a mesh axis runs over, the one named last changes fastest.
Arguments:
- target: bfloat16 [65536, 512], P(('wide', 'narrow')), may hold values from -6 to 6
- memory: bfloat16 [65536, 512], P(('wide', 'narrow')), may hold values from -6 to 6
- out_grad: bfloat16 [65536, 512], P(('wide', 'narrow')), may hold values from -6 to 6
- target_segments: int32 [64, 1024], P(('wide', 'narrow')), may hold values from 0 to 24, as said below
- source_segments: int32 [64, 1024], P(('wide', 'narrow')), may hold values from 0 to 24, as said below
- target_positions: int32 [64, 1024], P(('wide', 'narrow')), may hold values from 0 to 999, as said below
- self_qkv: bfloat16 [512, 1536], P(('wide', 'narrow')), may hold values from -0.25 to 0.25
- self_out: bfloat16 [512, 512], P(('wide', 'narrow')), may hold values from -1 to 1
- cross_query: bfloat16 [512, 512], P(('wide', 'narrow')), may hold values from -0.25 to 0.25
- cross_kv: bfloat16 [512, 1024], P(('wide', 'narrow')), may hold values from -0.25 to 0.25
- cross_out: bfloat16 [512, 512], P(('wide', 'narrow')), may hold values from -1 to 1
- ffn_in: bfloat16 [512, 2048], P(('wide', 'narrow')), may hold values from -0.25 to 0.25
- ffn_out: bfloat16 [2048, 512], P(('wide', 'narrow')), may hold values from -0.125 to 0.125
- self_bias: bfloat16 [1536], P(('wide', 'narrow')), may hold values from -3 to 3
- self_gain: bfloat16 [512], P(('wide', 'narrow')), may hold values from 0.5 to 1.5
- self_shift: bfloat16 [512], P(('wide', 'narrow')), may hold values from -2 to 2
- cross_bias: bfloat16 [1536], P(('wide', 'narrow')), may hold values from -3 to 3
- cross_gain: bfloat16 [512], P(('wide', 'narrow')), may hold values from 0.5 to 1.5
- cross_shift: bfloat16 [512], P(('wide', 'narrow')), may hold values from -2 to 2
- ffn_in_bias: bfloat16 [2048], P(('wide', 'narrow')), may hold values from -3 to 3
- ffn_out_bias: bfloat16 [512], P(('wide', 'narrow')), may hold values from -2 to 2
- ffn_gain: bfloat16 [512], P(('wide', 'narrow')), may hold values from 0.5 to 1.5
- ffn_shift: bfloat16 [512], P(('wide', 'narrow')), may hold values from -2 to 2
Outputs:
- output: bfloat16 [65536, 512], P(('wide', 'narrow'))
- target_grad: bfloat16 [65536, 512], P(('wide', 'narrow'))
- memory_grad: bfloat16 [65536, 512], P(('wide', 'narrow'))
- self_qkv_grad: float32 [512, 1536], P(('wide', 'narrow'))
- self_out_grad: float32 [512, 512], P(('wide', 'narrow'))
- cross_query_grad: float32 [512, 512], P(('wide', 'narrow'))
- cross_kv_grad: float32 [512, 1024], P(('wide', 'narrow'))
- cross_out_grad: float32 [512, 512], P(('wide', 'narrow'))
- ffn_in_grad: float32 [512, 2048], P(('wide', 'narrow'))
- ffn_out_grad: float32 [2048, 512], P(('wide', 'narrow'))
- self_bias_grad: float32 [1536], P(('wide', 'narrow'))
- self_gain_grad: float32 [512], P(('wide', 'narrow'))
- self_shift_grad: float32 [512], P(('wide', 'narrow'))
- cross_bias_grad: float32 [1536], P(('wide', 'narrow'))
- cross_gain_grad: float32 [512], P(('wide', 'narrow'))
- cross_shift_grad: float32 [512], P(('wide', 'narrow'))
- ffn_in_bias_grad: float32 [2048], P(('wide', 'narrow'))
- ffn_out_bias_grad: float32 [512], P(('wide', 'narrow'))
- ffn_gain_grad: float32 [512], P(('wide', 'narrow'))
- ffn_shift_grad: float32 [512], P(('wide', 'narrow'))
Inputs may be any that keep to these rules, and one draw needn't show every extreme that they name: `target_segments`: each row holds 24 target sentences numbered 1 to 24 in order, each a run of consecutive tokens, then padding numbered 0 of 1 to 64 tokens at its end. In one row, drawn from the seed, sentences 1 to 23 have one token each and the padding is one token. `source_segments`: each row holds 24 source sentences numbered 1 to 24 in order, each a run of consecutive tokens, then padding numbered 0 of 1 to 64 tokens at its end. `target_positions`: A token's offset from the first token of its sentence (of its padding for padding tokens).
All inputs are finite; a program needn't handle non-finite values.
Results may differ from a plain program's by a relative error of at most 0.028.
Values may be sent and summed in bfloat16 or wider, within the bound.
No kernel may reach another device: no remote copies, remote signals or barrier semaphores. Data moves between devices by JAX's collectives and lax.ppermute only.
A program may use at most 256 MiB of HBM per device.

v0:
```python
import functools

import jax
import jax.numpy as jnp
from jax import lax
from jax.experimental import pallas as pl
from jax.experimental.pallas import tpu as pltpu
from jax.sharding import PartitionSpec as P

MASKED = -1e30
EPSILON = 1e-05
BLOCK = 128
WINDOW = 256
UNIT = 16
AXES = ("wide", "narrow")
NT = (((1,), (1,)), ((), ()))
TN = (((0,), (0,)), ((), ()))
NN = (((1,), (0,)), ((), ()))
BF = jnp.bfloat16
F32 = jnp.float32


def mxu(a, b, dims=NN):
    return lax.dot_general(a, b, dims, preferred_element_type=F32)


def low(x):
    return x.astype(BF)


def wide(x):
    return x.astype(F32)


def shape_of(shape, dtype=BF):
    return jax.ShapeDtypeStruct(shape, dtype)


def smem():
    return pl.BlockSpec(memory_space=pltpu.SMEM)


def vmem():
    return pl.BlockSpec(memory_space=pltpu.VMEM)


def fixed(shape, *index):
    return pl.BlockSpec(shape, lambda i, index=index: index, pipeline_mode=pl.Buffered(1))


def tiled(rows, cols, col=0):
    return pl.BlockSpec((rows, cols), lambda i, col=col: (i, col))


def params(mib):
    return pltpu.CompilerParams(vmem_limit_bytes=mib << 20)


def cost(micros):
    return pl.CostEstimate(flops=int(micros * 1e9), bytes_accessed=1 << 20, transcendentals=0)


def lane_masks(scale):
    lane = lax.broadcasted_iota(jnp.int32, (1, 128), 1)
    return low(jnp.where(lane < 64, scale, 0.0)), low(jnp.where(lane < 64, 0.0, scale))


def stacked(pair, masks):
    return jnp.concatenate([pair * masks[0], pair * masks[1]], axis=0)


def pick(both):
    sub = lax.broadcasted_iota(jnp.int32, (128, BLOCK), 0)
    return jnp.where(sub < 64, both[:, :BLOCK], both[:, BLOCK:])


def columns_of(row):
    return jnp.transpose(jnp.broadcast_to(row, (128, row.shape[1])))


def prepare_masks(causal, qseg_ref, kseg_ref, qone, kout, still):
    lane = wide(lax.broadcasted_iota(jnp.int32, (1, 128), 1))
    qone[...] = low(jnp.where(columns_of(qseg_ref[0]) == lane, 1.0, 0.0))
    kout[...] = low(jnp.where(columns_of(kseg_ref[0]) == lane, 0.0, MASKED))
    if causal:
        key = lax.broadcasted_iota(jnp.int32, (WINDOW, BLOCK), 0)
        query = lax.broadcasted_iota(jnp.int32, (WINDOW, BLOCK), 1)
        still[0] = jnp.where(key <= query, 0.0, MASKED)
        still[1] = jnp.where(key <= query + BLOCK, 0.0, MASKED)
        still[2] = jnp.zeros((WINDOW, BLOCK), F32)
        still[3] = jnp.where(key < BLOCK, 0.0, MASKED)


MASK_SCRATCH = lambda length: [pltpu.VMEM((length, 128), BF), pltpu.VMEM((length, 128), BF), pltpu.VMEM((4, WINDOW, BLOCK), F32)]


def bias_of(causal, still, qb, c, start, bound):
    if causal:
        at = jnp.minimum(qb, 1) if c is None else jnp.where(bound < WINDOW, 3, 2)
        return still[at]
    if c is None:
        return None
    key = lax.broadcasted_iota(jnp.int32, (WINDOW, BLOCK), 0) + start
    return jnp.where(key >= bound, 0.0, MASKED)


def masked(scores, bias):
    return scores if bias is None else scores + jnp.concatenate([bias, bias], axis=1)


def window(causal, first_ref, r, qb, c, length):
    c = 0 if c is None else c
    if causal:
        end = (qb + 1) * BLOCK - c * WINDOW
        return pl.multiple_of(jnp.maximum(end - WINDOW, 0), BLOCK), end
    begin = first_ref[r, qb] + c * WINDOW
    return pl.multiple_of(jnp.minimum(begin, length - WINDOW), 16), begin


def lanes_at(offset, p):
    return slice(offset + 128 * p, offset + 128 * p + 128)


UNROLL = 4


def most(extra_ref, r, qbs):
    count = extra_ref[r, qbs[0]]
    for qb in qbs[1:]:
        count = jnp.maximum(count, extra_ref[r, qb])
    return count


def attend(causal, r, first_ref, extra_ref, q, k, v, out_ref, lse_ref, masking, top, total, mix):
    length = q[0].shape[0]
    masks = lane_masks(0.125)
    joint = 2 if causal else 1
    qone, kout, still = masking

    def windows(qbs, c):
        scores, values, biases = [], [], []
        for qb in qbs:
            q0 = pl.multiple_of(qb * BLOCK, BLOCK)
            start, bound = window(causal, first_ref, r, qb, c, length)
            bias = bias_of(causal, still, qb, c, start, bound)
            queries, keys = qone[pl.ds(q0, BLOCK), :], kout[pl.ds(start, WINDOW), :]
            queries = jnp.concatenate([queries, queries], axis=0)
            for p in range(4):
                qs = jnp.concatenate([stacked(q[0][pl.ds(q0, BLOCK), lanes_at(q[1], p)], masks), queries], axis=1)
                ks = jnp.concatenate([k[0][pl.ds(start, WINDOW), lanes_at(k[1], p)], keys], axis=1)
                scores.append(mxu(ks, qs, NT))
                values.append(v[0][pl.ds(start, WINDOW), lanes_at(v[1], p)])
                biases.append(bias)
        return [masked(x, bias) for x, bias in zip(scores, biases)], values

    def step(i, _):
        qbs = [i * UNROLL + u for u in range(UNROLL)]
        scores, values = windows(qbs, None)
        highs = [jnp.max(x, axis=0, keepdims=True) for x in scores]
        weights = [jnp.exp(x - high) for x, high in zip(scores, highs)]
        sums = [jnp.sum(x, axis=0, keepdims=True) for x in weights]
        mixed = [pick(mxu(val, low(x), TN)) for val, x in zip(values, weights)]
        for n in range(4 * UNROLL):
            top[n] = highs[n]
            total[n] = sums[n]
            mix[n] = mixed[n]
        for u in range(0, UNROLL, joint):
            def more(c, _, u=u):
                scores, values = windows(qbs[u:u + joint], c + 1)
                highs = [jnp.maximum(top[4 * u + p], jnp.max(x, axis=0, keepdims=True)) for p, x in enumerate(scores)]
                weights = [jnp.exp(x - high) for x, high in zip(scores, highs)]
                mixed = [pick(mxu(val, low(x), TN)) for val, x in zip(values, weights)]
                for p in range(4 * joint):
                    n = 4 * u + p
                    fade = jnp.exp(top[n] - highs[p])
                    top[n] = highs[p]
                    total[n] = total[n] * fade + jnp.sum(weights[p], axis=0, keepdims=True)
                    mix[n] = mix[n] * pick(jnp.broadcast_to(fade, (128, 2 * BLOCK))) + mixed[p]
                return 0

            lax.fori_loop(0, most(extra_ref, r, qbs[u:u + joint]), more, 0)
        for u, qb in enumerate(qbs):
            q0 = pl.multiple_of(qb * BLOCK, BLOCK)
            for p in range(4):
                sums = total[4 * u + p]
                inverse = pick(jnp.broadcast_to(1.0 / sums, (128, 2 * BLOCK)))
                out_ref[pl.ds(q0, BLOCK), lanes_at(0, p)] = low(jnp.transpose(mix[4 * u + p] * inverse))
                lse = top[4 * u + p] + jnp.log(sums)
                lse_ref[0, 2 * p:2 * p + 1, pl.ds(q0, BLOCK)] = lse[:, :BLOCK]
                lse_ref[0, 2 * p + 1:2 * p + 2, pl.ds(q0, BLOCK)] = lse[:, BLOCK:]
        return 0

    lax.fori_loop(0, length // BLOCK // UNROLL, step, 0)


ATTEND_SCRATCH = lambda length: MASK_SCRATCH(length) + [
    pltpu.VMEM((4 * UNROLL, 1, 2 * BLOCK), F32),
    pltpu.VMEM((4 * UNROLL, 1, 2 * BLOCK), F32), pltpu.VMEM((4 * UNROLL, 128, BLOCK), F32)]


def norm(hidden):
    average = jnp.mean(hidden, axis=-1, keepdims=True)
    centred = hidden - average
    inverse = lax.rsqrt(jnp.mean(centred * centred, axis=-1, keepdims=True) + EPSILON)
    return centred * inverse, inverse


def norm_back(grad, normed, inverse, gain):
    scaled = grad * gain
    return inverse * (scaled - jnp.mean(scaled, axis=-1, keepdims=True)
                      - normed * jnp.mean(scaled * normed, axis=-1, keepdims=True))


def head_sums(grad, mix):
    lane = lax.broadcasted_iota(jnp.int32, (16, 512), 1) // 64
    heads = low(jnp.where(lane == lax.broadcasted_iota(jnp.int32, (16, 512), 0), 1.0, 0.0))
    prod = wide(grad) * wide(mix)
    upper = low(prod)
    return (mxu(heads, upper, NT) + mxu(heads, low(prod - wide(upper)), NT))[:8]


def rows_spec(t, length):
    per = length // t
    return pl.BlockSpec((1, 8, t), lambda i: (i // per, 0, i % per))


def sum_rows(x):
    return jnp.sum(wide(x), axis=0, keepdims=True)


S_BIAS, S_GAIN, S_SHIFT, C_BIAS, C_GAIN, C_SHIFT, I_BIAS, O_BIAS, F_GAIN, F_SHIFT = range(10)


def vec(ref, row, block=0, size=512):
    return ref[row:row + 1, block * size:(block + 1) * size]


def self_kernel(first_ref, extra_ref, x_ref, w_ref, vec_ref, seg_ref, qkv_ref, mix_ref, lse_ref, qone, kout, still, *state):
    r = pl.program_id(0)
    prepare_masks(True, seg_ref, seg_ref, qone, kout, still)
    x = x_ref[...]
    qkv_ref[:, :512] = low(mxu(x, w_ref[:, :512]) + vec(vec_ref, S_BIAS, 0))
    qkv_ref[:, 512:1024] = low(mxu(x, w_ref[:, 512:1024]))
    qkv_ref[:, 1024:] = low(mxu(x, w_ref[:, 1024:]) + vec(vec_ref, S_BIAS, 1))
    attend(True, r, first_ref, extra_ref, (qkv_ref, 0), (qkv_ref, 512), (qkv_ref, 1024), mix_ref, lse_ref,
           (qone, kout, still), *state)


def self_forward(plan, x, w, vectors, seg):
    rows, _, length = seg.shape
    return pl.pallas_call(
        self_kernel, grid=(rows,),
        in_specs=[smem(), smem(), tiled(length, 512), fixed((512, 1536), 0, 0), fixed((16, 2048), 0, 0),
                  pl.BlockSpec((1, 1, length), lambda i: (i, 0, 0))],
        out_specs=[tiled(length, 1536), tiled(length, 512), pl.BlockSpec((1, 8, length), lambda i: (i, 0, 0))],
        out_shape=[shape_of((rows * length, 1536)), shape_of((rows * length, 512)), shape_of((rows, 8, length), F32)],
        scratch_shapes=ATTEND_SCRATCH(length), compiler_params=params(40), cost_estimate=cost(20), name="self_forward",
    )(*plan, x, w, vectors, seg)


def cross_kernel(first_ref, extra_ref, x_ref, mix_ref, mem_ref, wo_ref, wq_ref, wkv_ref, vec_ref, qseg_ref, kseg_ref,
                 hid_ref, q_ref, kv_ref, out_ref, lse_ref, qone, kout, still, *state):
    r = pl.program_id(0)
    prepare_masks(False, qseg_ref, kseg_ref, qone, kout, still)
    hidden = wide(x_ref[...]) + mxu(mix_ref[...], wo_ref[...]) + vec(vec_ref, S_BIAS, 2)
    hid_ref[...] = hidden
    first = low(norm(hidden)[0] * vec(vec_ref, S_GAIN) + vec(vec_ref, S_SHIFT))
    q_ref[...] = low(mxu(first, wq_ref[...]) + vec(vec_ref, C_BIAS, 0))
    mem = mem_ref[...]
    kv_ref[:, :512] = low(mxu(mem, wkv_ref[:, :512]))
    kv_ref[:, 512:] = low(mxu(mem, wkv_ref[:, 512:]) + vec(vec_ref, C_BIAS, 1))
    attend(False, r, first_ref, extra_ref, (q_ref, 0), (kv_ref, 0), (kv_ref, 512), out_ref, lse_ref,
           (qone, kout, still), *state)


def cross_forward(plan, x, mix, mem, weights, vectors, qseg, kseg):
    rows, _, length = qseg.shape
    seg = pl.BlockSpec((1, 1, length), lambda i: (i, 0, 0))
    total = rows * length
    return pl.pallas_call(
        cross_kernel, grid=(rows,),
        in_specs=[smem(), smem(), tiled(length, 512), tiled(length, 512), tiled(length, 512),
                  fixed((512, 512), 0, 0), fixed((512, 512), 0, 1), fixed((512, 1024), 0, 1), fixed((16, 2048), 0, 0), seg, seg],
        out_specs=[tiled(length, 512), tiled(length, 512), tiled(length, 1024), tiled(length, 512),
                   pl.BlockSpec((1, 8, length), lambda i: (i, 0, 0))],
        out_shape=[shape_of((total, 512), F32), shape_of((total, 512)), shape_of((total, 1024)), shape_of((total, 512)),
                   shape_of((rows, 8, length), F32)],
        scratch_shapes=ATTEND_SCRATCH(length), compiler_params=params(48), cost_estimate=cost(25), name="cross_forward",
    )(*plan, x, mix, mem, weights, weights, weights, vectors, qseg, kseg)


def pair_row(ref, p, q0):
    return jnp.concatenate([ref[0, 2 * p + h:2 * p + h + 1, pl.ds(q0, BLOCK)] for h in range(2)], axis=1)


def back_kernel(causal, first_ref, extra_ref, q_ref, k_ref, v_ref, delta_ref, grad_ref, lse_ref, qseg_ref, kseg_ref, *refs):
    dq_ref, dk_ref, dv_ref, qone, kout, still, dk, dv, dq = refs[-9:]
    r = pl.program_id(0)
    length = q_ref.shape[0]
    joint = 2 if causal else 1
    prepare_masks(causal, qseg_ref, kseg_ref, qone, kout, still)
    dk[...] = jnp.zeros_like(dk)
    dv[...] = jnp.zeros_like(dv)
    masks = lane_masks(0.125)
    ones = lane_masks(1.0)

    def windows(qbs, c):
        places, qs, gs, deltas, lses, keys, biases, scores = [], [], [], [], [], [], [], []
        for qb in qbs:
            q0 = pl.multiple_of(qb * BLOCK, BLOCK)
            start, bound = window(causal, first_ref, r, qb, c, length)
            bias = bias_of(causal, still, qb, c, start, bound)
            queries, outs = qone[pl.ds(q0, BLOCK), :], kout[pl.ds(start, WINDOW), :]
            queries = jnp.concatenate([queries, queries], axis=0)
            for p in range(4):
                lanes = lanes_at(0, p)
                grad = grad_ref[pl.ds(q0, BLOCK), lanes]
                deltas.append(pair_row(delta_ref, p, q0))
                lses.append(pair_row(lse_ref, p, q0))
                qs.append(stacked(q_ref[pl.ds(q0, BLOCK), lanes], masks))
                gs.append(stacked(grad, ones))
                keys.append(k_ref[pl.ds(start, WINDOW), lanes])
                places.append((pl.ds(start, WINDOW), lanes))
                biases.append(bias)
                scores.append(mxu(jnp.concatenate([keys[-1], outs], axis=1), jnp.concatenate([qs[-1], queries], axis=1), NT))
        dprobs = [mxu(v_ref[place], g, NT) for place, g in zip(places, gs)]
        probs = [jnp.exp(masked(x, bias) - lse) for x, bias, lse in zip(scores, biases, lses)]
        dscores = [low(x * (d - delta)) for x, d, delta in zip(probs, dprobs, deltas)]
        new_dv = [mxu(low(x), g) for x, g in zip(probs, gs)]
        new_dk = [mxu(d, x) for d, x in zip(dscores, qs)]
        parts = [pick(mxu(key, d, TN)) for key, d in zip(keys, dscores)]
        for place, more_dv, more_dk in zip(places, new_dv, new_dk):
            dv[place] += more_dv
            dk[place] += more_dk
        return parts

    def step(i, _):
        qbs = [i * UNROLL + u for u in range(UNROLL)]
        for n, part in enumerate(windows(qbs, None)):
            dq[n] = part
        for u in range(0, UNROLL, joint):
            def more(c, _, u=u):
                for p, part in enumerate(windows(qbs[u:u + joint], c + 1)):
                    dq[4 * u + p] += part
                return 0

            lax.fori_loop(0, most(extra_ref, r, qbs[u:u + joint]), more, 0)
        for u, qb in enumerate(qbs):
            q0 = pl.multiple_of(qb * BLOCK, BLOCK)
            for p in range(4):
                dq_ref[pl.ds(q0, BLOCK), lanes_at(0, p)] = low(jnp.transpose(dq[4 * u + p]) * 0.125)
        return 0

    lax.fori_loop(0, length // BLOCK // UNROLL, step, 0)
    dk_ref[...] = low(dk[...])
    dv_ref[...] = low(dv[...])


def attend_back(causal, plan, q, k, v, delta, grad, lse, qseg, kseg, after=()):
    rows, _, length = qseg.shape
    seg = pl.BlockSpec((1, 1, length), lambda i: (i, 0, 0))
    line = pl.BlockSpec((1, 8, length), lambda i: (i, 0, 0))
    return pl.pallas_call(
        functools.partial(back_kernel, causal), grid=(rows,),
        in_specs=[smem(), smem(), tiled(length, 512, q[1]), tiled(length, 512, k[1]), tiled(length, 512, v[1]), line,
                  tiled(length, 512), line, seg, seg] + [pl.BlockSpec(memory_space=pl.ANY)] * len(after),
        out_specs=[tiled(length, 512)] * 3, out_shape=[shape_of((rows * length, 512))] * 3,
        scratch_shapes=MASK_SCRATCH(length) + [pltpu.VMEM((length, 512), F32), pltpu.VMEM((length, 512), F32),
                                               pltpu.VMEM((4 * UNROLL, 128, BLOCK), F32)],
        compiler_params=params(40), cost_estimate=cost(20), name="self_back" if causal else "cross_back",
    )(*plan, q[0], k[0], v[0], delta, grad, lse, qseg, kseg, *after)


def emit(outs, col, acc, index_ref, acc_col, width):
    half = outs[0].shape[0]
    for r in range(512 // UNIT):
        row = pl.multiple_of(index_ref[r] * UNIT, UNIT)
        outs[r // half][r % half, :, col:col + width] = low(acc[pl.ds(row, UNIT), acc_col:acc_col + width])


def halves(width):
    half = 512 // UNIT // 2
    return [fixed((half, UNIT, width), 0, 0, 0)] * 2, [shape_of((half, UNIT, width))] * 2


MID_TILE = 512
PARTS = 2
CHUNK = 1024


def mid_kernel(index_a, index_b, hid_ref, mix_ref, grad_ref, win_ref, gout_ref, wco_ref, vec_ref,
               out_ref, h2_ref, mg_ref, delta_ref, keep_ref, send_ref, co_ref, small_ref,
               wout, dwin, dwout, dwco, act, slope):
    step = pl.program_id(0)
    hidden_width = win_ref.shape[1]
    tokens = hid_ref.shape[0]

    @pl.when(step == 0)
    def _():
        for d in range(512 // UNIT):
            for b in range(4):
                wout[(4 * d + b) * UNIT:(4 * d + b + 1) * UNIT, :] = gout_ref[d * UNIT:(d + 1) * UNIT, 512 * b:512 * b + 512]
        dwin[...] = jnp.zeros_like(dwin)
        dwout[...] = jnp.zeros_like(dwout)
        dwco[...] = jnp.zeros_like(dwco)
        small_ref[...] = jnp.zeros_like(small_ref)

    chunks = [slice(c, c + CHUNK) for c in range(0, hidden_width, CHUNK)]
    part = tokens // PARTS
    parts = [slice(i * part, i * part + part) for i in range(PARTS)]
    firsts = [norm(hid_ref[t, :])[0] * vec(vec_ref, S_GAIN) + vec(vec_ref, S_SHIFT) for t in parts]
    norms2 = [norm(first + mxu(mix_ref[t, :], wco_ref[...]) + vec(vec_ref, C_BIAS, 2)) for t, first in zip(parts, firsts)]
    seconds = [normed * vec(vec_ref, C_GAIN) + vec(vec_ref, C_SHIFT) for normed, _ in norms2]
    lows = [low(second) for second in seconds]
    norms3 = []
    for t, second, second_low in zip(parts, seconds, lows):
        hidden3 = second + vec(vec_ref, O_BIAS)
        for c in chunks:
            pre = mxu(second_low, win_ref[:, c]) + vec_ref[I_BIAS:I_BIAS + 1, c]
            sig = 0.5 + 0.5 * jnp.tanh(0.5 * pre)
            active = low(pre * sig)
            act[t, c] = active
            slope[t, c] = sig * (1.0 + pre * (1.0 - sig))
            hidden3 += mxu(active, wout[c, :])
        norms3.append(norm(hidden3))
    backs3 = []
    for t, (normed3, inverse3) in zip(parts, norms3):
        out_ref[t, :] = low(normed3 * vec(vec_ref, F_GAIN) + vec(vec_ref, F_SHIFT))
        grad = wide(grad_ref[t, :])
        backs3.append(norm_back(grad, normed3, inverse3, vec(vec_ref, F_GAIN)))
        small_ref[2:3, :512] += sum_rows(grad * normed3)
        small_ref[3:4, :512] += sum_rows(grad)
    b3s = [low(back3) for back3 in backs3]
    us = [[] for _ in chunks]
    grads2 = []
    for t, back3, b3 in zip(parts, backs3, b3s):
        grad2 = back3
        for n, c in enumerate(chunks):
            u = low(mxu(b3, wout[c, :], NT) * slope[t, c])
            us[n].append(u)
            grad2 += mxu(u, win_ref[:, c], NT)
        grads2.append(grad2)
    b2s = []
    for t, grad2, (normed2, inverse2) in zip(parts, grads2, norms2):
        h2 = norm_back(grad2, normed2, inverse2, vec(vec_ref, C_GAIN))
        b2 = low(h2)
        h2_ref[t, :] = b2
        b2s.append(b2)
        small_ref[4:5, :512] += sum_rows(grad2 * normed2)
        small_ref[5:6, :512] += sum_rows(grad2)
    second_low = jnp.concatenate(lows, axis=0)
    b3 = jnp.concatenate(b3s, axis=0)
    second_t, b3_t = jnp.transpose(second_low), jnp.transpose(b3)
    small_ref[1:2, :512] += sum_rows(b3)
    for n, c in enumerate(chunks):
        u = jnp.concatenate(us[n], axis=0)
        dwin[:, c] += mxu(second_t, u)
        dwout[:, c] += mxu(b3_t, act[:, c])
        small_ref[0:1, c] += sum_rows(u)
    b2 = jnp.concatenate(b2s, axis=0)
    small_ref[6:7, :512] += sum_rows(b2)
    dwco[...] += mxu(jnp.transpose(mix_ref[...]), b2)
    mix_grad = low(mxu(b2, wco_ref[...], NT))
    mg_ref[...] = mix_grad
    delta_ref[0] = head_sums(mix_grad, mix_ref[...])

    @pl.when(step == pl.num_programs(0) - 1)
    def _():
        outs = keep_ref, send_ref
        emit(outs, 0, dwin, index_a, 0, hidden_width)
        for c in chunks:
            wout[c, :] = low(jnp.transpose(dwout[:, c]))
        half = keep_ref.shape[0]
        for r in range(512 // UNIT):
            for b in range(4):
                row = pl.multiple_of((index_b[r] * 4 + b) * UNIT, UNIT)
                outs[r // half][r % half, :, 2048 + 512 * b:2560 + 512 * b] = wout[pl.ds(row, UNIT), :]
        co_ref[...] = dwco[...]


def middle(index_a, index_b, hid, mix, grad, rest, vectors, length):
    total = hid.shape[0]
    t = MID_TILE
    specs, shapes = halves(4096)
    return pl.pallas_call(
        mid_kernel, grid=(total // t,),
        in_specs=[smem(), smem(), tiled(t, 512), tiled(t, 512), tiled(t, 512),
                  fixed((512, 2048), 0, 0), fixed((512, 2048), 0, 1), fixed((512, 512), 0, 8), fixed((16, 2048), 0, 0)],
        out_specs=[tiled(t, 512)] * 3 + [rows_spec(t, length)] + specs + [fixed((512, 512), 0, 0), fixed((8, 2048), 0, 0)],
        out_shape=[shape_of((total, 512))] * 3 + [shape_of((total // length, 8, length), F32)] + shapes
        + [shape_of((512, 512), F32), shape_of((8, 2048), F32)],
        scratch_shapes=[pltpu.VMEM((2048, 512), BF), pltpu.VMEM((512, 2048), F32), pltpu.VMEM((512, 2048), F32),
                        pltpu.VMEM((512, 512), F32), pltpu.VMEM((t, 2048), BF), pltpu.VMEM((t, 2048), F32)],
        compiler_params=params(56), cost_estimate=cost(40), name="middle",
    )(index_a, index_b, hid, mix, grad, rest, rest, rest, vectors)


DENSE_TILE = 512
SELF_TILE = 1024


def cross_dense_kernel(index_a, index_b, cq_ref, ck_ref, cv_ref, mem_ref, hid_ref, h2_ref, mix_ref,
                       wq_ref, wo_ref, co_ref, vec_ref,
                       h1_ref, mg_ref, delta_ref, keep_ref, send_ref, small_ref, dq, dkv, do):
    step = pl.program_id(0)

    @pl.when(step == 0)
    def _():
        dq[...] = jnp.zeros_like(dq)
        dkv[...] = jnp.zeros_like(dkv)
        do[...] = jnp.zeros_like(do)
        small_ref[...] = jnp.zeros_like(small_ref)

    cq, ck, cv = cq_ref[...], ck_ref[...], cv_ref[...]
    normed, inverse = norm(hid_ref[...])
    first = low(normed * vec(vec_ref, S_GAIN) + vec(vec_ref, S_SHIFT))
    grad1 = wide(h2_ref[...]) + mxu(cq, wq_ref[...], NT)
    h1 = norm_back(grad1, normed, inverse, vec(vec_ref, S_GAIN))
    b1 = low(h1)
    h1_ref[...] = b1
    mix_grad = low(mxu(b1, wo_ref[...], NT))
    mg_ref[...] = mix_grad
    delta_ref[0] = head_sums(mix_grad, mix_ref[...])
    dq[...] += mxu(jnp.transpose(first), cq)
    mem_t = jnp.transpose(mem_ref[...])
    dkv[:, :512] += mxu(mem_t, ck)
    dkv[:, 512:] += mxu(mem_t, cv)
    do[...] += mxu(jnp.transpose(mix_ref[...]), b1)
    small_ref[0:1, :] += sum_rows(cq)
    small_ref[1:2, :] += sum_rows(cv)
    small_ref[2:3, :] += sum_rows(grad1 * normed)
    small_ref[3:4, :] += sum_rows(grad1)
    small_ref[4:5, :] += sum_rows(b1)

    @pl.when(step == pl.num_programs(0) - 1)
    def _():
        outs = keep_ref, send_ref
        emit(outs, 0, dq, index_a, 0, 512)
        emit(outs, 512, co_ref, index_a, 0, 512)
        emit(outs, 1024, do, index_a, 0, 256)
        emit(outs, 1280, do, index_b, 256, 256)
        emit(outs, 1536, dkv, index_b, 0, 1024)


def cross_dense(index_a, index_b, grads, mem, hid, h2, mix, weights, dco, vectors, length):
    total = hid.shape[0]
    t = DENSE_TILE
    specs, shapes = halves(2560)
    return pl.pallas_call(
        cross_dense_kernel, grid=(total // t,),
        in_specs=[smem(), smem()] + [tiled(t, 512)] * 7
        + [fixed((512, 512), 0, 1), fixed((512, 512), 0, 0), fixed((512, 512), 0, 0), fixed((16, 2048), 0, 0)],
        out_specs=[tiled(t, 512)] * 2 + [rows_spec(t, length)] + specs + [fixed((8, 512), 0, 0)],
        out_shape=[shape_of((total, 512))] * 2 + [shape_of((total // length, 8, length), F32)] + shapes + [shape_of((8, 512), F32)],
        scratch_shapes=[pltpu.VMEM((512, 512), F32), pltpu.VMEM((512, 1024), F32), pltpu.VMEM((512, 512), F32)],
        compiler_params=params(40), cost_estimate=cost(12), name="cross_dense",
    )(index_a, index_b, *grads, mem, hid, h2, mix, weights, weights, dco, vectors)


def memory_kernel(ck_ref, cv_ref, w_ref, *refs):
    refs[-1][...] = low(mxu(ck_ref[...], w_ref[:, :512], NT) + mxu(cv_ref[...], w_ref[:, 512:], NT))


def memory_back(ck, cv, weights, after=()):
    total = ck.shape[0]
    t = 512
    return pl.pallas_call(
        memory_kernel, grid=(total // t,), in_specs=[tiled(t, 512)] * 2 + [fixed((512, 1024), 0, 1)]
        + [pl.BlockSpec(memory_space=pl.ANY)] * len(after),
        out_specs=tiled(t, 512), out_shape=shape_of((total, 512)), compiler_params=params(40), cost_estimate=cost(4), name="memory_grad",
    )(ck, cv, weights, *after)


VECTORS = (1536, 512, 512, 1536, 512, 512, 2048, 512, 512, 512)


def places(n, per, count, axis):
    shape = (1, n)
    at = wide(lax.broadcasted_iota(jnp.int32, shape, 1))
    owner = jnp.floor((at + 0.5) * (1.0 / per))
    return owner, at - owner * per


def one_hot(n, per):
    _, place = places(n, per, n // per, 1)
    return low(jnp.where(wide(lax.broadcasted_iota(jnp.int32, (128, n), 0)) == place, 1.0, 0.0))


def owned(n, per, count):
    owner, _ = places(n, per, count, 1)
    return wide(lax.broadcasted_iota(jnp.int32, (count, n), 0)) == owner


def self_grad_kernel(count, index_a, index_b, dq_ref, dk_ref, dv_ref, x_ref, mid_ref, small_ref, keep_ref, send_ref, lines_ref, dw, table):
    step = pl.program_id(0)

    @pl.when(step == 0)
    def _():
        dw[...] = jnp.zeros_like(dw)
        lines_ref[...] = jnp.zeros_like(lines_ref)

    x_t = jnp.transpose(x_ref[...])
    dw[:, :512] += mxu(x_t, dq_ref[...])
    dw[:, 512:1024] += mxu(x_t, dk_ref[...])
    dw[:, 1024:] += mxu(x_t, dv_ref[...])
    lines_ref[S_BIAS:S_BIAS + 1, :512] += sum_rows(dq_ref[...])
    lines_ref[S_BIAS:S_BIAS + 1, 512:1024] += sum_rows(dv_ref[...])

    @pl.when(step == pl.num_programs(0) - 1)
    def _():
        outs = keep_ref, send_ref
        emit(outs, 0, dw, index_a, 0, 768)
        emit(outs, 896, dw, index_b, 768, 768)
        for row, col, source, source_row in (
            (S_BIAS, 1024, small_ref, 4), (S_GAIN, 0, small_ref, 2), (S_SHIFT, 0, small_ref, 3),
            (C_BIAS, 0, small_ref, 0), (C_BIAS, 512, small_ref, 1), (C_BIAS, 1024, mid_ref, 6),
            (C_GAIN, 0, mid_ref, 4), (C_SHIFT, 0, mid_ref, 5),
            (O_BIAS, 0, mid_ref, 1), (F_GAIN, 0, mid_ref, 2), (F_SHIFT, 0, mid_ref, 3),
        ):
            lines_ref[row:row + 1, col:col + 512] = source[source_row:source_row + 1, :512]
        lines_ref[I_BIAS:I_BIAS + 1, :] = mid_ref[0:1, :]
        if count:
            table[...] = jnp.zeros_like(table)
            for n in (512, 1536, 2048):
                hot, mine = one_hot(n, n // count), owned(n, n // count, count)
                for j, size in enumerate(VECTORS):
                    if size == n:
                        line = jnp.broadcast_to(lines_ref[j:j + 1, :n], (count, n))
                        table[:, j, :] = mxu(low(jnp.where(mine, line, 0.0)), hot, NT)
            for r in range(count):
                outs[2 * r // count][r % (count // 2), :, 768:896] = low(table[index_a[r]])


def self_grad(count, index_a, index_b, grads, x, mid_small, small):
    total = x.shape[0]
    t = SELF_TILE
    specs, shapes = halves(1664)
    return pl.pallas_call(
        functools.partial(self_grad_kernel, count), grid=(total // t,),
        in_specs=[smem(), smem()] + [tiled(t, 512)] * 4 + [fixed((8, 2048), 0, 0), fixed((8, 512), 0, 0)],
        out_specs=specs + [fixed((16, 2048), 0, 0)],
        out_shape=shapes + [shape_of((16, 2048), F32)],
        scratch_shapes=[pltpu.VMEM((512, 1536), F32), pltpu.VMEM((max(count, 8), 16, 128), F32)],
        compiler_params=params(40), cost_estimate=cost(5), name="self_grad",
    )(index_a, index_b, *grads, x, mid_small, small)


def target_kernel(h1_ref, dq_ref, dk_ref, dv_ref, w_ref, *refs):
    out_ref = refs[-1]
    total = wide(h1_ref[...]) + mxu(dq_ref[...], w_ref[:, :512], NT)
    total += mxu(dk_ref[...], w_ref[:, 512:1024], NT)
    out_ref[...] = low(total + mxu(dv_ref[...], w_ref[:, 1024:], NT))


def target_grad(h1, grads, w, after=()):
    total = h1.shape[0]
    t = 512
    return pl.pallas_call(
        target_kernel, grid=(total // t,), in_specs=[tiled(t, 512)] * 4 + [fixed((512, 1536), 0, 0)]
        + [pl.BlockSpec(memory_space=pl.ANY)] * len(after),
        out_specs=tiled(t, 512), out_shape=shape_of((total, 512)), compiler_params=params(40), cost_estimate=cost(5), name="target_grad",
    )(h1, *grads, w, *after)


class Net:
    def __init__(self):
        self.wide = lax.axis_size("wide")
        self.narrow = lax.axis_size("narrow")
        self.count = self.wide * self.narrow
        self.wide_bits = self.wide.bit_length() - 1
        self.narrow_bits = self.narrow.bit_length() - 1
        self.bits = self.wide_bits + self.narrow_bits
        self.me = lax.axis_index("wide") * self.narrow + lax.axis_index("narrow")
        inner = list(range(self.narrow_bits))
        core, second = [self.narrow_bits], [self.narrow_bits + 1]
        far = list(range(self.narrow_bits + 2, self.bits))
        self.near = self.bits - len(far)
        self.orders = (core + second + inner + far, core + inner + second + far)

    def exchange(self, x, bit):
        if bit < self.narrow_bits:
            return lax.ppermute(x, "narrow", [(i, i ^ (1 << bit)) for i in range(self.narrow)])
        return self.across(x, 1 << bit)

    def across(self, x, mask):
        mask >>= self.narrow_bits
        return lax.ppermute(x, "wide", [(i, i ^ mask) for i in range(self.wide)])

    def far_masks(self, order):
        return [sum(((r >> s) & 1) << bit for s, bit in enumerate(order)) for r in range(1 << len(order))]

    def index(self, chain):
        order, n = self.orders[chain], self.bits
        mask = [sum(((r >> (n - 1 - s)) & 1) << bit for s, bit in enumerate(order)) for r in range(self.count)]
        return jnp.array(mask, jnp.int32) ^ self.me

    def gather_index(self, chain):
        order = self.orders[chain][::-1]
        mask = [sum(((r >> s) & 1) << bit for s, bit in enumerate(order)) for r in range(self.count)]
        return jnp.array(mask, jnp.int32) ^ self.me


def pack_kernel(*refs):
    vectors, (qkv, so, cq, ckv, co, fin, fout, packed_ref, cross_ref, rest_ref) = refs[:10], refs[10:20]
    lines, sem = refs[20:30], refs[30]
    moves = list(zip(vectors, lines))
    moves += [(qkv.at[:, :768], packed_ref.at[0, :, :768]), (qkv.at[:, 768:], packed_ref.at[0, :, 896:]), (fin, rest_ref.at[:, :2048])]
    moves += [(fout.at[UNIT * b:UNIT * b + UNIT, :], rest_ref.at[:, 2048 + 512 * b:2560 + 512 * b]) for b in range(4)]
    moves += [(co, rest_ref.at[:, 4096:]), (so, cross_ref.at[0, :, :512]),
              (cq, cross_ref.at[0, :, 512:1024]), (ckv, cross_ref.at[0, :, 1024:])]
    copies = [pltpu.make_async_copy(src, dst, sem.at[i]) for i, (src, dst) in enumerate(moves)]
    for copy in copies:
        copy.start()
    for copy in copies:
        copy.wait()
    rows = []
    for v in lines:
        line = wide(v[...])
        rows.append(jnp.concatenate([line, jnp.zeros((1, 128 - line.shape[1]), F32)], axis=1))
    rows.append(jnp.zeros((6, 128), F32))
    packed_ref[0, :, 768:896] = low(jnp.concatenate(rows, axis=0))


def unpack_kernel(count, index_a, index_b, *refs):
    n = (len(refs) - 3) // 2
    pieces_a, pieces_b, (w_ref, vec_ref, table) = refs[:n], refs[n:2 * n], refs[2 * n:]
    for pieces, index, col, width in ((pieces_a, index_a, 0, 768), (pieces_b, index_b, 768, 768)):
        r = 0
        for piece in pieces:
            for j in range(piece.shape[0]):
                owner = index[r]
                w_ref[pl.ds(pl.multiple_of(owner * UNIT, UNIT), UNIT), col:col + width] = piece[j, :, :width]
                if col == 0:
                    table[owner] = wide(piece[j, :, 768:896])
                r += 1
    vec_ref[...] = jnp.zeros_like(vec_ref)
    for n in (512, 1536, 2048):
        hot, mine = one_hot(n, n // count), owned(n, n // count, count)
        for j, size in enumerate(VECTORS):
            if size == n:
                spread = mxu(low(table[:, j, :]), hot)
                vec_ref[j:j + 1, :n] = jnp.sum(jnp.where(mine, spread, 0.0), axis=0, keepdims=True)


def place_kernel(index_a, index_b, *refs):
    n = (len(refs) - 1) // 2
    w_ref = refs[-1]
    for pieces, index, col in ((refs[:n], index_a, 0), (refs[n:2 * n], index_b, 1024)):
        r = 0
        for piece in pieces:
            for j in range(piece.shape[0]):
                row = pl.multiple_of(index[r] * UNIT, UNIT)
                w_ref[pl.ds(row, UNIT), col:col + 1024] = piece[j]
                r += 1


def gather_weights(net, small, big):
    qkv, so, cq, ckv, co, fin, fout = big
    if qkv.shape[0] % UNIT or net.bits < 5:
        small, big = lax.all_gather((small, big), AXES, axis=0, tiled=True) if net.count > 1 else (small, big)
        qkv, so, cq, ckv, co, fin, fout = big
        fout = fout.reshape(-1, 4, UNIT, 512).transpose(0, 2, 1, 3).reshape(512, 2048)
        rows = [jnp.pad(wide(v), (0, 2048 - v.shape[0])) for v in small]
        vectors = jnp.stack(rows + [jnp.zeros((2048,), F32)] * 6)
        return qkv, vectors, jnp.concatenate([fin, fout, co], axis=1), lambda x: (x, jnp.concatenate([so, cq, ckv], axis=1))
    packed, cross, rest = pl.pallas_call(
        pack_kernel, in_specs=[pl.BlockSpec(memory_space=pl.ANY)] * 17, out_specs=[vmem()] * 3,
        out_shape=[shape_of((1, UNIT, 1664)), shape_of((1, UNIT, 2048)), shape_of((UNIT, 4608))],
        scratch_shapes=[pltpu.VMEM((1, v.shape[0]), BF) for v in small] + [pltpu.SemaphoreType.DMA((21,))],
        compiler_params=params(60), cost_estimate=cost(2), name="pack",
    )(*[v[None] for v in small], *big)
    rest = lax.all_gather(rest, AXES, axis=0, tiled=True)
    orders = [order[::-1] for order in net.orders]
    far = net.bits - net.near
    masks = net.far_masks(orders[0][:far])[1:]
    everywhere = lambda x: jnp.concatenate([x] + [net.across(x, mask) for mask in masks], axis=0)
    packed = everywhere(packed)
    packed, cross = lax.optimization_barrier((packed, cross))
    cross = everywhere(cross)
    parts = [packed[:, :, :896], packed[:, :, 896:], cross[:, :, :1024], cross[:, :, 1024:]]
    orders = orders + orders
    parts = [jnp.concatenate([x, net.exchange(x, order[far])], axis=0) for x, order in zip(parts, orders)]

    def spread(pieces, s):
        got = [[net.exchange(x, order[s]) for x in chain] for chain, order in zip(pieces, orders)]
        return [chain + more for chain, more in zip(pieces, got)]

    pieces = spread(spread([[x] for x in parts[:2]], far + 1), far + 2)
    later = spread([[x] for x in parts[2:]], far + 1)
    gather_index = [net.gather_index(0), net.gather_index(1)]

    def cross_weights(values):
        held, values = lax.optimization_barrier((later, values))
        held = spread(held, far + 2)
        return values, pl.pallas_call(
            place_kernel, in_specs=[smem(), smem()] + [vmem()] * (len(held[0]) * 2), out_specs=vmem(),
            out_shape=shape_of((512, 2048)), compiler_params=params(32), cost_estimate=cost(2), name="place",
        )(*gather_index, *held[0], *held[1])

    w, vectors = pl.pallas_call(
        functools.partial(unpack_kernel, net.count), in_specs=[smem(), smem()] + [vmem()] * (len(pieces[0]) * 2), out_specs=[vmem()] * 2,
        out_shape=[shape_of((512, 1536)), shape_of((16, 2048), F32)],
        scratch_shapes=[pltpu.VMEM((net.count, 16, 128), F32)],
        compiler_params=params(40), cost_estimate=cost(2), name="unpack",
    )(*gather_index, *pieces[0], *pieces[1])
    return w, vectors, rest, cross_weights


class Reduction:
    def __init__(self, net, keep, send, cut):
        self.net, self.cut = net, cut
        self.keep, self.send = [keep], [send]
        self.stage = 0
        self.sums = None

    def state(self):
        return tuple(self.send) if self.sums is None else ()

    def start(self):
        if self.sums is not None:
            return
        if self.stage < self.net.near:
            self.got = [self.net.exchange(x, order[self.stage]) for x, order in zip(self.send, self.net.orders)]
        else:
            far = self.net.far_masks(self.net.orders[0][:self.net.near - 1:-1])
            self.got = [self.net.across(x, mask) for x, mask in zip(self.send, far[1:])]

    def add(self):
        if self.sums is not None:
            return
        self.stage += 1
        if self.stage > self.net.near:
            self.sums = sum((wide(got[0]) for got in self.got), self.keep[0][0])
            return
        sums = [wide(k) + wide(g) for k, g in zip(self.keep, self.got)]
        if self.stage == 1:
            sums = [sums[0][:, :, :self.cut], sums[0][:, :, self.cut:]]
        elif self.stage == self.net.near:
            total = jnp.concatenate(sums, axis=2)
            self.keep = [total[:1]]
            self.send = [low(total[r:r + 1]) for r in range(1, total.shape[0])]
            return
        half = sums[0].shape[0] // 2
        self.keep = [low(s[:half]) for s in sums]
        self.send = [low(s[half:]) for s in sums]


def hold(groups, values):
    waiting = [group for group in groups if group.sums is None]
    if not waiting:
        return values
    got, values = lax.optimization_barrier(([group.got for group in waiting], values))
    for group, x in zip(waiting, got):
        group.got = x
    return values


def together(groups):
    if groups:
        state = lax.optimization_barrier([(group.keep, group.send) for group in groups])
        for group, (keep, send) in zip(groups, state):
            group.keep, group.send = keep, send


def plan_self(seg, positions):
    rows, length = seg.shape
    starts = jnp.arange(0, length, BLOCK, dtype=jnp.int32)
    begin = starts[None, :] - positions[:, ::BLOCK]
    left = jnp.maximum(starts[None, :] + BLOCK - WINDOW - begin, 0)
    return jnp.zeros_like(begin), (left + WINDOW - 1) // WINDOW


def plan_cross(tseg, sseg):
    last = jnp.int32(1 << 20)
    tkey = jnp.where(tseg == 0, last, tseg)
    skey = jnp.where(sseg == 0, last, sseg)
    begin = jnp.sum(skey[:, None, :] < tkey[:, ::BLOCK, None], axis=2, dtype=jnp.int32)
    end = jnp.sum(skey[:, None, :] <= tkey[:, BLOCK - 1::BLOCK, None], axis=2, dtype=jnp.int32)
    first = (begin // 16) * 16
    return first, jnp.maximum((end - first + WINDOW - 1) // WINDOW - 1, 0)


def per_device(
    target, memory, out_grad, target_segments, source_segments, target_positions,
    self_qkv, self_out, cross_query, cross_kv, cross_out, ffn_in, ffn_out, *small,
):
    net = Net()
    rows, length = target_segments.shape
    fast = self_qkv.shape[0] % UNIT == 0 and net.bits >= 5
    self_plan = plan_self(target_segments, target_positions)
    cross_plan = plan_cross(target_segments, source_segments)
    tseg = wide(target_segments)[:, None, :]
    sseg = wide(source_segments)[:, None, :]
    w_qkv, vectors, rest, cross_weights = gather_weights(net, small, (self_qkv, self_out, cross_query, cross_kv, cross_out, ffn_in, ffn_out))
    if fast:
        index_a, index_b = net.index(0), net.index(1)
    else:
        index_a = index_b = jnp.arange(512 // UNIT, dtype=jnp.int32)

    (qkv, self_mix, self_lse), cross_w = cross_weights(tuple(self_forward(self_plan, target, w_qkv, vectors, tseg)))
    hid, cq, pairs, cross_mix, cross_lse = cross_forward(cross_plan, target, self_mix, memory, cross_w, vectors, tseg, sseg)
    output, h2, cross_mg, cross_delta, ffn_keep, ffn_send, dco, mid_small = middle(index_a, index_b, hid, cross_mix, out_grad, rest, vectors, length)

    groups = [Reduction(net, ffn_keep, ffn_send, 2048)] if fast else []

    def backward(causal, plan, q, k, v, delta, grad, lse, kseg):
        tied = tuple(x for group in groups for x in group.state())
        for group in groups:
            group.start()
        out = hold(groups, attend_back(causal, plan, q, k, v, delta, grad, lse, tseg, kseg, tied))
        for group in groups:
            group.add()
        return out

    cross_grads = backward(False, cross_plan, (cq, 0), (pairs, 0), (pairs, 1), cross_delta, cross_mg, cross_lse, sseg)
    for group in groups:
        group.start()
    h1, self_mg, self_delta, cross_keep, cross_send, small_sums = cross_dense(
        index_a, index_b, cross_grads, memory, hid, h2, self_mix, cross_w, dco, vectors, length)
    h1, self_mg, self_delta, cross_keep, cross_send, small_sums = hold(
        groups, (h1, self_mg, self_delta, cross_keep, cross_send, small_sums))
    for group in groups:
        group.add()
    if fast:
        groups.append(Reduction(net, cross_keep, cross_send, 1280))
    self_grads = backward(True, self_plan, (qkv, 0), (qkv, 1), (qkv, 2), self_delta, self_mg, self_lse, tseg)
    for group in groups:
        group.start()
    self_keep, self_send, lines = self_grad(net.count if fast else 0, index_a, index_b, self_grads, target, mid_small, small_sums)
    self_keep, self_send, lines = hold(groups, (self_keep, self_send, lines))
    for group in groups:
        group.add()

    if not fast:
        target_out = target_grad(h1, self_grads, w_qkv)
        memory_grad = memory_back(*cross_grads[1:], cross_w)
        total = lambda x: lax.psum_scatter(low(x), AXES, scatter_dimension=0, tiled=True).astype(F32) if net.count > 1 else wide(x)
        whole = lambda keep, send: jnp.concatenate([keep, send], axis=0).reshape(512, -1)
        d_self, d_cross, d_ffn = whole(self_keep, self_send), whole(cross_keep, cross_send), whole(ffn_keep, ffn_send)
        d_out = d_ffn[:, 2048:].reshape(-1, UNIT, 4, 512).transpose(0, 2, 1, 3).reshape(2048, 512)
        weights = (jnp.concatenate([d_self[:, :768], d_self[:, 896:]], axis=1), d_cross[:, 1024:1536],
                   d_cross[:, :512], d_cross[:, 1536:], d_cross[:, 512:1024], d_ffn[:, :2048], d_out)
        return (output, target_out, memory_grad, *[total(w) for w in weights], *[total(lines[j, :n]) for j, n in enumerate(VECTORS)])

    groups.append(Reduction(net, self_keep, self_send, 896))
    target_out = None
    while any(group.sums is None for group in groups):
        open_groups = [group for group in groups if group.sums is None]
        tied = tuple(x for group in open_groups for x in group.state())
        for group in open_groups:
            group.start()
        if groups[-1].stage == 1:
            target_out = target_grad(h1, self_grads, w_qkv, tied)
        if groups[-1].stage == 2:
            memory_grad = memory_back(*cross_grads[1:], cross_w, tied)
        for group in open_groups:
            group.add()
        together([group for group in open_groups if group.sums is None])
    d_ffn, d_cross, d_self = (group.sums for group in groups)
    vectors_out = [d_self[j, 768:768 + n // net.count] for j, n in enumerate(VECTORS)]
    return (
        output, target_out, memory_grad,
        jnp.concatenate([d_self[:, :768], d_self[:, 896:]], axis=1), d_cross[:, 1024:1536],
        d_cross[:, :512], d_cross[:, 1536:], d_cross[:, 512:1024],
        d_ffn[:, :2048], jnp.concatenate([d_ffn[:, 2048 + 512 * b:2560 + 512 * b] for b in range(4)], axis=0),
        *vectors_out,
    )


def solution(mesh):
    both = ("wide", "narrow")
    matrix, vector = P(both, None), P(both)
    return jax.shard_map(
        per_device, mesh=mesh,
        in_specs=(matrix,) * 13 + (vector,) * 10,
        out_specs=(matrix,) * 10 + (vector,) * 10,
        check_vma=False,
    )
```

profile of v0, /device:TPU:0, one launch (start us, length us, event | category | flops | bytes accessed | tf_op | source)
XLA Modules:
  0.0 276.2 jit_solution(9138453084816480025)
XLA Ops:
  7.3 1.9 pack.1
  9.2 5.1 %collective-permute-start.2 = (bf16[1,16,1664]{2,1,0:T(8,128)(2,1)}, bf16[1,16,1664]{2,1,0:T(8,128)(2,1)S(1)}, u32[]{:S(2)}, u32[]{:S(2)}) collective-permute-start(bf16[1,16,1664]{2,1,0:T(8,128)(2,1)} %get-tuple-element.105), channel_id=1, source_target_pairs={{0,24},{2,26},{4,28},{6,30},{8,16},{10,18},{12,20},{14,22},{16,8},... | collective-permute-start | bytes 159752 | tf_op jit(solution)/shard_map/ppermute | solution.py:687
  15.8 1.1 collective-permute-done.2
  17.0 1.8 collective-permute-done.1
  18.7 1.2 collective-permute-done
  20.8 1.8 collective-permute-start.5
  22.8 2.4 collective-permute-start.3
  26.1 1.6 collective-permute-start.14
  27.7 1.5 collective-permute-start.10
  30.0 1.9 collective-permute-start.8
  32.0 1.6 collective-permute-start.6
  35.4 1.5 collective-permute-done.6
  36.9 2.9 %collective-permute-done.15.refs_5_ = bf16[8,16,768]{2,1,0:T(8,128)(2,1)S(1)} collective-permute-done((bf16[8,16,768]{2,1,0:T(8,128)(2,1)S(1)}, bf16[8,16,768]{2,1,0:T(8,128)(2,1)S(1)}, u32[]{:S(2)}, u32[]{:S(2)}) %collective-permute-start.15) | collective-permute-done | bytes 196640 | tf_op jit(solution)/shard_map/ppermute | solution.py:682
  40.4 1.7 collective-permute-start.7
  42.1 1.4 collective-permute-start.9
  43.5 1.3 unpack.1
  45.1 14.4 %self_forward.1 = (bf16[2048,1536]{1,0:T(8,128)(2,1)S(1)}, bf16[2048,512]{1,0:T(8,128)(2,1)S(1)}, f32[2,8,1024]{2,1,0:T(8,128)S(1)}) custom-call(s32[2,8]{1,0:T(2,128)S(1)} %broadcast.64.first_ref, s32[2,8]{1,0:T(2,128)S(1)} %and_select_fusion.extra_ref, bf16[2048,512]{1,0:T(8,128)(2,1)S(1)} %copy-done.4, bf16[512,1536]{1,0:T(8,128)(2,1)S(1)} %get-tuple-element.109.w_ref, ...), custom_call_target="tpu_custom_call" | custom-call | flops 20000000000 | bytes 1048576 | tf_op jit(solution)/shard_map/self_forward/pallas_call | solution.py:251
  59.5 2.6 copy-done.16
  65.9 1.3 copy-done.7
  67.2 21.6 %cross_forward.1 = (f32[2048,512]{1,0:T(8,128)}, bf16[2048,512]{1,0:T(8,128)(2,1)S(1)}, bf16[2048,1024]{1,0:T(8,128)(2,1)}, bf16[2048,512]{1,0:T(8,128)(2,1)S(1)}, f32[2,8,1024]{2,1,0:T(8,128)S(1)}) custom-call(s32[2,8]{1,0:T(2,128)S(1)} %get-tuple-element.193.first_ref, s32[2,8]{1,0:T(2,128)S(1)} %get-tuple-element.192.extra_ref, bf16[2048,512]{1,0:T(8,128)(2,1)} %x_ref.5, ...), custom_call_target="tpu_custom_call" | custom-call | flops 24999999488 | bytes 1048576 | tf_op jit(solution)/shard_map/cross_forward/pallas_call | solution.py:280
  88.7 1.3 copy-done.19
  90.0 1.3 copy-done.22
  91.4 45.6 %middle.1 = (bf16[2048,512]{1,0:T(8,128)(2,1)}, bf16[2048,512]{1,0:T(8,128)(2,1)}, bf16[2048,512]{1,0:T(8,128)(2,1)}, f32[2,8,1024]{2,1,0:T(8,128)}, bf16[16,16,...) custom-call(s32[32]{0:T(128)} %copy-done.2, s32[32]{0:T(128)} %copy-done, ...), custom_call_target="tpu_custom_call" | custom-call | flops 40000000000 | bytes 1048576 | tf_op jit(solution)/shard_map/middle/pallas_call | solution.py:485
  137.0 1.6 copy-done.6
  138.6 1.6 copy-done.20
  140.2 1.6 copy-done.21
  142.6 19.3 %cross_back.1 = (bf16[2048,512]{1,0:T(8,128)(2,1)S(1)}, bf16[2048,512]{1,0:T(8,128)(2,1)S(1)}, bf16[2048,512]{1,0:T(8,128)(2,1)S(1)}) custom-call(s32[2,8]{1,0:T(2,128)S(1)} %get-tuple-element.193.first_ref, s32[2,8]{1,0:T(2,128)S(1)} %get-tuple-element.192.extra_ref, bf16[2048,512]{1,0:T(8,128)(2,1)S(1)} %copy-done.20, ...), custom_call_target="tpu_custom_call" | custom-call | flops 20000000000 | bytes 1048576 | tf_op jit(solution)/shard_map/cross_back/pallas_call | solution.py:363
  164.1 14.7 %cross_dense.1 = (bf16[2048,512]{1,0:T(8,128)(2,1)S(1)}, bf16[2048,512]{1,0:T(8,128)(2,1)S(1)}, f32[2,8,1024]{2,1,0:T(8,128)S(1)}, bf16[16,16,2560]{2,1,0:T(8,12...) custom-call(s32[32]{0:T(128)S(1)} %copy-done.3, s32[32]{0:T(128)S(1)} %copy-done.1, ...), custom_call_target="tpu_custom_call" | custom-call | flops 12000000000 | bytes 1048576 | tf_op jit(solution)/shard_map/cross_dense/pallas_call | solution.py:549
  179.3 1.0 collective-permute-start.25
  180.3 2.0 collective-permute-start.26
  182.3 18.9 %self_back.1 = (bf16[2048,512]{1,0:T(8,128)(2,1)S(1)}, bf16[2048,512]{1,0:T(8,128)(2,1)S(1)}, bf16[2048,512]{1,0:T(8,128)(2,1)S(1)}) custom-call(s32[2,8]{1,0:T(2,128)S(1)} %broadcast.64.first_ref, s32[2,8]{1,0:T(2,128)S(1)} %and_select_fusion.extra_ref, bf16[2048,1536]{1,0:T(8,128)(2,1)} %copy-done.16, bf16[2048,1536]{1,0:T(8,128)(2,1)} %copy-done.16, ...), custom_call_target="tpu_custom_call" | custom-call | flops 20000000000 | bytes 1048576 | tf_op jit(solution)/shard_map/self_back/pallas_call | solution.py:363
  201.5 7.4 %collective-permute-start.30 = (bf16[1,16,4096]{2,1,0:T(8,128)(2,1)S(1)}, bf16[1,16,4096]{2,1,0:T(8,128)(2,1)S(1)}, u32[]{:S(2)}, u32[]{:S(2)}) collective-permute-start(bf16[1,16,4096]{2,1,0:T(8,128)(2,1)S(1)} %get-tuple-element.206), channel_id=1, source_target_pairs={{0,24},{2,26},{4,28},{6,30},{8,16},{10,18},{12,20},{14,22},{16,8},... | collective-permute-start | bytes 393224 | tf_op jit(solution)/shard_map/ppermute | solution.py:687
  210.0 11.7 %collective-permute-start.32 = (bf16[8,16,1280]{2,1,0:T(8,128)(2,1)S(1)}, bf16[8,16,1280]{2,1,0:T(8,128)(2,1)S(1)}, u32[]{:S(2)}, u32[]{:S(2)}) collective-permute-start(bf16[8,16,1280]{2,1,0:T(8,128)(2,1)S(1)} %get-tuple-element.200), channel_id=1, source_target_pairs={{0,1},{1,0},{2,3},{3,2},{4,5},{5,4},{6,7},{7,6},{8,9},{9,8},{10,11... | collective-permute-start | bytes 983048 | tf_op jit(solution)/shard_map/ppermute | solution.py:682
  221.7 6.7 %self_grad.1 = (bf16[16,16,1664]{2,1,0:T(8,128)(2,1)S(1)}, bf16[16,16,1664]{2,1,0:T(8,128)(2,1)S(1)}, f32[16,2048]{1,0:T(8,128)}) custom-call(s32[32]{0:T(128)S(1)} %copy-done.3, s32[32]{0:T(128)S(1)} %copy-done.1, bf16[2048,512]{1,0:T(8,128)(2,1)S(1)} %get-tuple-element.156.dq_ref, bf16[2048,512]{1,0:T(8,128)(2,1)S(1)} %get-tuple-element.157.dk_ref, ...), custom_call_target="tpu_custom_call" | custom-call | flops 5000000000 | bytes 1048576 | tf_op jit(solution)/shard_map/self_grad/pallas_call | solution.py:638
  229.0 1.5 collective-permute-start.33
  232.3 2.1 collective-permute-done.33
  234.4 2.2 collective-permute-done.34
  237.1 2.2 collective-permute-start.43
  240.2 1.4 collective-permute-start.45
  242.2 1.7 collective-permute-start.36
  243.9 4.9 %target_grad.1 = bf16[2048,512]{1,0:T(8,128)(2,1)} custom-call(bf16[2048,512]{1,0:T(8,128)(2,1)S(1)} %get-tuple-element.145.h1_ref, bf16[2048,512]{1,0:T(8,128)(2,1)S(1)} %get-tuple-element.156.dq_ref, bf16[2048,512]{1,0:T(8,128)(2,1)S(1)} %get-tuple-element.157.dk_ref, bf16[2048,512]{1,0:T(8,128)(2,1)S(1)} %get-tuple-element.158.dv_ref, ...), custom_call_target="tpu_custom_call" | custom-call | flops 5000000000 | bytes 1048576 | tf_op jit(solution)/shard_map/target_grad/pallas_call | solution.py:658
  249.0 1.4 collective-permute-start.39
  252.1 1.6 collective-permute-done.39
  253.7 2.8 collective-permute-done.38
  256.6 1.4 collective-permute-start.40
  257.9 3.0 %collective-permute-start.41 = (bf16[1,16,1664]{2,1,0:T(8,128)(2,1)S(1)}, bf16[1,16,1664]{2,1,0:T(8,128)(2,1)S(1)}, u32[]{:S(2)}, u32[]{:S(2)}) collective-permute-start(bf16[1,16,1664]{2,1,0:T(8,128)(2,1)S(1)} %get-tuple-element.184), channel_id=1, source_target_pairs={{0,8},{2,10},{4,12},{6,14},{8,0},{10,2},{12,4},{14,6},{16,24},{18,... | collective-permute-start | bytes 159752 | tf_op jit(solution)/shard_map/ppermute | solution.py:687
  261.0 3.9 %memory_grad.1 = bf16[2048,512]{1,0:T(8,128)(2,1)} custom-call(bf16[2048,512]{1,0:T(8,128)(2,1)S(1)} %get-tuple-element.135.ck_ref, bf16[2048,512]{1,0:T(8,128)(2,1)S(1)} %copy-done.10, bf16[512,2048]{1,0:T(8,128)(2,1)S(1)} %copy-done.8, bf16[4,16,896]{2,1,0:T(8,128)(2,1)S(1)} %get-tuple-element.178.refs_0_, bf16[4,16,768]{2,1,0:T(8,128)(2,1)S(1)} %get-tuple-element.179.refs_1_), custom_call_target="tpu_custom_call" | custom-call | flops 4000000000 | bytes 1048576 | tf_op jit(solution)/shard_map/memory_grad/pallas_call | solution.py:567
  264.9 2.0 collective-permute-done.42
  (186 shorter events, 24.2 us)
Async XLA Ops:
  7.2 84.2 %all-gather.2.cloned.1.call-start = ((), (), s32[]{:S(2)}) async-start(), calls=%async_computation | async-start | bytes 4866048 | tf_op jit(solution)/shard_map/all_gather | solution.py:772
  9.2 7.7 %collective-permute-start.2 = (bf16[1,16,1664]{2,1,0:T(8,128)(2,1)}, bf16[1,16,1664]{2,1,0:T(8,128)(2,1)S(1)}, u32[]{:S(2)}, u32[]{:S(2)}) collective-permute-start(bf16[1,16,1664]{2,1,0:T(8,128)(2,1)} %get-tuple-element.105), channel_id=1, source_target_pairs={{0,24},{2,26},{4,28},{6,30},{8,16},{10,18},{12,20},{14,22},{16,8},... | collective-permute-start | bytes 159752 | tf_op jit(solution)/shard_map/ppermute | solution.py:687
  14.3 4.4 %collective-permute-start.1 = (bf16[1,16,1664]{2,1,0:T(8,128)(2,1)}, bf16[1,16,1664]{2,1,0:T(8,128)(2,1)S(1)}, u32[]{:S(2)}, u32[]{:S(2)}) collective-permute-start(bf16[1,16,1664]{2,1,0:T(8,128)(2,1)} %get-tuple-element.105), channel_id=1, source_target_pairs={{0,8},{2,10},{4,12},{6,14},{8,0},{10,2},{12,4},{14,6},{16,24},{18,... | collective-permute-start | bytes 159752 | tf_op jit(solution)/shard_map/ppermute | solution.py:687
  14.3 5.6 %collective-permute-start = (bf16[1,16,1664]{2,1,0:T(8,128)(2,1)}, bf16[1,16,1664]{2,1,0:T(8,128)(2,1)S(1)}, u32[]{:S(2)}, u32[]{:S(2)}) collective-permute-start(bf16[1,16,1664]{2,1,0:T(8,128)(2,1)} %get-tuple-element.105), channel_id=1, source_target_pairs={{0,16},{2,18},{4,20},{6,22},{8,24},{10,26},{12,28},{14,30},{16,0},... | collective-permute-start | bytes 159752 | tf_op jit(solution)/shard_map/ppermute | solution.py:687
  20.8 9.2 %collective-permute-start.5 = (bf16[1,16,2048]{2,1,0:T(8,128)(2,1)}, bf16[1,16,2048]{2,1,0:T(8,128)(2,1)S(1)}, u32[]{:S(2)}, u32[]{:S(2)}) collective-permute-start(bf16[1,16,2048]{2,1,0:T(8,128)(2,1)} %get-tuple-element.107), channel_id=1, source_target_pairs={{0,24},{2,26},{4,28},{6,30},{8,16},{10,18},{12,20},{14,22},{16,8},... | collective-permute-start | bytes 196616 | tf_op jit(solution)/shard_map/ppermute | solution.py:687
  22.5 7.4 %collective-permute-start.4 = (bf16[1,16,2048]{2,1,0:T(8,128)(2,1)}, bf16[1,16,2048]{2,1,0:T(8,128)(2,1)S(1)}, u32[]{:S(2)}, u32[]{:S(2)}) collective-permute-start(bf16[1,16,2048]{2,1,0:T(8,128)(2,1)} %get-tuple-element.107), channel_id=1, source_target_pairs={{0,8},{2,10},{4,12},{6,14},{8,0},{10,2},{12,4},{14,6},{16,24},{18,... | collective-permute-start | bytes 196616 | tf_op jit(solution)/shard_map/ppermute | solution.py:687
  22.8 7.2 %collective-permute-start.3 = (bf16[1,16,2048]{2,1,0:T(8,128)(2,1)}, bf16[1,16,2048]{2,1,0:T(8,128)(2,1)S(1)}, u32[]{:S(2)}, u32[]{:S(2)}) collective-permute-start(bf16[1,16,2048]{2,1,0:T(8,128)(2,1)} %get-tuple-element.107), channel_id=1, source_target_pairs={{0,16},{2,18},{4,20},{6,22},{8,24},{10,26},{12,28},{14,30},{16,0},... | collective-permute-start | bytes 196616 | tf_op jit(solution)/shard_map/ppermute | solution.py:687
  26.1 7.9 %collective-permute-start.14 = (bf16[4,16,768]{2,1,0:T(8,128)(2,1)S(1)}, bf16[4,16,768]{2,1,0:T(8,128)(2,1)S(1)}, u32[]{:S(2)}, u32[]{:S(2)}) collective-permute-start(bf16[4,16,768]{2,1,0:T(8,128)(2,1)S(1)} %slice.249), channel_id=1, source_target_pairs={{0,4},{2,6},{4,0},{6,2},{8,12},{10,14},{12,8},{14,10},{16,20},{18,... | collective-permute-start | bytes 294920 | tf_op jit(solution)/shard_map/ppermute | solution.py:687
  27.7 5.8 %collective-permute-start.10 = (bf16[4,16,896]{2,1,0:T(8,128)(2,1)S(1)}, bf16[4,16,896]{2,1,0:T(8,128)(2,1)S(1)}, u32[]{:S(2)}, u32[]{:S(2)}) collective-permute-start(bf16[4,16,896]{2,1,0:T(8,128)(2,1)S(1)} %slice.248), channel_id=1, source_target_pairs={{0,1},{1,0},{2,3},{3,2},{4,5},{5,4},{6,7},{7,6},{8,9},{9,8},{10,11... | collective-permute-start | bytes 344072 | tf_op jit(solution)/shard_map/ppermute | solution.py:682
  30.0 10.3 %collective-permute-start.8 = (bf16[4,16,1024]{2,1,0:T(8,128)(2,1)S(1)}, bf16[4,16,1024]{2,1,0:T(8,128)(2,1)S(1)}, u32[]{:S(2)}, u32[]{:S(2)}) collective-permute-start(bf16[4,16,1024]{2,1,0:T(8,128)(2,1)S(1)} %get-tuple-element.216), channel_id=1, source_target_pairs={{0,4},{2,6},{4,0},{6,2},{8,12},{10,14},{12,8},{14,10},{16,20},{18,... | collective-permute-start | bytes 393224 | tf_op jit(solution)/shard_map/ppermute | solution.py:687
  32.0 5.0 %collective-permute-start.6 = (bf16[4,16,1024]{2,1,0:T(8,128)(2,1)S(1)}, bf16[4,16,1024]{2,1,0:T(8,128)(2,1)S(1)}, u32[]{:S(2)}, u32[]{:S(2)}) collective-permute-start(bf16[4,16,1024]{2,1,0:T(8,128)(2,1)S(1)} %get-tuple-element.217), channel_id=1, source_target_pairs={{0,1},{1,0},{2,3},{3,2},{4,5},{5,4},{6,7},{7,6},{8,9},{9,8},{10,11... | collective-permute-start | bytes 393224 | tf_op jit(solution)/shard_map/ppermute | solution.py:682
  33.6 6.3 %collective-permute-start.11 = (bf16[8,16,896]{2,1,0:T(8,128)(2,1)S(1)}, bf16[8,16,896]{2,1,0:T(8,128)(2,1)S(1)}, u32[]{:S(2)}, u32[]{:S(2)}) collective-permute-start(bf16[8,16,896]{2,1,0:T(8,128)(2,1)S(1)} %pad_maximum_fusion.5.refs_0_), channel_id=1, source_target_pairs={{0,4},{2,6},{4,0},{6,2},{8,12},{10,14},{12,8},{14,10},{16,20},{18,... | collective-permute-start | bytes 688136 | tf_op jit(solution)/shard_map/ppermute | solution.py:687
  34.1 5.7 %collective-permute-start.15 = (bf16[8,16,768]{2,1,0:T(8,128)(2,1)S(1)}, bf16[8,16,768]{2,1,0:T(8,128)(2,1)S(1)}, u32[]{:S(2)}, u32[]{:S(2)}) collective-permute-start(bf16[8,16,768]{2,1,0:T(8,128)(2,1)S(1)} %pad_maximum_fusion.7.refs_4_), channel_id=1, source_target_pairs={{0,1},{1,0},{2,3},{3,2},{4,5},{5,4},{6,7},{7,6},{8,9},{9,8},{10,11... | collective-permute-start | bytes 589832 | tf_op jit(solution)/shard_map/ppermute | solution.py:682
  35.1 30.1 %copy-start = (s32[32]{0:T(128)}, s32[32]{0:T(128)S(1)}, u32[]{:S(2)}) copy-start(s32[32]{0:T(128)S(1)} %get-tuple-element.243.index_b) | copy-start | bytes 388
  35.3 6.8 %collective-permute-start.16 = (bf16[8,16,768]{2,1,0:T(8,128)(2,1)S(1)}, bf16[8,16,768]{2,1,0:T(8,128)(2,1)S(1)}, u32[]{:S(2)}, u32[]{:S(2)}) collective-permute-start(bf16[8,16,768]{2,1,0:T(8,128)(2,1)S(1)} %pad_maximum_fusion.7.refs_4_), channel_id=1, source_target_pairs={{0,2},{2,0},{4,6},{6,4},{8,10},{10,8},{12,14},{14,12},{16,18},{18,... | collective-permute-start | bytes 589832 | tf_op jit(solution)/shard_map/ppermute | solution.py:687
  36.9 6.5 %collective-permute-start.12 = (bf16[8,16,896]{2,1,0:T(8,128)(2,1)S(1)}, bf16[8,16,896]{2,1,0:T(8,128)(2,1)S(1)}, u32[]{:S(2)}, u32[]{:S(2)}) collective-permute-start(bf16[8,16,896]{2,1,0:T(8,128)(2,1)S(1)} %pad_maximum_fusion.5.refs_0_), channel_id=1, source_target_pairs={{0,2},{2,0},{4,6},{6,4},{8,10},{10,8},{12,14},{14,12},{16,18},{18,... | collective-permute-start | bytes 688136 | tf_op jit(solution)/shard_map/ppermute | solution.py:687
  39.8 3.7 %collective-permute-start.17 = (bf16[8,16,768]{2,1,0:T(8,128)(2,1)S(1)}, bf16[8,16,768]{2,1,0:T(8,128)(2,1)S(1)}, u32[]{:S(2)}, u32[]{:S(2)}) collective-permute-start(bf16[8,16,768]{2,1,0:T(8,128)(2,1)S(1)} %collective-permute-done.15.refs_5_), channel_id=1, source_target_pairs={{0,2},{2,0},{4,6},{6,4},{8,10},{10,8},{12,14},{14,12},{16,18},{18,... | collective-permute-start | bytes 589832 | tf_op jit(solution)/shard_map/ppermute | solution.py:687
  39.8 3.7 %collective-permute-start.13 = (bf16[8,16,896]{2,1,0:T(8,128)(2,1)S(1)}, bf16[8,16,896]{2,1,0:T(8,128)(2,1)S(1)}, u32[]{:S(2)}, u32[]{:S(2)}) collective-permute-start(bf16[8,16,896]{2,1,0:T(8,128)(2,1)S(1)} %collective-permute-done.11.refs_1_), channel_id=1, source_target_pairs={{0,2},{2,0},{4,6},{6,4},{8,10},{10,8},{12,14},{14,12},{16,18},{18,... | collective-permute-start | bytes 688136 | tf_op jit(solution)/shard_map/ppermute | solution.py:687
  40.4 21.7 %collective-permute-start.7 = (bf16[8,16,1024]{2,1,0:T(8,128)(2,1)S(1)}, bf16[8,16,1024]{2,1,0:T(8,128)(2,1)S(1)}, u32[]{:S(2)}, u32[]{:S(2)}) collective-permute-start(bf16[8,16,1024]{2,1,0:T(8,128)(2,1)S(1)} %pad_maximum_fusion.3.refs_0_), channel_id=1, source_target_pairs={{0,4},{2,6},{4,0},{6,2},{8,12},{10,14},{12,8},{14,10},{16,20},{18,... | collective-permute-start | bytes 786440 | tf_op jit(solution)/shard_map/ppermute | solution.py:687
  42.1 20.0 %collective-permute-start.9 = (bf16[8,16,1024]{2,1,0:T(8,128)(2,1)S(1)}, bf16[8,16,1024]{2,1,0:T(8,128)(2,1)S(1)}, u32[]{:S(2)}, u32[]{:S(2)}) collective-permute-start(bf16[8,16,1024]{2,1,0:T(8,128)(2,1)S(1)} %pad_maximum_fusion.4.refs_4_), channel_id=1, source_target_pairs={{0,1},{1,0},{2,3},{3,2},{4,5},{5,4},{6,7},{7,6},{8,9},{9,8},{10,11... | collective-permute-start | bytes 786440 | tf_op jit(solution)/shard_map/ppermute | solution.py:682
  62.1 2.0 collective-permute-start.18
  62.2 2.3 collective-permute-start.19
  62.7 2.1 collective-permute-start.20
  62.7 2.4 collective-permute-start.21
  136.9 25.0 %collective-permute-start.22 = (bf16[16,16,4096]{2,1,0:T(8,128)(2,1)}, bf16[16,16,4096]{2,1,0:T(8,128)(2,1)S(1)}, u32[]{:S(2)}, u32[]{:S(2)}) collective-permute-start(bf16[16,16,4096]{2,1,0:T(8,128)(2,1)} %get-tuple-element.124.refs_0_), channel_id=1, source_target_pairs={{0,2},{2,0},{4,6},{6,4},{8,10},{10,8},{12,14},{14,12},{16,18},{18,... | collective-permute-start | bytes 6291464 | tf_op jit(solution)/shard_map/ppermute | solution.py:687
  162.9 15.9 %collective-permute-start.24 = (bf16[8,16,2048]{2,1,0:T(8,128)(2,1)S(1)}, bf16[8,16,2048]{2,1,0:T(8,128)(2,1)S(1)}, u32[]{:S(2)}, u32[]{:S(2)}) collective-permute-start(bf16[8,16,2048]{2,1,0:T(8,128)(2,1)S(1)} %get-tuple-element.196), channel_id=1, source_target_pairs={{0,1},{1,0},{2,3},{3,2},{4,5},{5,4},{6,7},{7,6},{8,9},{9,8},{10,11... | collective-permute-start | bytes 1572872 | tf_op jit(solution)/shard_map/ppermute | solution.py:682
  163.2 15.6 %collective-permute-start.23 = (bf16[8,16,2048]{2,1,0:T(8,128)(2,1)S(1)}, bf16[8,16,2048]{2,1,0:T(8,128)(2,1)S(1)}, u32[]{:S(2)}, u32[]{:S(2)}) collective-permute-start(bf16[8,16,2048]{2,1,0:T(8,128)(2,1)S(1)} %get-tuple-element.197), channel_id=1, source_target_pairs={{0,4},{2,6},{4,0},{6,2},{8,12},{10,14},{12,8},{14,10},{16,20},{18,... | collective-permute-start | bytes 1572872 | tf_op jit(solution)/shard_map/ppermute | solution.py:687
  179.3 22.0 %collective-permute-start.25 = (bf16[4,16,2048]{2,1,0:T(8,128)(2,1)S(1)}, bf16[4,16,2048]{2,1,0:T(8,128)(2,1)S(1)}, u32[]{:S(2)}, u32[]{:S(2)}) collective-permute-start(bf16[4,16,2048]{2,1,0:T(8,128)(2,1)S(1)} %slice.312.refs_0_), channel_id=1, source_target_pairs={{0,1},{1,0},{2,3},{3,2},{4,5},{5,4},{6,7},{7,6},{8,9},{9,8},{10,11... | collective-permute-start | bytes 786440 | tf_op jit(solution)/shard_map/ppermute | solution.py:682
  180.3 21.0 %collective-permute-start.26 = (bf16[4,16,2048]{2,1,0:T(8,128)(2,1)S(1)}, bf16[4,16,2048]{2,1,0:T(8,128)(2,1)S(1)}, u32[]{:S(2)}, u32[]{:S(2)}) collective-permute-start(bf16[4,16,2048]{2,1,0:T(8,128)(2,1)S(1)} %slice.314.refs_1_), channel_id=1, source_target_pairs={{0,4},{2,6},{4,0},{6,2},{8,12},{10,14},{12,8},{14,10},{16,20},{18,... | collective-permute-start | bytes 786440 | tf_op jit(solution)/shard_map/ppermute | solution.py:687
  182.3 18.9 %collective-permute-start.27 = (bf16[16,16,2560]{2,1,0:T(8,128)(2,1)S(1)}, bf16[16,16,2560]{2,1,0:T(8,128)(2,1)S(1)}, u32[]{:S(2)}, u32[]{:S(2)}) collective-permute-start(bf16[16,16,2560]{2,1,0:T(8,128)(2,1)S(1)} %get-tuple-element.148.refs_2_), channel_id=1, source_target_pairs={{0,2},{2,0},{4,6},{6,4},{8,10},{10,8},{12,14},{14,12},{16,18},{18,... | collective-permute-start | bytes 3932168 | tf_op jit(solution)/shard_map/ppermute | solution.py:687
  201.5 26.9 %collective-permute-start.30 = (bf16[1,16,4096]{2,1,0:T(8,128)(2,1)S(1)}, bf16[1,16,4096]{2,1,0:T(8,128)(2,1)S(1)}, u32[]{:S(2)}, u32[]{:S(2)}) collective-permute-start(bf16[1,16,4096]{2,1,0:T(8,128)(2,1)S(1)} %get-tuple-element.206), channel_id=1, source_target_pairs={{0,24},{2,26},{4,28},{6,30},{8,16},{10,18},{12,20},{14,22},{16,8},... | collective-permute-start | bytes 393224 | tf_op jit(solution)/shard_map/ppermute | solution.py:687
  208.9 19.5 %collective-permute-start.29 = (bf16[1,16,4096]{2,1,0:T(8,128)(2,1)S(1)}, bf16[1,16,4096]{2,1,0:T(8,128)(2,1)S(1)}, u32[]{:S(2)}, u32[]{:S(2)}) collective-permute-start(bf16[1,16,4096]{2,1,0:T(8,128)(2,1)S(1)} %get-tuple-element.207), channel_id=1, source_target_pairs={{0,8},{2,10},{4,12},{6,14},{8,0},{10,2},{12,4},{14,6},{16,24},{18,... | collective-permute-start | bytes 393224 | tf_op jit(solution)/shard_map/ppermute | solution.py:687
  208.9 19.5 %collective-permute-start.28 = (bf16[1,16,4096]{2,1,0:T(8,128)(2,1)S(1)}, bf16[1,16,4096]{2,1,0:T(8,128)(2,1)S(1)}, u32[]{:S(2)}, u32[]{:S(2)}) collective-permute-start(bf16[1,16,4096]{2,1,0:T(8,128)(2,1)S(1)} %get-tuple-element.208), channel_id=1, source_target_pairs={{0,16},{2,18},{4,20},{6,22},{8,24},{10,26},{12,28},{14,30},{16,0},... | collective-permute-start | bytes 393224 | tf_op jit(solution)/shard_map/ppermute | solution.py:687
  210.0 18.4 %collective-permute-start.32 = (bf16[8,16,1280]{2,1,0:T(8,128)(2,1)S(1)}, bf16[8,16,1280]{2,1,0:T(8,128)(2,1)S(1)}, u32[]{:S(2)}, u32[]{:S(2)}) collective-permute-start(bf16[8,16,1280]{2,1,0:T(8,128)(2,1)S(1)} %get-tuple-element.200), channel_id=1, source_target_pairs={{0,1},{1,0},{2,3},{3,2},{4,5},{5,4},{6,7},{7,6},{8,9},{9,8},{10,11... | collective-permute-start | bytes 983048 | tf_op jit(solution)/shard_map/ppermute | solution.py:682
  221.7 7.2 %collective-permute-start.31 = (bf16[8,16,1280]{2,1,0:T(8,128)(2,1)S(1)}, bf16[8,16,1280]{2,1,0:T(8,128)(2,1)S(1)}, u32[]{:S(2)}, u32[]{:S(2)}) collective-permute-start(bf16[8,16,1280]{2,1,0:T(8,128)(2,1)S(1)} %get-tuple-element.201), channel_id=1, source_target_pairs={{0,4},{2,6},{4,0},{6,2},{8,12},{10,14},{12,8},{14,10},{16,20},{18,... | collective-permute-start | bytes 983048 | tf_op jit(solution)/shard_map/ppermute | solution.py:687
  229.0 5.4 %collective-permute-start.33 = (bf16[4,16,1280]{2,1,0:T(8,128)(2,1)S(1)}, bf16[4,16,1280]{2,1,0:T(8,128)(2,1)S(1)}, u32[]{:S(2)}, u32[]{:S(2)}) collective-permute-start(bf16[4,16,1280]{2,1,0:T(8,128)(2,1)S(1)} %slice.324), channel_id=1, source_target_pairs={{0,1},{1,0},{2,3},{3,2},{4,5},{5,4},{6,7},{7,6},{8,9},{9,8},{10,11... | collective-permute-start | bytes 491528 | tf_op jit(solution)/shard_map/ppermute | solution.py:682
  231.2 5.4 %collective-permute-start.34 = (bf16[4,16,1280]{2,1,0:T(8,128)(2,1)S(1)}, bf16[4,16,1280]{2,1,0:T(8,128)(2,1)S(1)}, u32[]{:S(2)}, u32[]{:S(2)}) collective-permute-start(bf16[4,16,1280]{2,1,0:T(8,128)(2,1)S(1)} %slice.327), channel_id=1, source_target_pairs={{0,4},{2,6},{4,0},{6,2},{8,12},{10,14},{12,8},{14,10},{16,20},{18,... | collective-permute-start | bytes 491528 | tf_op jit(solution)/shard_map/ppermute | solution.py:687
  231.7 5.1 %collective-permute-start.35 = (bf16[16,16,1664]{2,1,0:T(8,128)(2,1)S(1)}, bf16[16,16,1664]{2,1,0:T(8,128)(2,1)S(1)}, u32[]{:S(2)}, u32[]{:S(2)}) collective-permute-start(bf16[16,16,1664]{2,1,0:T(8,128)(2,1)S(1)} %get-tuple-element.170), channel_id=1, source_target_pairs={{0,2},{2,0},{4,6},{6,4},{8,10},{10,8},{12,14},{14,12},{16,18},{18,... | collective-permute-start | bytes 2555912 | tf_op jit(solution)/shard_map/ppermute | solution.py:687
  237.1 11.6 %collective-permute-start.43 = (bf16[1,16,2560]{2,1,0:T(8,128)(2,1)S(1)}, bf16[1,16,2560]{2,1,0:T(8,128)(2,1)S(1)}, u32[]{:S(2)}, u32[]{:S(2)}) collective-permute-start(bf16[1,16,2560]{2,1,0:T(8,128)(2,1)S(1)} %get-tuple-element.171.refs_0_), channel_id=1, source_target_pairs={{0,16},{2,18},{4,20},{6,22},{8,24},{10,26},{12,28},{14,30},{16,0},... | collective-permute-start | bytes 245768 | tf_op jit(solution)/shard_map/ppermute | solution.py:687
  239.3 9.4 %collective-permute-start.44 = (bf16[1,16,2560]{2,1,0:T(8,128)(2,1)S(1)}, bf16[1,16,2560]{2,1,0:T(8,128)(2,1)S(1)}, u32[]{:S(2)}, u32[]{:S(2)}) collective-permute-start(bf16[1,16,2560]{2,1,0:T(8,128)(2,1)S(1)} %get-tuple-element.172.refs_1_), channel_id=1, source_target_pairs={{0,8},{2,10},{4,12},{6,14},{8,0},{10,2},{12,4},{14,6},{16,24},{18,... | collective-permute-start | bytes 245768 | tf_op jit(solution)/shard_map/ppermute | solution.py:687
  240.2 8.6 %collective-permute-start.45 = (bf16[1,16,2560]{2,1,0:T(8,128)(2,1)S(1)}, bf16[1,16,2560]{2,1,0:T(8,128)(2,1)S(1)}, u32[]{:S(2)}, u32[]{:S(2)}) collective-permute-start(bf16[1,16,2560]{2,1,0:T(8,128)(2,1)S(1)} %get-tuple-element.173.refs_2_), channel_id=1, source_target_pairs={{0,24},{2,26},{4,28},{6,30},{8,16},{10,18},{12,20},{14,22},{16,8},... | collective-permute-start | bytes 245768 | tf_op jit(solution)/shard_map/ppermute | solution.py:687
  241.6 7.2 %collective-permute-start.37 = (bf16[8,16,768]{2,1,0:T(8,128)(2,1)S(1)}, bf16[8,16,768]{2,1,0:T(8,128)(2,1)S(1)}, u32[]{:S(2)}, u32[]{:S(2)}) collective-permute-start(bf16[8,16,768]{2,1,0:T(8,128)(2,1)S(1)} %get-tuple-element.175.refs_4_), channel_id=1, source_target_pairs={{0,1},{1,0},{2,3},{3,2},{4,5},{5,4},{6,7},{7,6},{8,9},{9,8},{10,11... | collective-permute-start | bytes 589832 | tf_op jit(solution)/shard_map/ppermute | solution.py:682
  242.2 6.7 %collective-permute-start.36 = (bf16[8,16,896]{2,1,0:T(8,128)(2,1)S(1)}, bf16[8,16,896]{2,1,0:T(8,128)(2,1)S(1)}, u32[]{:S(2)}, u32[]{:S(2)}) collective-permute-start(bf16[8,16,896]{2,1,0:T(8,128)(2,1)S(1)} %get-tuple-element.174.refs_3_), channel_id=1, source_target_pairs={{0,4},{2,6},{4,0},{6,2},{8,12},{10,14},{12,8},{14,10},{16,20},{18,... | collective-permute-start | bytes 688136 | tf_op jit(solution)/shard_map/ppermute | solution.py:687
  249.0 4.7 %collective-permute-start.39 = (bf16[4,16,768]{2,1,0:T(8,128)(2,1)S(1)}, bf16[4,16,768]{2,1,0:T(8,128)(2,1)S(1)}, u32[]{:S(2)}, u32[]{:S(2)}) collective-permute-start(bf16[4,16,768]{2,1,0:T(8,128)(2,1)S(1)} %get-tuple-element.179.refs_1_), channel_id=1, source_target_pairs={{0,4},{2,6},{4,0},{6,2},{8,12},{10,14},{12,8},{14,10},{16,20},{18,... | collective-permute-start | bytes 294920 | tf_op jit(solution)/shard_map/ppermute | solution.py:687
  251.7 4.8 %collective-permute-start.38 = (bf16[4,16,896]{2,1,0:T(8,128)(2,1)S(1)}, bf16[4,16,896]{2,1,0:T(8,128)(2,1)S(1)}, u32[]{:S(2)}, u32[]{:S(2)}) collective-permute-start(bf16[4,16,896]{2,1,0:T(8,128)(2,1)S(1)} %get-tuple-element.178.refs_0_), channel_id=1, source_target_pairs={{0,1},{1,0},{2,3},{3,2},{4,5},{5,4},{6,7},{7,6},{8,9},{9,8},{10,11... | collective-permute-start | bytes 344072 | tf_op jit(solution)/shard_map/ppermute | solution.py:682
  256.6 8.4 %collective-permute-start.40 = (bf16[1,16,1664]{2,1,0:T(8,128)(2,1)S(1)}, bf16[1,16,1664]{2,1,0:T(8,128)(2,1)S(1)}, u32[]{:S(2)}, u32[]{:S(2)}) collective-permute-start(bf16[1,16,1664]{2,1,0:T(8,128)(2,1)S(1)} %get-tuple-element.183), channel_id=1, source_target_pairs={{0,16},{2,18},{4,20},{6,22},{8,24},{10,26},{12,28},{14,30},{16,0},... | collective-permute-start | bytes 159752 | tf_op jit(solution)/shard_map/ppermute | solution.py:687
  257.9 7.0 %collective-permute-start.41 = (bf16[1,16,1664]{2,1,0:T(8,128)(2,1)S(1)}, bf16[1,16,1664]{2,1,0:T(8,128)(2,1)S(1)}, u32[]{:S(2)}, u32[]{:S(2)}) collective-permute-start(bf16[1,16,1664]{2,1,0:T(8,128)(2,1)S(1)} %get-tuple-element.184), channel_id=1, source_target_pairs={{0,8},{2,10},{4,12},{6,14},{8,0},{10,2},{12,4},{14,6},{16,24},{18,... | collective-permute-start | bytes 159752 | tf_op jit(solution)/shard_map/ppermute | solution.py:687
  261.0 5.9 %collective-permute-start.42 = (bf16[1,16,1664]{2,1,0:T(8,128)(2,1)S(1)}, bf16[1,16,1664]{2,1,0:T(8,128)(2,1)S(1)}, u32[]{:S(2)}, u32[]{:S(2)}) collective-permute-start(bf16[1,16,1664]{2,1,0:T(8,128)(2,1)S(1)} %get-tuple-element.185), channel_id=1, source_target_pairs={{0,24},{2,26},{4,28},{6,30},{8,16},{10,18},{12,20},{14,22},{16,8},... | collective-permute-start | bytes 159752 | tf_op jit(solution)/shard_map/ppermute | solution.py:687
  (28 other events, 234.8 us)
Sparse Core Ops, SparseCore 0:
  11.5 70.1 all-gather.1
where the time goes:
time: 276 us
  Pallas kernels  154 us (56%)
  starting transfers between devices  61 us (22%)
  waiting for transfers between devices  22.1 us (8%)
  local copies, waits for them, and re-layouts  19.2 us (7%)
  between operations  15.1 us (5%)
  other arithmetic  5.15 us (2%)
    pallas_call x1, Pallas kernels, middle(): pl.pallas_call(mid_kernel, grid=(total // t,), in_specs=[smem(), smem(),...  45.6 us
    ppermute x36, starting transfers between devices, across(): return lax.ppermute(x, 'wide', [(i, i ^ mask) for i in range(self.wide)])  40 us
    pallas_call x2, Pallas kernels, attend_back(): pl.pallas_call(functools.partial(back_kernel, causal), grid=(rows,), in_s...  38.2 us
    pallas_call x1, Pallas kernels, cross_forward(): pl.pallas_call(cross_kernel, grid=(rows,), in_specs=[smem(), smem(), tile...  21.6 us
    ppermute x10, starting transfers between devices, exchange(): lax.ppermute(x, 'narrow', [(i, i ^ 1 << bit) for i in range(self.narrow)])  20.9 us
    pallas_call x1, Pallas kernels, cross_dense(): pl.pallas_call(cross_dense_kernel, grid=(total // t,), in_specs=[smem(),...  14.7 us
    pallas_call x1, Pallas kernels, self_forward(): pl.pallas_call(self_kernel, grid=(rows,), in_specs=[smem(), smem(), tiled...  14.4 us
    unnamed x61, local copies, waits for them, and re-layouts  14.2 us
  transfers between devices with their start and end apart: 47, of which 16 were waited for; matrix products, arithmetic and copies ran while one was open for 2% of the time, Pallas kernels for 38%

commit v1 on v0

--- a/solution.py
+++ b/solution.py
@@ -214,14 +214,16 @@
 def head_sums(grad, mix):
     lane = lax.broadcasted_iota(jnp.int32, (16, 512), 1) // 64
     heads = low(jnp.where(lane == lax.broadcasted_iota(jnp.int32, (16, 512), 0), 1.0, 0.0))
-    prod = wide(grad) * wide(mix)
-    upper = low(prod)
-    return (mxu(heads, upper, NT) + mxu(heads, low(prod - wide(upper)), NT))[:8]
+    return mxu(heads, low(wide(grad) * wide(mix)), NT)[:8]
 
 
 def rows_spec(t, length):
     per = length // t
     return pl.BlockSpec((1, 8, t), lambda i: (i // per, 0, i % per))
+
+
+def accumulate(ref, where, value):
+    ref[where] = jnp.where(pl.program_id(0) == 0, 0.0, ref[where]) + value
 
 
 def sum_rows(x):
@@ -253,7 +255,7 @@
         in_specs=[smem(), smem(), tiled(length, 512), fixed((512, 1536), 0, 0), fixed((16, 2048), 0, 0),
                   pl.BlockSpec((1, 1, length), lambda i: (i, 0, 0))],
         out_specs=[tiled(length, 1536), tiled(length, 512), pl.BlockSpec((1, 8, length), lambda i: (i, 0, 0))],
-        out_shape=[shape_of((rows * length, 1536)), shape_of((rows * length, 512)), shape_of((rows, 8, length), F32)],
+        out_shape=[pltpu.HBM((rows * length, 1536), BF), pltpu.HBM((rows * length, 512), BF), shape_of((rows, 8, length), F32)],
         scratch_shapes=ATTEND_SCRATCH(length), compiler_params=params(40), cost_estimate=cost(20), name="self_forward",
     )(*plan, x, w, vectors, seg)
 
@@ -263,7 +265,7 @@
     r = pl.program_id(0)
     prepare_masks(False, qseg_ref, kseg_ref, qone, kout, still)
     hidden = wide(x_ref[...]) + mxu(mix_ref[...], wo_ref[...]) + vec(vec_ref, S_BIAS, 2)
-    hid_ref[...] = hidden
+    hid_ref[...] = low(hidden)
     first = low(norm(hidden)[0] * vec(vec_ref, S_GAIN) + vec(vec_ref, S_SHIFT))
     q_ref[...] = low(mxu(first, wq_ref[...]) + vec(vec_ref, C_BIAS, 0))
     mem = mem_ref[...]
@@ -283,9 +285,9 @@
                   fixed((512, 512), 0, 0), fixed((512, 512), 0, 1), fixed((512, 1024), 0, 1), fixed((16, 2048), 0, 0), seg, seg],
         out_specs=[tiled(length, 512), tiled(length, 512), tiled(length, 1024), tiled(length, 512),
                    pl.BlockSpec((1, 8, length), lambda i: (i, 0, 0))],
-        out_shape=[shape_of((total, 512), F32), shape_of((total, 512)), shape_of((total, 1024)), shape_of((total, 512)),
+        out_shape=[shape_of((total, 512)), shape_of((total, 512)), shape_of((total, 1024)), shape_of((total, 512)),
                    shape_of((rows, 8, length), F32)],
-        scratch_shapes=ATTEND_SCRATCH(length), compiler_params=params(48), cost_estimate=cost(25), name="cross_forward",
+        scratch_shapes=ATTEND_SCRATCH(length), compiler_params=params(60), cost_estimate=cost(25), name="cross_forward",
     )(*plan, x, mix, mem, weights, weights, weights, vectors, qseg, kseg)
 
 
@@ -367,7 +369,7 @@
         out_specs=[tiled(length, 512)] * 3, out_shape=[shape_of((rows * length, 512))] * 3,
         scratch_shapes=MASK_SCRATCH(length) + [pltpu.VMEM((length, 512), F32), pltpu.VMEM((length, 512), F32),
                                                pltpu.VMEM((4 * UNROLL, 128, BLOCK), F32)],
-        compiler_params=params(40), cost_estimate=cost(20), name="self_back" if causal else "cross_back",
+        compiler_params=params(40 if causal else 60), cost_estimate=cost(20), name="self_back" if causal else "cross_back",
     )(*plan, q[0], k[0], v[0], delta, grad, lse, qseg, kseg, *after)
 
 
@@ -400,15 +402,12 @@
         for d in range(512 // UNIT):
             for b in range(4):
                 wout[(4 * d + b) * UNIT:(4 * d + b + 1) * UNIT, :] = gout_ref[d * UNIT:(d + 1) * UNIT, 512 * b:512 * b + 512]
-        dwin[...] = jnp.zeros_like(dwin)
-        dwout[...] = jnp.zeros_like(dwout)
-        dwco[...] = jnp.zeros_like(dwco)
         small_ref[...] = jnp.zeros_like(small_ref)
 
     chunks = [slice(c, c + CHUNK) for c in range(0, hidden_width, CHUNK)]
     part = tokens // PARTS
     parts = [slice(i * part, i * part + part) for i in range(PARTS)]
-    firsts = [norm(hid_ref[t, :])[0] * vec(vec_ref, S_GAIN) + vec(vec_ref, S_SHIFT) for t in parts]
+    firsts = [norm(wide(hid_ref[t, :]))[0] * vec(vec_ref, S_GAIN) + vec(vec_ref, S_SHIFT) for t in parts]
     norms2 = [norm(first + mxu(mix_ref[t, :], wco_ref[...]) + vec(vec_ref, C_BIAS, 2)) for t, first in zip(parts, firsts)]
     seconds = [normed * vec(vec_ref, C_GAIN) + vec(vec_ref, C_SHIFT) for normed, _ in norms2]
     lows = [low(second) for second in seconds]
@@ -450,16 +449,16 @@
         small_ref[5:6, :512] += sum_rows(grad2)
     second_low = jnp.concatenate(lows, axis=0)
     b3 = jnp.concatenate(b3s, axis=0)
-    second_t, b3_t = jnp.transpose(second_low), jnp.transpose(b3)
+    second_t = jnp.transpose(second_low)
     small_ref[1:2, :512] += sum_rows(b3)
     for n, c in enumerate(chunks):
         u = jnp.concatenate(us[n], axis=0)
-        dwin[:, c] += mxu(second_t, u)
-        dwout[:, c] += mxu(b3_t, act[:, c])
+        accumulate(dwin, (slice(None), c), mxu(second_t, u))
+        accumulate(dwout, (c, slice(None)), mxu(act[:, c], b3, TN))
         small_ref[0:1, c] += sum_rows(u)
     b2 = jnp.concatenate(b2s, axis=0)
     small_ref[6:7, :512] += sum_rows(b2)
-    dwco[...] += mxu(jnp.transpose(mix_ref[...]), b2)
+    accumulate(dwco, ..., mxu(jnp.transpose(mix_ref[...]), b2))
     mix_grad = low(mxu(b2, wco_ref[...], NT))
     mg_ref[...] = mix_grad
     delta_ref[0] = head_sums(mix_grad, mix_ref[...])
@@ -468,13 +467,11 @@
     def _():
         outs = keep_ref, send_ref
         emit(outs, 0, dwin, index_a, 0, hidden_width)
-        for c in chunks:
-            wout[c, :] = low(jnp.transpose(dwout[:, c]))
         half = keep_ref.shape[0]
         for r in range(512 // UNIT):
             for b in range(4):
                 row = pl.multiple_of((index_b[r] * 4 + b) * UNIT, UNIT)
-                outs[r // half][r % half, :, 2048 + 512 * b:2560 + 512 * b] = wout[pl.ds(row, UNIT), :]
+                outs[r // half][r % half, :, 2048 + 512 * b:2560 + 512 * b] = low(dwout[pl.ds(row, UNIT), :])
         co_ref[...] = dwco[...]
 
 
@@ -489,9 +486,9 @@
         out_specs=[tiled(t, 512)] * 3 + [rows_spec(t, length)] + specs + [fixed((512, 512), 0, 0), fixed((8, 2048), 0, 0)],
         out_shape=[shape_of((total, 512))] * 3 + [shape_of((total // length, 8, length), F32)] + shapes
         + [shape_of((512, 512), F32), shape_of((8, 2048), F32)],
-        scratch_shapes=[pltpu.VMEM((2048, 512), BF), pltpu.VMEM((512, 2048), F32), pltpu.VMEM((512, 2048), F32),
+        scratch_shapes=[pltpu.VMEM((2048, 512), BF), pltpu.VMEM((512, 2048), F32), pltpu.VMEM((2048, 512), F32),
                         pltpu.VMEM((512, 512), F32), pltpu.VMEM((t, 2048), BF), pltpu.VMEM((t, 2048), F32)],
-        compiler_params=params(56), cost_estimate=cost(40), name="middle",
+        compiler_params=params(62), cost_estimate=cost(40), name="middle",
     )(index_a, index_b, hid, mix, grad, rest, rest, rest, vectors)
 
 
@@ -506,13 +503,10 @@
 
     @pl.when(step == 0)
     def _():
-        dq[...] = jnp.zeros_like(dq)
-        dkv[...] = jnp.zeros_like(dkv)
-        do[...] = jnp.zeros_like(do)
         small_ref[...] = jnp.zeros_like(small_ref)
 
     cq, ck, cv = cq_ref[...], ck_ref[...], cv_ref[...]
-    normed, inverse = norm(hid_ref[...])
+    normed, inverse = norm(wide(hid_ref[...]))
     first = low(normed * vec(vec_ref, S_GAIN) + vec(vec_ref, S_SHIFT))
     grad1 = wide(h2_ref[...]) + mxu(cq, wq_ref[...], NT)
     h1 = norm_back(grad1, normed, inverse, vec(vec_ref, S_GAIN))
@@ -521,11 +515,11 @@
     mix_grad = low(mxu(b1, wo_ref[...], NT))
     mg_ref[...] = mix_grad
     delta_ref[0] = head_sums(mix_grad, mix_ref[...])
-    dq[...] += mxu(jnp.transpose(first), cq)
+    accumulate(dq, ..., mxu(jnp.transpose(first), cq))
     mem_t = jnp.transpose(mem_ref[...])
-    dkv[:, :512] += mxu(mem_t, ck)
-    dkv[:, 512:] += mxu(mem_t, cv)
-    do[...] += mxu(jnp.transpose(mix_ref[...]), b1)
+    accumulate(dkv, (slice(None), slice(0, 512)), mxu(mem_t, ck))
+    accumulate(dkv, (slice(None), slice(512, 1024)), mxu(mem_t, cv))
+    accumulate(do, ..., mxu(jnp.transpose(mix_ref[...]), b1))
     small_ref[0:1, :] += sum_rows(cq)
     small_ref[1:2, :] += sum_rows(cv)
     small_ref[2:3, :] += sum_rows(grad1 * normed)
@@ -596,13 +590,12 @@
 
     @pl.when(step == 0)
     def _():
-        dw[...] = jnp.zeros_like(dw)
         lines_ref[...] = jnp.zeros_like(lines_ref)
 
     x_t = jnp.transpose(x_ref[...])
-    dw[:, :512] += mxu(x_t, dq_ref[...])
-    dw[:, 512:1024] += mxu(x_t, dk_ref[...])
-    dw[:, 1024:] += mxu(x_t, dv_ref[...])
+    accumulate(dw, (slice(None), slice(0, 512)), mxu(x_t, dq_ref[...]))
+    accumulate(dw, (slice(None), slice(512, 1024)), mxu(x_t, dk_ref[...]))
+    accumulate(dw, (slice(None), slice(1024, 1536)), mxu(x_t, dv_ref[...]))
     lines_ref[S_BIAS:S_BIAS + 1, :512] += sum_rows(dq_ref[...])
     lines_ref[S_BIAS:S_BIAS + 1, 512:1024] += sum_rows(dv_ref[...])
 
@@ -610,7 +603,7 @@
     def _():
         outs = keep_ref, send_ref
         emit(outs, 0, dw, index_a, 0, 768)
-        emit(outs, 896, dw, index_b, 768, 768)
+        emit(outs, 768, dw, index_b, 768, 768)
         for row, col, source, source_row in (
             (S_BIAS, 1024, small_ref, 4), (S_GAIN, 0, small_ref, 2), (S_SHIFT, 0, small_ref, 3),
             (C_BIAS, 0, small_ref, 0), (C_BIAS, 512, small_ref, 1), (C_BIAS, 1024, mid_ref, 6),
@@ -628,7 +621,7 @@
                         line = jnp.broadcast_to(lines_ref[j:j + 1, :n], (count, n))
                         table[:, j, :] = mxu(low(jnp.where(mine, line, 0.0)), hot, NT)
             for r in range(count):
-                outs[2 * r // count][r % (count // 2), :, 768:896] = low(table[index_a[r]])
+                outs[2 * r // count][r % (count // 2), :, 1536:] = low(table[index_b[r]])
 
 
 def self_grad(count, index_a, index_b, grads, x, mid_small, small):
@@ -742,16 +735,14 @@
                 vec_ref[j:j + 1, :n] = jnp.sum(jnp.where(mine, spread, 0.0), axis=0, keepdims=True)
 
 
-def place_kernel(index_a, index_b, *refs):
-    n = (len(refs) - 1) // 2
-    w_ref = refs[-1]
-    for pieces, index, col in ((refs[:n], index_a, 0), (refs[n:2 * n], index_b, 1024)):
-        r = 0
-        for piece in pieces:
-            for j in range(piece.shape[0]):
-                row = pl.multiple_of(index[r] * UNIT, UNIT)
-                w_ref[pl.ds(row, UNIT), col:col + 1024] = piece[j]
-                r += 1
+def place_kernel(index, *refs):
+    pieces, w_ref = refs[:-1], refs[-1]
+    r = 0
+    for piece in pieces:
+        for j in range(piece.shape[0]):
+            row = pl.multiple_of(index[r] * UNIT, UNIT)
+            w_ref[pl.ds(row, UNIT), :] = piece[j]
+            r += 1
 
 
 def gather_weights(net, small, big):
@@ -777,8 +768,8 @@
     packed = everywhere(packed)
     packed, cross = lax.optimization_barrier((packed, cross))
     cross = everywhere(cross)
-    parts = [packed[:, :, :896], packed[:, :, 896:], cross[:, :, :1024], cross[:, :, 1024:]]
-    orders = orders + orders
+    parts = [packed[:, :, :896], packed[:, :, 896:], cross]
+    orders = orders + orders[:1]
     parts = [jnp.concatenate([x, net.exchange(x, order[far])], axis=0) for x, order in zip(parts, orders)]
 
     def spread(pieces, s):
@@ -793,9 +784,9 @@
         held, values = lax.optimization_barrier((later, values))
         held = spread(held, far + 2)
         return values, pl.pallas_call(
-            place_kernel, in_specs=[smem(), smem()] + [vmem()] * (len(held[0]) * 2), out_specs=vmem(),
-            out_shape=shape_of((512, 2048)), compiler_params=params(32), cost_estimate=cost(2), name="place",
-        )(*gather_index, *held[0], *held[1])
+            place_kernel, in_specs=[smem()] + [vmem()] * len(held[0]), out_specs=vmem(),
+            out_shape=pltpu.HBM((512, 2048), BF), compiler_params=params(32), cost_estimate=cost(2), name="place",
+        )(gather_index[0], *held[0])
 
     w, vectors = pl.pallas_call(
         functools.partial(unpack_kernel, net.count), in_specs=[smem(), smem()] + [vmem()] * (len(pieces[0]) * 2), out_specs=[vmem()] * 2,
@@ -938,11 +929,11 @@
         whole = lambda keep, send: jnp.concatenate([keep, send], axis=0).reshape(512, -1)
         d_self, d_cross, d_ffn = whole(self_keep, self_send), whole(cross_keep, cross_send), whole(ffn_keep, ffn_send)
         d_out = d_ffn[:, 2048:].reshape(-1, UNIT, 4, 512).transpose(0, 2, 1, 3).reshape(2048, 512)
-        weights = (jnp.concatenate([d_self[:, :768], d_self[:, 896:]], axis=1), d_cross[:, 1024:1536],
+        weights = (d_self[:, :1536], d_cross[:, 1024:1536],
                    d_cross[:, :512], d_cross[:, 1536:], d_cross[:, 512:1024], d_ffn[:, :2048], d_out)
         return (output, target_out, memory_grad, *[total(w) for w in weights], *[total(lines[j, :n]) for j, n in enumerate(VECTORS)])
 
-    groups.append(Reduction(net, self_keep, self_send, 896))
+    groups.append(Reduction(net, self_keep, self_send, 768))
     target_out = None
     while any(group.sums is None for group in groups):
         open_groups = [group for group in groups if group.sums is None]
@@ -957,10 +948,10 @@
             group.add()
         together([group for group in open_groups if group.sums is None])
     d_ffn, d_cross, d_self = (group.sums for group in groups)
-    vectors_out = [d_self[j, 768:768 + n // net.count] for j, n in enumerate(VECTORS)]
+    vectors_out = [d_self[j, 1536:1536 + n // net.count] for j, n in enumerate(VECTORS)]
     return (
         output, target_out, memory_grad,
-        jnp.concatenate([d_self[:, :768], d_self[:, 896:]], axis=1), d_cross[:, 1024:1536],
+        d_self[:, :1536], d_cross[:, 1024:1536],
         d_cross[:, :512], d_cross[:, 1536:], d_cross[:, 512:1024],
         d_ffn[:, :2048], jnp.concatenate([d_ffn[:, 2048 + 512 * b:2560 + 512 * b] for b in range(4)], axis=0),
         *vectors_out,

time: 276 us -> 267 us (0.967)
  local copies, waits for them, and re-layouts: 19.2 us -> 7.39 us
  waiting for transfers between devices: 22.1 us -> 18.5 us
    unnamed x61 -> x50, local copies, waits for them, and re-layouts: 14.2 us -> 1.26 us
    ppermute x36 -> x33, starting transfers between devices: 40 us -> 47.8 us  [across(): return lax.ppermute(x, 'wide', [(i, i ^ mask) for i in range(self.wide)])]
    ppermute x10 -> x9, starting transfers between devices: 20.9 us -> 14 us  [exchange(): lax.ppermute(x, 'narrow', [(i, i ^ 1 << bit) for i in range(self.narrow)])]
    ppermute x36 -> x33, waiting for transfers between devices: 12.8 us -> 10.2 us  [across(): return lax.ppermute(x, 'wide', [(i, i ^ mask) for i in range(self.wide)])]
    ppermute x10 -> x9, waiting for transfers between devices: 9.25 us -> 8.18 us  [exchange(): lax.ppermute(x, 'narrow', [(i, i ^ 1 << bit) for i in range(self.narrow)])]
  transfers between devices with their start and end apart: 47 -> 43, of which waited for: 16 -> 12; matrix products, arithmetic and copies ran while one was open for 2% -> 3% of each run, Pallas kernels for 38% -> 41%
where the time goes in v1:
time: 267 us; the launch traced here: 265 us
  Pallas kernels  154 us (58%)
  starting transfers between devices  61.9 us (23%)
  waiting for transfers between devices  18.5 us (7%)
  between operations  15 us (6%)
  other arithmetic  7.58 us (3%)
  local copies, waits for them, and re-layouts  7.39 us (3%)
    ppermute x33, starting transfers between devices, across(): return lax.ppermute(x, 'wide', [(i, i ^ mask) for i in range(self.wide)])  47.8 us
    pallas_call x1, Pallas kernels, middle(): pl.pallas_call(mid_kernel, grid=(total // t,), in_specs=[smem(), smem(),...  43.8 us
    pallas_call x2, Pallas kernels, attend_back(): pl.pallas_call(functools.partial(back_kernel, causal), grid=(rows,), in_s...  40.1 us
    pallas_call x1, Pallas kernels, cross_forward(): pl.pallas_call(cross_kernel, grid=(rows,), in_specs=[smem(), smem(), tile...  21.3 us
    pallas_call x1, Pallas kernels, self_forward(): pl.pallas_call(self_kernel, grid=(rows,), in_specs=[smem(), smem(), tiled...  16 us
    ppermute x9, starting transfers between devices, exchange(): lax.ppermute(x, 'narrow', [(i, i ^ 1 << bit) for i in range(self.narrow)])  14 us
    pallas_call x1, Pallas kernels, cross_dense(): pl.pallas_call(cross_dense_kernel, grid=(total // t,), in_specs=[smem(),...  13 us
    ppermute x33, waiting for transfers between devices, across(): return lax.ppermute(x, 'wide', [(i, i ^ mask) for i in range(self.wide)])  10.2 us
  transfers between devices with their start and end apart: 43, of which 12 were waited for; matrix products, arithmetic and copies ran while one was open for 3% of the time, Pallas kernels for 41%

profile of v1, /device:TPU:0, one launch (start us, length us, event | category | flops | bytes accessed | tf_op | source)
XLA Modules:
  0.0 264.8 jit_solution(6013865927721084258)
XLA Ops:
  7.3 1.9 pack.1
  9.2 5.1 %collective-permute-start.2 = (bf16[1,16,1664]{2,1,0:T(8,128)(2,1)}, bf16[1,16,1664]{2,1,0:T(8,128)(2,1)S(1)}, u32[]{:S(2)}, u32[]{:S(2)}) collective-permute-start(bf16[1,16,1664]{2,1,0:T(8,128)(2,1)} %get-tuple-element.103), channel_id=1, source_target_pairs={{0,24},{2,26},{4,28},{6,30},{8,16},{10,18},{12,20},{14,22},{16,8},... | collective-permute-start | bytes 159752 | tf_op jit(solution)/shard_map/ppermute | solution.py:680
  15.0 0.8 slice.236
  16.1 0.9 collective-permute-done.2
  17.0 1.8 collective-permute-done.1
  18.7 1.2 collective-permute-done
  19.9 0.8 pad_maximum_fusion.5
  20.8 1.8 collective-permute-start.5
  22.8 2.4 collective-permute-start.3
  25.2 0.9 constant_dynamic-update-slice_fusion.4
  26.1 1.6 collective-permute-start.12
  27.7 1.5 collective-permute-start.8
  30.0 0.9 pad_maximum_fusion.3
  30.8 1.9 collective-permute-start.6
  32.7 1.0 collective-permute-done.8
  34.5 1.4 collective-permute-start.13
  36.4 4.1 %collective-permute-done.13.refs_5_ = bf16[8,16,768]{2,1,0:T(8,128)(2,1)S(1)} collective-permute-done((bf16[8,16,768]{2,1,0:T(8,128)(2,1)S(1)}, bf16[8,16,768]{2,1,0:T(8,128)(2,1)S(1)}, u32[]{:S(2)}, u32[]{:S(2)}) %collective-permute-start.13) | collective-permute-done | bytes 196640 | tf_op jit(solution)/shard_map/ppermute | solution.py:675
  41.0 1.5 collective-permute-start.7
  42.5 1.3 unpack.1
  44.1 16.0 %self_forward.1 = (bf16[2048,1536]{1,0:T(8,128)(2,1)}, bf16[2048,512]{1,0:T(8,128)(2,1)}, f32[2,8,1024]{2,1,0:T(8,128)S(1)}) custom-call(s32[2,8]{1,0:T(2,128)S(1)} %broadcast.64.first_ref, s32[2,8]{1,0:T(2,128)S(1)} %and_select_fusion.extra_ref, bf16[2048,512]{1,0:T(8,128)(2,1)S(1)} %copy-done.6, bf16[512,1536]{1,0:T(8,128)(2,1)S(1)} %get-tuple-element.107.w_ref, ...), custom_call_target="tpu_custom_call" | custom-call | flops 20000000000 | bytes 1048576 | tf_op jit(solution)/shard_map/self_forward/pallas_call | solution.py:253
  62.8 2.1 place.1.wo_ref.wq_ref.wkv_ref.w_ref
  64.9 21.3 %cross_forward.1 = (bf16[2048,512]{1,0:T(8,128)(2,1)}, bf16[2048,512]{1,0:T(8,128)(2,1)}, bf16[2048,1024]{1,0:T(8,128)(2,1)}, bf16[2048,512]{1,0:T(8,128)(2,1)}, f32[2,8,1024]{2,1,0:T(8,128)}) custom-call(s32[2,8]{1,0:T(2,128)} %get-tuple-element.189.first_ref, s32[2,8]{1,0:T(2,128)} %get-tuple-element.188.extra_ref, bf16[2048,512]{1,0:T(8,128)(2,1)} %x_ref.5, ...), custom_call_target="tpu_custom_call" | custom-call | flops 24999999488 | bytes 1048576 | tf_op jit(solution)/shard_map/cross_forward/pallas_call | solution.py:282
  86.2 43.8 %middle.1 = (bf16[2048,512]{1,0:T(8,128)(2,1)}, bf16[2048,512]{1,0:T(8,128)(2,1)}, bf16[2048,512]{1,0:T(8,128)(2,1)}, f32[2,8,1024]{2,1,0:T(8,128)}, bf16[16,16,...) custom-call(s32[32]{0:T(128)} %copy-done.4, s32[32]{0:T(128)} %copy-done.2, ...), custom_call_target="tpu_custom_call" | custom-call | flops 40000000000 | bytes 1048576 | tf_op jit(solution)/shard_map/middle/pallas_call | solution.py:482
  130.3 21.0 %cross_back.1 = (bf16[2048,512]{1,0:T(8,128)(2,1)}, bf16[2048,512]{1,0:T(8,128)(2,1)}, bf16[2048,512]{1,0:T(8,128)(2,1)}) custom-call(s32[2,8]{1,0:T(2,128)} %get-tuple-element.189.first_ref, s32[2,8]{1,0:T(2,128)} %get-tuple-element.188.extra_ref, bf16[2048,512]{1,0:T(8,128)(2,1)} %get-tuple-element.121.q_ref, ...), custom_call_target="tpu_custom_call" | custom-call | flops 20000000000 | bytes 1048576 | tf_op jit(solution)/shard_map/cross_back/pallas_call | solution.py:365
  151.3 2.5 add_convert_fusion
  154.0 2.8 %collective-permute-start.19 = (bf16[8,16,2048]{2,1,0:T(8,128)(2,1)S(1)}, bf16[8,16,2048]{2,1,0:T(8,128)(2,1)S(1)}, u32[]{:S(2)}, u32[]{:S(2)}) collective-permute-start(bf16[8,16,2048]{2,1,0:T(8,128)(2,1)S(1)} %get-tuple-element.193), channel_id=1, source_target_pairs={{0,4},{2,6},{4,0},{6,2},{8,12},{10,14},{12,8},{14,10},{16,20},{18,... | collective-permute-start | bytes 1572872 | tf_op jit(solution)/shard_map/ppermute | solution.py:680
  156.9 13.0 %cross_dense.1 = (bf16[2048,512]{1,0:T(8,128)(2,1)S(1)}, bf16[2048,512]{1,0:T(8,128)(2,1)S(1)}, f32[2,8,1024]{2,1,0:T(8,128)S(1)}, bf16[16,16,2560]{2,1,0:T(8,12...) custom-call(s32[32]{0:T(128)S(1)} %copy-done.5, s32[32]{0:T(128)S(1)} %copy-done.3, ...), custom_call_target="tpu_custom_call" | custom-call | flops 12000000000 | bytes 1048576 | tf_op jit(solution)/shard_map/cross_dense/pallas_call | solution.py:543
  170.4 2.0 collective-permute-start.21
  172.5 19.1 %self_back.1 = (bf16[2048,512]{1,0:T(8,128)(2,1)S(1)}, bf16[2048,512]{1,0:T(8,128)(2,1)S(1)}, bf16[2048,512]{1,0:T(8,128)(2,1)S(1)}) custom-call(s32[2,8]{1,0:T(2,128)S(1)} %broadcast.64.first_ref, s32[2,8]{1,0:T(2,128)S(1)} %and_select_fusion.extra_ref, bf16[2048,1536]{1,0:T(8,128)(2,1)} %get-tuple-element.145.q_ref.k_ref.v_ref, ...), custom_call_target="tpu_custom_call" | custom-call | flops 20000000000 | bytes 1048576 | tf_op jit(solution)/shard_map/self_back/pallas_call | solution.py:365
  191.9 1.1 collective-permute-start.26
  193.0 7.5 %collective-permute-start.25 = (bf16[1,16,4096]{2,1,0:T(8,128)(2,1)S(1)}, bf16[1,16,4096]{2,1,0:T(8,128)(2,1)S(1)}, u32[]{:S(2)}, u32[]{:S(2)}) collective-permute-start(bf16[1,16,4096]{2,1,0:T(8,128)(2,1)S(1)} %get-tuple-element.203), channel_id=1, source_target_pairs={{0,8},{2,10},{4,12},{6,14},{8,0},{10,2},{12,4},{14,6},{16,24},{18,... | collective-permute-start | bytes 393224 | tf_op jit(solution)/shard_map/ppermute | solution.py:680
  200.5 1.4 collective-permute-start.24
  202.3 3.6 %collective-permute-start.28 = (bf16[8,16,1280]{2,1,0:T(8,128)(2,1)S(1)}, bf16[8,16,1280]{2,1,0:T(8,128)(2,1)S(1)}, u32[]{:S(2)}, u32[]{:S(2)}) collective-permute-start(bf16[8,16,1280]{2,1,0:T(8,128)(2,1)S(1)} %get-tuple-element.196), channel_id=1, source_target_pairs={{0,1},{1,0},{2,3},{3,2},{4,5},{5,4},{6,7},{7,6},{8,9},{9,8},{10,11... | collective-permute-start | bytes 983048 | tf_op jit(solution)/shard_map/ppermute | solution.py:675
  206.0 6.3 %self_grad.1 = (bf16[16,16,1664]{2,1,0:T(8,128)(2,1)S(1)}, bf16[16,16,1664]{2,1,0:T(8,128)(2,1)S(1)}, f32[16,2048]{1,0:T(8,128)}) custom-call(s32[32]{0:T(128)S(1)} %copy-done.5, s32[32]{0:T(128)S(1)} %copy-done.3, bf16[2048,512]{1,0:T(8,128)(2,1)S(1)} %get-tuple-element.152.dq_ref, bf16[2048,512]{1,0:T(8,128)(2,1)S(1)} %get-tuple-element.153.dk_ref, ...), custom_call_target="tpu_custom_call" | custom-call | flops 5000000000 | bytes 1048576 | tf_op jit(solution)/shard_map/self_grad/pallas_call | solution.py:631
  214.1 1.3 collective-permute-start.30
  215.4 8.2 %collective-permute-start.31 = (bf16[16,16,1664]{2,1,0:T(8,128)(2,1)S(1)}, bf16[16,16,1664]{2,1,0:T(8,128)(2,1)S(1)}, u32[]{:S(2)}, u32[]{:S(2)}) collective-permute-start(bf16[16,16,1664]{2,1,0:T(8,128)(2,1)S(1)} %get-tuple-element.166), channel_id=1, source_target_pairs={{0,2},{2,0},{4,6},{6,4},{8,10},{10,8},{12,14},{14,12},{16,18},{18,... | collective-permute-start | bytes 2555912 | tf_op jit(solution)/shard_map/ppermute | solution.py:680
  224.4 1.2 collective-permute-done.31
  225.9 1.6 collective-permute-start.39
  228.0 2.4 collective-permute-start.41
  230.7 1.6 collective-permute-start.33
  232.3 4.9 %target_grad.1 = bf16[2048,512]{1,0:T(8,128)(2,1)} custom-call(bf16[2048,512]{1,0:T(8,128)(2,1)S(1)} %get-tuple-element.141.h1_ref, bf16[2048,512]{1,0:T(8,128)(2,1)S(1)} %get-tuple-element.152.dq_ref, bf16[2048,512]{1,0:T(8,128)(2,1)S(1)} %get-tuple-element.153.dk_ref, bf16[2048,512]{1,0:T(8,128)(2,1)S(1)} %get-tuple-element.154.dv_ref, ...), custom_call_target="tpu_custom_call" | custom-call | flops 5000000000 | bytes 1048576 | tf_op jit(solution)/shard_map/target_grad/pallas_call | solution.py:651
  237.3 1.7 collective-permute-done.33
  239.1 1.7 collective-permute-start.34
  242.6 1.4 collective-permute-done.34
  244.0 2.9 %collective-permute-done.35 = bf16[4,16,896]{2,1,0:T(8,128)(2,1)S(1)} collective-permute-done((bf16[4,16,896]{2,1,0:T(8,128)(2,1)S(1)}, bf16[4,16,896]{2,1,0:T(8,128)(2,1)S(1)}, u32[]{:S(2)}, u32[]{:S(2)}) %collective-permute-start.35) | collective-permute-done | bytes 114720 | tf_op jit(solution)/shard_map/ppermute | solution.py:680
  247.8 1.4 collective-permute-start.37
  249.1 2.4 collective-permute-start.38
  251.5 3.9 %memory_grad.1 = bf16[2048,512]{1,0:T(8,128)(2,1)} custom-call(bf16[2048,512]{1,0:T(8,128)(2,1)S(1)} %copy-done.10, bf16[2048,512]{1,0:T(8,128)(2,1)S(1)} %copy-done.12, bf16[512,2048]{1,0:T(8,128)(2,1)S(1)} %copy-done.8, bf16[4,16,768]{2,1,0:T(8,128)(2,1)S(1)} %get-tuple-element.174.refs_0_, bf16[4,16,896]{2,1,0:T(8,128)(2,1)S(1)} %get-tuple-element.175.refs_1_), custom_call_target="tpu_custom_call" | custom-call | flops 4000000000 | bytes 1048576 | tf_op jit(solution)/shard_map/memory_grad/pallas_call | solution.py:561
  (164 shorter events, 17.2 us)
Async XLA Ops:
  7.2 79.0 %all-gather.2.cloned.1.call-start = ((), (), s32[]{:S(2)}) async-start(), calls=%async_computation | async-start | bytes 4866048 | tf_op jit(solution)/shard_map/all_gather | solution.py:763
  9.2 7.7 %collective-permute-start.2 = (bf16[1,16,1664]{2,1,0:T(8,128)(2,1)}, bf16[1,16,1664]{2,1,0:T(8,128)(2,1)S(1)}, u32[]{:S(2)}, u32[]{:S(2)}) collective-permute-start(bf16[1,16,1664]{2,1,0:T(8,128)(2,1)} %get-tuple-element.103), channel_id=1, source_target_pairs={{0,24},{2,26},{4,28},{6,30},{8,16},{10,18},{12,20},{14,22},{16,8},... | collective-permute-start | bytes 159752 | tf_op jit(solution)/shard_map/ppermute | solution.py:680
  14.3 4.4 %collective-permute-start.1 = (bf16[1,16,1664]{2,1,0:T(8,128)(2,1)}, bf16[1,16,1664]{2,1,0:T(8,128)(2,1)S(1)}, u32[]{:S(2)}, u32[]{:S(2)}) collective-permute-start(bf16[1,16,1664]{2,1,0:T(8,128)(2,1)} %get-tuple-element.103), channel_id=1, source_target_pairs={{0,8},{2,10},{4,12},{6,14},{8,0},{10,2},{12,4},{14,6},{16,24},{18,... | collective-permute-start | bytes 159752 | tf_op jit(solution)/shard_map/ppermute | solution.py:680
  14.3 5.6 %collective-permute-start = (bf16[1,16,1664]{2,1,0:T(8,128)(2,1)}, bf16[1,16,1664]{2,1,0:T(8,128)(2,1)S(1)}, u32[]{:S(2)}, u32[]{:S(2)}) collective-permute-start(bf16[1,16,1664]{2,1,0:T(8,128)(2,1)} %get-tuple-element.103), channel_id=1, source_target_pairs={{0,16},{2,18},{4,20},{6,22},{8,24},{10,26},{12,28},{14,30},{16,0},... | collective-permute-start | bytes 159752 | tf_op jit(solution)/shard_map/ppermute | solution.py:680
  15.8 28.0 %copy-start.2 = (s32[32]{0:T(128)}, s32[32]{0:T(128)S(1)}, u32[]{:S(2)}) copy-start(s32[32]{0:T(128)S(1)} %get-tuple-element.235.index_b) | copy-start | bytes 388
  15.8 47.0 %copy-start.4 = (s32[32]{0:T(128)}, s32[32]{0:T(128)S(1)}, u32[]{:S(2)}) copy-start(s32[32]{0:T(128)S(1)} %get-tuple-element.236.index_a.index) | copy-start | bytes 388
  16.1 27.8 %copy-start = (f32[2,1,1024]{2,1,0:T(1,128)}, f32[2,1,1024]{2,1,0:T(1,128)S(1)}, u32[]{:S(2)}) copy-start(f32[2,1,1024]{2,1,0:T(1,128)S(1)} %broadcast_in_dim.58.seg_ref.qseg_ref.kseg_ref) | copy-start | bytes 24580
  20.8 8.4 %collective-permute-start.5 = (bf16[1,16,2048]{2,1,0:T(8,128)(2,1)}, bf16[1,16,2048]{2,1,0:T(8,128)(2,1)S(1)}, u32[]{:S(2)}, u32[]{:S(2)}) collective-permute-start(bf16[1,16,2048]{2,1,0:T(8,128)(2,1)} %get-tuple-element.105), channel_id=1, source_target_pairs={{0,24},{2,26},{4,28},{6,30},{8,16},{10,18},{12,20},{14,22},{16,8},... | collective-permute-start | bytes 196616 | tf_op jit(solution)/shard_map/ppermute | solution.py:680
  22.5 6.7 %collective-permute-start.4 = (bf16[1,16,2048]{2,1,0:T(8,128)(2,1)}, bf16[1,16,2048]{2,1,0:T(8,128)(2,1)S(1)}, u32[]{:S(2)}, u32[]{:S(2)}) collective-permute-start(bf16[1,16,2048]{2,1,0:T(8,128)(2,1)} %get-tuple-element.105), channel_id=1, source_target_pairs={{0,8},{2,10},{4,12},{6,14},{8,0},{10,2},{12,4},{14,6},{16,24},{18,... | collective-permute-start | bytes 196616 | tf_op jit(solution)/shard_map/ppermute | solution.py:680
  22.8 7.2 %collective-permute-start.3 = (bf16[1,16,2048]{2,1,0:T(8,128)(2,1)}, bf16[1,16,2048]{2,1,0:T(8,128)(2,1)S(1)}, u32[]{:S(2)}, u32[]{:S(2)}) collective-permute-start(bf16[1,16,2048]{2,1,0:T(8,128)(2,1)} %get-tuple-element.105), channel_id=1, source_target_pairs={{0,16},{2,18},{4,20},{6,22},{8,24},{10,26},{12,28},{14,30},{16,0},... | collective-permute-start | bytes 196616 | tf_op jit(solution)/shard_map/ppermute | solution.py:680
  26.1 8.3 %collective-permute-start.12 = (bf16[4,16,768]{2,1,0:T(8,128)(2,1)S(1)}, bf16[4,16,768]{2,1,0:T(8,128)(2,1)S(1)}, u32[]{:S(2)}, u32[]{:S(2)}) collective-permute-start(bf16[4,16,768]{2,1,0:T(8,128)(2,1)S(1)} %slice.238), channel_id=1, source_target_pairs={{0,4},{2,6},{4,0},{6,2},{8,12},{10,14},{12,8},{14,10},{16,20},{18,... | collective-permute-start | bytes 294920 | tf_op jit(solution)/shard_map/ppermute | solution.py:680
  27.7 6.1 %collective-permute-start.8 = (bf16[4,16,896]{2,1,0:T(8,128)(2,1)S(1)}, bf16[4,16,896]{2,1,0:T(8,128)(2,1)S(1)}, u32[]{:S(2)}, u32[]{:S(2)}) collective-permute-start(bf16[4,16,896]{2,1,0:T(8,128)(2,1)S(1)} %slice.237), channel_id=1, source_target_pairs={{0,1},{1,0},{2,3},{3,2},{4,5},{5,4},{6,7},{7,6},{8,9},{9,8},{10,11... | collective-permute-start | bytes 344072 | tf_op jit(solution)/shard_map/ppermute | solution.py:675
  30.8 10.2 %collective-permute-start.6 = (bf16[4,16,2048]{2,1,0:T(8,128)(2,1)S(1)}, bf16[4,16,2048]{2,1,0:T(8,128)(2,1)S(1)}, u32[]{:S(2)}, u32[]{:S(2)}) collective-permute-start(bf16[4,16,2048]{2,1,0:T(8,128)(2,1)S(1)} %pad_maximum_fusion.3), channel_id=1, source_target_pairs={{0,1},{1,0},{2,3},{3,2},{4,5},{5,4},{6,7},{7,6},{8,9},{9,8},{10,11... | collective-permute-start | bytes 786440 | tf_op jit(solution)/shard_map/ppermute | solution.py:675
  33.8 6.7 %collective-permute-start.9 = (bf16[8,16,896]{2,1,0:T(8,128)(2,1)S(1)}, bf16[8,16,896]{2,1,0:T(8,128)(2,1)S(1)}, u32[]{:S(2)}, u32[]{:S(2)}) collective-permute-start(bf16[8,16,896]{2,1,0:T(8,128)(2,1)S(1)} %pad_maximum_fusion.4.refs_0_), channel_id=1, source_target_pairs={{0,4},{2,6},{4,0},{6,2},{8,12},{10,14},{12,8},{14,10},{16,20},{18,... | collective-permute-start | bytes 688136 | tf_op jit(solution)/shard_map/ppermute | solution.py:680
  34.5 6.0 %collective-permute-start.13 = (bf16[8,16,768]{2,1,0:T(8,128)(2,1)S(1)}, bf16[8,16,768]{2,1,0:T(8,128)(2,1)S(1)}, u32[]{:S(2)}, u32[]{:S(2)}) collective-permute-start(bf16[8,16,768]{2,1,0:T(8,128)(2,1)S(1)} %pad_maximum_fusion.6.refs_4_), channel_id=1, source_target_pairs={{0,1},{1,0},{2,3},{3,2},{4,5},{5,4},{6,7},{7,6},{8,9},{9,8},{10,11... | collective-permute-start | bytes 589832 | tf_op jit(solution)/shard_map/ppermute | solution.py:675
  35.9 6.6 %collective-permute-start.14 = (bf16[8,16,768]{2,1,0:T(8,128)(2,1)S(1)}, bf16[8,16,768]{2,1,0:T(8,128)(2,1)S(1)}, u32[]{:S(2)}, u32[]{:S(2)}) collective-permute-start(bf16[8,16,768]{2,1,0:T(8,128)(2,1)S(1)} %pad_maximum_fusion.6.refs_4_), channel_id=1, source_target_pairs={{0,2},{2,0},{4,6},{6,4},{8,10},{10,8},{12,14},{14,12},{16,18},{18,... | collective-permute-start | bytes 589832 | tf_op jit(solution)/shard_map/ppermute | solution.py:680
  35.9 6.6 %collective-permute-start.10 = (bf16[8,16,896]{2,1,0:T(8,128)(2,1)S(1)}, bf16[8,16,896]{2,1,0:T(8,128)(2,1)S(1)}, u32[]{:S(2)}, u32[]{:S(2)}) collective-permute-start(bf16[8,16,896]{2,1,0:T(8,128)(2,1)S(1)} %pad_maximum_fusion.4.refs_0_), channel_id=1, source_target_pairs={{0,2},{2,0},{4,6},{6,4},{8,10},{10,8},{12,14},{14,12},{16,18},{18,... | collective-permute-start | bytes 688136 | tf_op jit(solution)/shard_map/ppermute | solution.py:680
  40.5 2.0 collective-permute-start.15
  40.5 2.0 collective-permute-start.11
  41.0 19.1 %collective-permute-start.7 = (bf16[8,16,2048]{2,1,0:T(8,128)(2,1)S(1)}, bf16[8,16,2048]{2,1,0:T(8,128)(2,1)S(1)}, u32[]{:S(2)}, u32[]{:S(2)}) collective-permute-start(bf16[8,16,2048]{2,1,0:T(8,128)(2,1)S(1)} %constant_dynamic-update-slice_fusion.refs_0_), channel_id=1, source_target_pairs={{0,4},{2,6},{4,0},{6,2},{8,12},{10,14},{12,8},{14,10},{16,20},{18,... | collective-permute-start | bytes 1572872 | tf_op jit(solution)/shard_map/ppermute | solution.py:680
  60.1 2.0 collective-permute-start.16
  60.2 2.6 collective-permute-start.17
  130.1 21.2 %collective-permute-start.18 = (bf16[16,16,4096]{2,1,0:T(8,128)(2,1)}, bf16[16,16,4096]{2,1,0:T(8,128)(2,1)}, u32[]{:S(2)}, u32[]{:S(2)}) collective-permute-start(bf16[16,16,4096]{2,1,0:T(8,128)(2,1)} %get-tuple-element.120.refs_0_), channel_id=1, source_target_pairs={{0,2},{2,0},{4,6},{6,4},{8,10},{10,8},{12,14},{14,12},{16,18},{18,... | collective-permute-start | bytes 6291464 | tf_op jit(solution)/shard_map/ppermute | solution.py:680
  130.3 21.0 %copy-start.18 = (bf16[16,16,4096]{2,1,0:T(8,128)(2,1)S(1)}, bf16[16,16,4096]{2,1,0:T(8,128)(2,1)}, u32[]{:S(2)}) copy-start(bf16[16,16,4096]{2,1,0:T(8,128)(2,1)} %get-tuple-element.119) | copy-start | bytes 6291460
  153.9 16.0 %collective-permute-start.20 = (bf16[8,16,2048]{2,1,0:T(8,128)(2,1)S(1)}, bf16[8,16,2048]{2,1,0:T(8,128)(2,1)S(1)}, u32[]{:S(2)}, u32[]{:S(2)}) collective-permute-start(bf16[8,16,2048]{2,1,0:T(8,128)(2,1)S(1)} %get-tuple-element.192), channel_id=1, source_target_pairs={{0,1},{1,0},{2,3},{3,2},{4,5},{5,4},{6,7},{7,6},{8,9},{9,8},{10,11... | collective-permute-start | bytes 1572872 | tf_op jit(solution)/shard_map/ppermute | solution.py:675
  154.0 15.9 %collective-permute-start.19 = (bf16[8,16,2048]{2,1,0:T(8,128)(2,1)S(1)}, bf16[8,16,2048]{2,1,0:T(8,128)(2,1)S(1)}, u32[]{:S(2)}, u32[]{:S(2)}) collective-permute-start(bf16[8,16,2048]{2,1,0:T(8,128)(2,1)S(1)} %get-tuple-element.193), channel_id=1, source_target_pairs={{0,4},{2,6},{4,0},{6,2},{8,12},{10,14},{12,8},{14,10},{16,20},{18,... | collective-permute-start | bytes 1572872 | tf_op jit(solution)/shard_map/ppermute | solution.py:680
  170.4 21.2 %collective-permute-start.21 = (bf16[4,16,2048]{2,1,0:T(8,128)(2,1)S(1)}, bf16[4,16,2048]{2,1,0:T(8,128)(2,1)S(1)}, u32[]{:S(2)}, u32[]{:S(2)}) collective-permute-start(bf16[4,16,2048]{2,1,0:T(8,128)(2,1)S(1)} %slice.298.refs_0_), channel_id=1, source_target_pairs={{0,1},{1,0},{2,3},{3,2},{4,5},{5,4},{6,7},{7,6},{8,9},{9,8},{10,11... | collective-permute-start | bytes 786440 | tf_op jit(solution)/shard_map/ppermute | solution.py:675
  172.4 19.2 %collective-permute-start.22 = (bf16[4,16,2048]{2,1,0:T(8,128)(2,1)S(1)}, bf16[4,16,2048]{2,1,0:T(8,128)(2,1)S(1)}, u32[]{:S(2)}, u32[]{:S(2)}) collective-permute-start(bf16[4,16,2048]{2,1,0:T(8,128)(2,1)S(1)} %slice.300.refs_1_), channel_id=1, source_target_pairs={{0,4},{2,6},{4,0},{6,2},{8,12},{10,14},{12,8},{14,10},{16,20},{18,... | collective-permute-start | bytes 786440 | tf_op jit(solution)/shard_map/ppermute | solution.py:680
  172.5 19.1 %collective-permute-start.23 = (bf16[16,16,2560]{2,1,0:T(8,128)(2,1)S(1)}, bf16[16,16,2560]{2,1,0:T(8,128)(2,1)S(1)}, u32[]{:S(2)}, u32[]{:S(2)}) collective-permute-start(bf16[16,16,2560]{2,1,0:T(8,128)(2,1)S(1)} %get-tuple-element.144.refs_2_), channel_id=1, source_target_pairs={{0,2},{2,0},{4,6},{6,4},{8,10},{10,8},{12,14},{14,12},{16,18},{18,... | collective-permute-start | bytes 3932168 | tf_op jit(solution)/shard_map/ppermute | solution.py:680
  191.9 20.4 %collective-permute-start.26 = (bf16[1,16,4096]{2,1,0:T(8,128)(2,1)S(1)}, bf16[1,16,4096]{2,1,0:T(8,128)(2,1)S(1)}, u32[]{:S(2)}, u32[]{:S(2)}) collective-permute-start(bf16[1,16,4096]{2,1,0:T(8,128)(2,1)S(1)} %get-tuple-element.202), channel_id=1, source_target_pairs={{0,24},{2,26},{4,28},{6,30},{8,16},{10,18},{12,20},{14,22},{16,8},... | collective-permute-start | bytes 393224 | tf_op jit(solution)/shard_map/ppermute | solution.py:680
  193.0 19.3 %collective-permute-start.25 = (bf16[1,16,4096]{2,1,0:T(8,128)(2,1)S(1)}, bf16[1,16,4096]{2,1,0:T(8,128)(2,1)S(1)}, u32[]{:S(2)}, u32[]{:S(2)}) collective-permute-start(bf16[1,16,4096]{2,1,0:T(8,128)(2,1)S(1)} %get-tuple-element.203), channel_id=1, source_target_pairs={{0,8},{2,10},{4,12},{6,14},{8,0},{10,2},{12,4},{14,6},{16,24},{18,... | collective-permute-start | bytes 393224 | tf_op jit(solution)/shard_map/ppermute | solution.py:680
  200.5 11.8 %collective-permute-start.24 = (bf16[1,16,4096]{2,1,0:T(8,128)(2,1)S(1)}, bf16[1,16,4096]{2,1,0:T(8,128)(2,1)S(1)}, u32[]{:S(2)}, u32[]{:S(2)}) collective-permute-start(bf16[1,16,4096]{2,1,0:T(8,128)(2,1)S(1)} %get-tuple-element.204), channel_id=1, source_target_pairs={{0,16},{2,18},{4,20},{6,22},{8,24},{10,26},{12,28},{14,30},{16,0},... | collective-permute-start | bytes 393224 | tf_op jit(solution)/shard_map/ppermute | solution.py:680
  202.3 9.9 %collective-permute-start.28 = (bf16[8,16,1280]{2,1,0:T(8,128)(2,1)S(1)}, bf16[8,16,1280]{2,1,0:T(8,128)(2,1)S(1)}, u32[]{:S(2)}, u32[]{:S(2)}) collective-permute-start(bf16[8,16,1280]{2,1,0:T(8,128)(2,1)S(1)} %get-tuple-element.196), channel_id=1, source_target_pairs={{0,1},{1,0},{2,3},{3,2},{4,5},{5,4},{6,7},{7,6},{8,9},{9,8},{10,11... | collective-permute-start | bytes 983048 | tf_op jit(solution)/shard_map/ppermute | solution.py:675
  206.0 7.1 %collective-permute-start.27 = (bf16[8,16,1280]{2,1,0:T(8,128)(2,1)S(1)}, bf16[8,16,1280]{2,1,0:T(8,128)(2,1)S(1)}, u32[]{:S(2)}, u32[]{:S(2)}) collective-permute-start(bf16[8,16,1280]{2,1,0:T(8,128)(2,1)S(1)} %get-tuple-element.197), channel_id=1, source_target_pairs={{0,4},{2,6},{4,0},{6,2},{8,12},{10,14},{12,8},{14,10},{16,20},{18,... | collective-permute-start | bytes 983048 | tf_op jit(solution)/shard_map/ppermute | solution.py:680
  213.2 11.0 %collective-permute-start.29 = (bf16[4,16,1280]{2,1,0:T(8,128)(2,1)S(1)}, bf16[4,16,1280]{2,1,0:T(8,128)(2,1)S(1)}, u32[]{:S(2)}, u32[]{:S(2)}) collective-permute-start(bf16[4,16,1280]{2,1,0:T(8,128)(2,1)S(1)} %slice.310), channel_id=1, source_target_pairs={{0,1},{1,0},{2,3},{3,2},{4,5},{5,4},{6,7},{7,6},{8,9},{9,8},{10,11... | collective-permute-start | bytes 491528 | tf_op jit(solution)/shard_map/ppermute | solution.py:675
  214.1 10.2 %collective-permute-start.30 = (bf16[4,16,1280]{2,1,0:T(8,128)(2,1)S(1)}, bf16[4,16,1280]{2,1,0:T(8,128)(2,1)S(1)}, u32[]{:S(2)}, u32[]{:S(2)}) collective-permute-start(bf16[4,16,1280]{2,1,0:T(8,128)(2,1)S(1)} %slice.313), channel_id=1, source_target_pairs={{0,4},{2,6},{4,0},{6,2},{8,12},{10,14},{12,8},{14,10},{16,20},{18,... | collective-permute-start | bytes 491528 | tf_op jit(solution)/shard_map/ppermute | solution.py:680
  215.4 10.2 %collective-permute-start.31 = (bf16[16,16,1664]{2,1,0:T(8,128)(2,1)S(1)}, bf16[16,16,1664]{2,1,0:T(8,128)(2,1)S(1)}, u32[]{:S(2)}, u32[]{:S(2)}) collective-permute-start(bf16[16,16,1664]{2,1,0:T(8,128)(2,1)S(1)} %get-tuple-element.166), channel_id=1, source_target_pairs={{0,2},{2,0},{4,6},{6,4},{8,10},{10,8},{12,14},{14,12},{16,18},{18,... | collective-permute-start | bytes 2555912 | tf_op jit(solution)/shard_map/ppermute | solution.py:680
  225.9 11.3 %collective-permute-start.39 = (bf16[1,16,2560]{2,1,0:T(8,128)(2,1)S(1)}, bf16[1,16,2560]{2,1,0:T(8,128)(2,1)S(1)}, u32[]{:S(2)}, u32[]{:S(2)}) collective-permute-start(bf16[1,16,2560]{2,1,0:T(8,128)(2,1)S(1)} %get-tuple-element.167.refs_0_), channel_id=1, source_target_pairs={{0,16},{2,18},{4,20},{6,22},{8,24},{10,26},{12,28},{14,30},{16,0},... | collective-permute-start | bytes 245768 | tf_op jit(solution)/shard_map/ppermute | solution.py:680
  227.5 9.7 %collective-permute-start.40 = (bf16[1,16,2560]{2,1,0:T(8,128)(2,1)S(1)}, bf16[1,16,2560]{2,1,0:T(8,128)(2,1)S(1)}, u32[]{:S(2)}, u32[]{:S(2)}) collective-permute-start(bf16[1,16,2560]{2,1,0:T(8,128)(2,1)S(1)} %get-tuple-element.168.refs_1_), channel_id=1, source_target_pairs={{0,8},{2,10},{4,12},{6,14},{8,0},{10,2},{12,4},{14,6},{16,24},{18,... | collective-permute-start | bytes 245768 | tf_op jit(solution)/shard_map/ppermute | solution.py:680
  228.0 9.2 %collective-permute-start.41 = (bf16[1,16,2560]{2,1,0:T(8,128)(2,1)S(1)}, bf16[1,16,2560]{2,1,0:T(8,128)(2,1)S(1)}, u32[]{:S(2)}, u32[]{:S(2)}) collective-permute-start(bf16[1,16,2560]{2,1,0:T(8,128)(2,1)S(1)} %get-tuple-element.169.refs_2_), channel_id=1, source_target_pairs={{0,24},{2,26},{4,28},{6,30},{8,16},{10,18},{12,20},{14,22},{16,8},... | collective-permute-start | bytes 245768 | tf_op jit(solution)/shard_map/ppermute | solution.py:680
  230.3 6.9 %collective-permute-start.32 = (bf16[8,16,768]{2,1,0:T(8,128)(2,1)S(1)}, bf16[8,16,768]{2,1,0:T(8,128)(2,1)S(1)}, u32[]{:S(2)}, u32[]{:S(2)}) collective-permute-start(bf16[8,16,768]{2,1,0:T(8,128)(2,1)S(1)} %get-tuple-element.170.refs_3_), channel_id=1, source_target_pairs={{0,4},{2,6},{4,0},{6,2},{8,12},{10,14},{12,8},{14,10},{16,20},{18,... | collective-permute-start | bytes 589832 | tf_op jit(solution)/shard_map/ppermute | solution.py:680
  230.7 8.3 %collective-permute-start.33 = (bf16[8,16,896]{2,1,0:T(8,128)(2,1)S(1)}, bf16[8,16,896]{2,1,0:T(8,128)(2,1)S(1)}, u32[]{:S(2)}, u32[]{:S(2)}) collective-permute-start(bf16[8,16,896]{2,1,0:T(8,128)(2,1)S(1)} %get-tuple-element.171.refs_4_), channel_id=1, source_target_pairs={{0,1},{1,0},{2,3},{3,2},{4,5},{5,4},{6,7},{7,6},{8,9},{9,8},{10,11... | collective-permute-start | bytes 688136 | tf_op jit(solution)/shard_map/ppermute | solution.py:675
  232.3 19.2 %copy-start.12 = (bf16[2048,512]{1,0:T(8,128)(2,1)S(1)}, bf16[2048,512]{1,0:T(8,128)(2,1)}, u32[]{:S(2)}) copy-start(bf16[2048,512]{1,0:T(8,128)(2,1)} %get-tuple-element.132.cv_ref) | copy-start | bytes 6291460
  239.1 4.9 %collective-permute-start.34 = (bf16[4,16,768]{2,1,0:T(8,128)(2,1)S(1)}, bf16[4,16,768]{2,1,0:T(8,128)(2,1)S(1)}, u32[]{:S(2)}, u32[]{:S(2)}) collective-permute-start(bf16[4,16,768]{2,1,0:T(8,128)(2,1)S(1)} %get-tuple-element.174.refs_0_), channel_id=1, source_target_pairs={{0,1},{1,0},{2,3},{3,2},{4,5},{5,4},{6,7},{7,6},{8,9},{9,8},{10,11... | collective-permute-start | bytes 294920 | tf_op jit(solution)/shard_map/ppermute | solution.py:675
  242.1 4.9 %collective-permute-start.35 = (bf16[4,16,896]{2,1,0:T(8,128)(2,1)S(1)}, bf16[4,16,896]{2,1,0:T(8,128)(2,1)S(1)}, u32[]{:S(2)}, u32[]{:S(2)}) collective-permute-start(bf16[4,16,896]{2,1,0:T(8,128)(2,1)S(1)} %get-tuple-element.175.refs_1_), channel_id=1, source_target_pairs={{0,4},{2,6},{4,0},{6,2},{8,12},{10,14},{12,8},{14,10},{16,20},{18,... | collective-permute-start | bytes 344072 | tf_op jit(solution)/shard_map/ppermute | solution.py:680
  247.1 8.4 %collective-permute-start.36 = (bf16[1,16,1664]{2,1,0:T(8,128)(2,1)S(1)}, bf16[1,16,1664]{2,1,0:T(8,128)(2,1)S(1)}, u32[]{:S(2)}, u32[]{:S(2)}) collective-permute-start(bf16[1,16,1664]{2,1,0:T(8,128)(2,1)S(1)} %get-tuple-element.179), channel_id=1, source_target_pairs={{0,16},{2,18},{4,20},{6,22},{8,24},{10,26},{12,28},{14,30},{16,0},... | collective-permute-start | bytes 159752 | tf_op jit(solution)/shard_map/ppermute | solution.py:680
  247.8 7.7 %collective-permute-start.37 = (bf16[1,16,1664]{2,1,0:T(8,128)(2,1)S(1)}, bf16[1,16,1664]{2,1,0:T(8,128)(2,1)S(1)}, u32[]{:S(2)}, u32[]{:S(2)}) collective-permute-start(bf16[1,16,1664]{2,1,0:T(8,128)(2,1)S(1)} %get-tuple-element.180), channel_id=1, source_target_pairs={{0,8},{2,10},{4,12},{6,14},{8,0},{10,2},{12,4},{14,6},{16,24},{18,... | collective-permute-start | bytes 159752 | tf_op jit(solution)/shard_map/ppermute | solution.py:680
  249.1 6.3 %collective-permute-start.38 = (bf16[1,16,1664]{2,1,0:T(8,128)(2,1)S(1)}, bf16[1,16,1664]{2,1,0:T(8,128)(2,1)S(1)}, u32[]{:S(2)}, u32[]{:S(2)}) collective-permute-start(bf16[1,16,1664]{2,1,0:T(8,128)(2,1)S(1)} %get-tuple-element.181), channel_id=1, source_target_pairs={{0,24},{2,26},{4,28},{6,30},{8,16},{10,18},{12,20},{14,22},{16,8},... | collective-permute-start | bytes 159752 | tf_op jit(solution)/shard_map/ppermute | solution.py:680
  (18 other events, 133.7 us)
Sparse Core Ops, SparseCore 0:
  11.5 67.3 all-gather.1

commit v2 on v1

--- a/solution.py
+++ b/solution.py
@@ -369,7 +369,7 @@
         out_specs=[tiled(length, 512)] * 3, out_shape=[shape_of((rows * length, 512))] * 3,
         scratch_shapes=MASK_SCRATCH(length) + [pltpu.VMEM((length, 512), F32), pltpu.VMEM((length, 512), F32),
                                                pltpu.VMEM((4 * UNROLL, 128, BLOCK), F32)],
-        compiler_params=params(40 if causal else 60), cost_estimate=cost(20), name="self_back" if causal else "cross_back",
+        compiler_params=params(40 if causal else 56), cost_estimate=cost(20), name="self_back" if causal else "cross_back",
     )(*plan, q[0], k[0], v[0], delta, grad, lse, qseg, kseg, *after)
 
 
@@ -745,7 +745,7 @@
             r += 1
 
 
-def gather_weights(net, small, big):
+def gather_weights(net, small, big, early):
     qkv, so, cq, ckv, co, fin, fout = big
     if qkv.shape[0] % UNIT or net.bits < 5:
         small, big = lax.all_gather((small, big), AXES, axis=0, tiled=True) if net.count > 1 else (small, big)
@@ -753,7 +753,7 @@
         fout = fout.reshape(-1, 4, UNIT, 512).transpose(0, 2, 1, 3).reshape(512, 2048)
         rows = [jnp.pad(wide(v), (0, 2048 - v.shape[0])) for v in small]
         vectors = jnp.stack(rows + [jnp.zeros((2048,), F32)] * 6)
-        return qkv, vectors, jnp.concatenate([fin, fout, co], axis=1), lambda x: (x, jnp.concatenate([so, cq, ckv], axis=1))
+        return qkv, vectors, jnp.concatenate([fin, fout, co], axis=1), lambda x: (x, jnp.concatenate([so, cq, ckv], axis=1)), early
     packed, cross, rest = pl.pallas_call(
         pack_kernel, in_specs=[pl.BlockSpec(memory_space=pl.ANY)] * 17, out_specs=[vmem()] * 3,
         out_shape=[shape_of((1, UNIT, 1664)), shape_of((1, UNIT, 2048)), shape_of((UNIT, 4608))],
@@ -766,7 +766,7 @@
     masks = net.far_masks(orders[0][:far])[1:]
     everywhere = lambda x: jnp.concatenate([x] + [net.across(x, mask) for mask in masks], axis=0)
     packed = everywhere(packed)
-    packed, cross = lax.optimization_barrier((packed, cross))
+    packed, cross, early = lax.optimization_barrier((packed, cross, early))
     cross = everywhere(cross)
     parts = [packed[:, :, :896], packed[:, :, 896:], cross]
     orders = orders + orders[:1]
@@ -794,7 +794,7 @@
         scratch_shapes=[pltpu.VMEM((net.count, 16, 128), F32)],
         compiler_params=params(40), cost_estimate=cost(2), name="unpack",
     )(*gather_index, *pieces[0], *pieces[1])
-    return w, vectors, rest, cross_weights
+    return w, vectors, rest, cross_weights, early
 
 
 class Reduction:
@@ -846,11 +846,9 @@
     return values
 
 
-def together(groups):
-    if groups:
-        state = lax.optimization_barrier([(group.keep, group.send) for group in groups])
-        for group, (keep, send) in zip(groups, state):
-            group.keep, group.send = keep, send
+def behind(groups, leader):
+    for group in groups:
+        (group.keep, group.send), _ = lax.optimization_barrier(((group.keep, group.send), leader.send))
 
 
 def plan_self(seg, positions):
@@ -882,12 +880,10 @@
     cross_plan = plan_cross(target_segments, source_segments)
     tseg = wide(target_segments)[:, None, :]
     sseg = wide(source_segments)[:, None, :]
-    w_qkv, vectors, rest, cross_weights = gather_weights(net, small, (self_qkv, self_out, cross_query, cross_kv, cross_out, ffn_in, ffn_out))
-    if fast:
-        index_a, index_b = net.index(0), net.index(1)
-    else:
-        index_a = index_b = jnp.arange(512 // UNIT, dtype=jnp.int32)
-
+    index = (net.index(0), net.index(1)) if fast else (jnp.arange(512 // UNIT, dtype=jnp.int32),) * 2
+    w_qkv, vectors, rest, cross_weights, early = gather_weights(
+        net, small, (self_qkv, self_out, cross_query, cross_kv, cross_out, ffn_in, ffn_out), (self_plan, cross_plan, tseg, sseg, index))
+    self_plan, cross_plan, tseg, sseg, (index_a, index_b) = early
     (qkv, self_mix, self_lse), cross_w = cross_weights(tuple(self_forward(self_plan, target, w_qkv, vectors, tseg)))
     hid, cq, pairs, cross_mix, cross_lse = cross_forward(cross_plan, target, self_mix, memory, cross_w, vectors, tseg, sseg)
     output, h2, cross_mg, cross_delta, ffn_keep, ffn_send, dco, mid_small = middle(index_a, index_b, hid, cross_mix, out_grad, rest, vectors, length)
@@ -946,7 +942,7 @@
             memory_grad = memory_back(*cross_grads[1:], cross_w, tied)
         for group in open_groups:
             group.add()
-        together([group for group in open_groups if group.sums is None])
+        behind([group for group in open_groups[:-1] if group.sums is None], open_groups[-1])
     d_ffn, d_cross, d_self = (group.sums for group in groups)
     vectors_out = [d_self[j, 1536:1536 + n // net.count] for j, n in enumerate(VECTORS)]
     return (

time: 267 us -> 266 us (level)
    ppermute x33, starting transfers between devices: 47.8 us -> 51.5 us  [across(): return lax.ppermute(x, 'wide', [(i, i ^ mask) for i in range(self.wide)])]
    ppermute x9, starting transfers between devices: 14 us -> 10.9 us  [exchange(): lax.ppermute(x, 'narrow', [(i, i ^ 1 << bit) for i in range(self.narrow)])]
  transfers between devices with their start and end apart: 43 -> 43, of which waited for: 12 -> 13; matrix products, arithmetic and copies ran while one was open for 3% -> 3% of each run, Pallas kernels for 41% -> 41%
where the time goes in v2:
time: 266 us; the launch traced here: 264 us
  Pallas kernels  153 us (58%)
  starting transfers between devices  62.4 us (23%)
  waiting for transfers between devices  20.2 us (8%)
  between operations  14.9 us (6%)
  local copies, waits for them, and re-layouts  7.1 us (3%)
  other arithmetic  5.83 us (2%)
    ppermute x33, starting transfers between devices, across(): return lax.ppermute(x, 'wide', [(i, i ^ mask) for i in range(self.wide)])  51.5 us
    pallas_call x1, Pallas kernels, middle(): pl.pallas_call(mid_kernel, grid=(total // t,), in_specs=[smem(), smem(),...  43.8 us
    pallas_call x2, Pallas kernels, attend_back(): pl.pallas_call(functools.partial(back_kernel, causal), grid=(rows,), in_s...  39.3 us
    pallas_call x1, Pallas kernels, cross_forward(): pl.pallas_call(cross_kernel, grid=(rows,), in_specs=[smem(), smem(), tile...  22 us
    pallas_call x1, Pallas kernels, self_forward(): pl.pallas_call(self_kernel, grid=(rows,), in_specs=[smem(), smem(), tiled...  14.8 us
    pallas_call x1, Pallas kernels, cross_dense(): pl.pallas_call(cross_dense_kernel, grid=(total // t,), in_specs=[smem(),...  13 us
    ppermute x9, starting transfers between devices, exchange(): lax.ppermute(x, 'narrow', [(i, i ^ 1 << bit) for i in range(self.narrow)])  10.9 us
    ppermute x33, waiting for transfers between devices, across(): return lax.ppermute(x, 'wide', [(i, i ^ mask) for i in range(self.wide)])  10.3 us
  transfers between devices with their start and end apart: 43, of which 13 were waited for; matrix products, arithmetic and copies ran while one was open for 3% of the time, Pallas kernels for 41%

profile of v2, /device:TPU:0, one launch (start us, length us, event | category | flops | bytes accessed | tf_op | source)
XLA Modules:
  0.0 263.6 jit_solution(15588978353622919975)
XLA Ops:
  7.3 1.9 pack.1
  9.2 5.1 %collective-permute-start.2 = (bf16[1,16,1664]{2,1,0:T(8,128)(2,1)}, bf16[1,16,1664]{2,1,0:T(8,128)(2,1)S(1)}, u32[]{:S(2)}, u32[]{:S(2)}) collective-permute-start(bf16[1,16,1664]{2,1,0:T(8,128)(2,1)} %get-tuple-element.99), channel_id=1, source_target_pairs={{0,24},{2,26},{4,28},{6,30},{8,16},{10,18},{12,20},{14,22},{16,8},... | collective-permute-start | bytes 159752 | tf_op jit(solution)/shard_map/ppermute | solution.py:680
  17.5 1.2 collective-permute-done.1
  18.7 1.2 collective-permute-done
  20.8 1.8 collective-permute-start.5
  22.8 2.4 collective-permute-start.3
  25.2 0.9 constant_dynamic-update-slice_fusion.4
  26.1 1.6 collective-permute-start.12
  27.7 1.5 collective-permute-start.8
  29.2 1.2 collective-permute-done.3
  30.4 0.9 pad_maximum_fusion.3
  31.3 1.6 collective-permute-start.6
  33.8 1.1 collective-permute-start.9
  35.0 0.9 collective-permute-start.13
  36.4 4.3 %collective-permute-done.13.refs_5_ = bf16[8,16,768]{2,1,0:T(8,128)(2,1)S(1)} collective-permute-done((bf16[8,16,768]{2,1,0:T(8,128)(2,1)S(1)}, bf16[8,16,768]{2,1,0:T(8,128)(2,1)S(1)}, u32[]{:S(2)}, u32[]{:S(2)}) %collective-permute-start.13) | collective-permute-done | bytes 196640 | tf_op jit(solution)/shard_map/ppermute | solution.py:675
  41.3 1.2 collective-permute-start.7
  42.5 1.3 unpack.1
  43.8 14.8 %self_forward.1 = (bf16[2048,1536]{1,0:T(8,128)(2,1)}, bf16[2048,512]{1,0:T(8,128)(2,1)}, f32[2,8,1024]{2,1,0:T(8,128)S(1)}) custom-call(s32[2,8]{1,0:T(2,128)S(1)} %broadcast.63.first_ref, s32[2,8]{1,0:T(2,128)S(1)} %and_select_fusion.2.extra_ref, bf16[2048,512]{1,0:T(8,128)(2,1)S(1)} %copy-done.2, bf16[512,1536]{1,0:T(8,128)(2,1)S(1)} %get-tuple-element.109.w_ref, ...), custom_call_target="tpu_custom_call" | custom-call | flops 20000000000 | bytes 1048576 | tf_op jit(solution)/shard_map/self_forward/pallas_call | solution.py:253
  59.3 2.1 collective-permute-done.16.refs_2_
  61.4 0.9 collective-permute-done.17.refs_3_
  62.3 2.0 place.1.wo_ref.wq_ref.wkv_ref.w_ref
  64.3 22.0 %cross_forward.1 = (bf16[2048,512]{1,0:T(8,128)(2,1)}, bf16[2048,512]{1,0:T(8,128)(2,1)}, bf16[2048,1024]{1,0:T(8,128)(2,1)}, bf16[2048,512]{1,0:T(8,128)(2,1)}, f32[2,8,1024]{2,1,0:T(8,128)}) custom-call(s32[2,8]{1,0:T(2,128)} %get-tuple-element.103.first_ref, s32[2,8]{1,0:T(2,128)} %get-tuple-element.104.extra_ref, bf16[2048,512]{1,0:T(8,128)(2,1)} %x_ref.5, ...), custom_call_target="tpu_custom_call" | custom-call | flops 24999999488 | bytes 1048576 | tf_op jit(solution)/shard_map/cross_forward/pallas_call | solution.py:282
  86.4 43.8 %middle.1 = (bf16[2048,512]{1,0:T(8,128)(2,1)}, bf16[2048,512]{1,0:T(8,128)(2,1)}, bf16[2048,512]{1,0:T(8,128)(2,1)}, f32[2,8,1024]{2,1,0:T(8,128)}, bf16[16,16,...) custom-call(s32[32]{0:T(128)} %copy-done.4, s32[32]{0:T(128)} %copy-done.6, ...), custom_call_target="tpu_custom_call" | custom-call | flops 40000000000 | bytes 1048576 | tf_op jit(solution)/shard_map/middle/pallas_call | solution.py:482
  130.3 21.9 %cross_back.1 = (bf16[2048,512]{1,0:T(8,128)(2,1)}, bf16[2048,512]{1,0:T(8,128)(2,1)}, bf16[2048,512]{1,0:T(8,128)(2,1)}) custom-call(s32[2,8]{1,0:T(2,128)} %get-tuple-element.103.first_ref, s32[2,8]{1,0:T(2,128)} %get-tuple-element.104.extra_ref, bf16[2048,512]{1,0:T(8,128)(2,1)} %get-tuple-element.125.q_ref, ...), custom_call_target="tpu_custom_call" | custom-call | flops 20000000000 | bytes 1048576 | tf_op jit(solution)/shard_map/cross_back/pallas_call | solution.py:365
  153.1 3.3 %collective-permute-start.20 = (bf16[8,16,2048]{2,1,0:T(8,128)(2,1)S(1)}, bf16[8,16,2048]{2,1,0:T(8,128)(2,1)S(1)}, u32[]{:S(2)}, u32[]{:S(2)}) collective-permute-start(bf16[8,16,2048]{2,1,0:T(8,128)(2,1)S(1)} %get-tuple-element.184), channel_id=1, source_target_pairs={{0,1},{1,0},{2,3},{3,2},{4,5},{5,4},{6,7},{7,6},{8,9},{9,8},{10,11... | collective-permute-start | bytes 1572872 | tf_op jit(solution)/shard_map/ppermute | solution.py:675
  156.3 1.0 collective-permute-start.19
  157.3 13.0 %cross_dense.1 = (bf16[2048,512]{1,0:T(8,128)(2,1)S(1)}, bf16[2048,512]{1,0:T(8,128)(2,1)S(1)}, f32[2,8,1024]{2,1,0:T(8,128)S(1)}, bf16[16,16,2560]{2,1,0:T(8,12...) custom-call(s32[32]{0:T(128)S(1)} %copy-done.5, s32[32]{0:T(128)S(1)} %copy-done.7, ...), custom_call_target="tpu_custom_call" | custom-call | flops 12000000000 | bytes 1048576 | tf_op jit(solution)/shard_map/cross_dense/pallas_call | solution.py:543
  170.8 1.5 collective-permute-start.21
  172.3 1.0 collective-permute-start.22
  173.6 17.5 %self_back.1 = (bf16[2048,512]{1,0:T(8,128)(2,1)S(1)}, bf16[2048,512]{1,0:T(8,128)(2,1)S(1)}, bf16[2048,512]{1,0:T(8,128)(2,1)S(1)}) custom-call(s32[2,8]{1,0:T(2,128)S(1)} %broadcast.63.first_ref, s32[2,8]{1,0:T(2,128)S(1)} %and_select_fusion.2.extra_ref, bf16[2048,1536]{1,0:T(8,128)(2,1)} %get-tuple-element.149.q_ref.k_ref.v_ref, ...), custom_call_target="tpu_custom_call" | custom-call | flops 20000000000 | bytes 1048576 | tf_op jit(solution)/shard_map/self_back/pallas_call | solution.py:365
  191.4 9.3 %collective-permute-start.26 = (bf16[1,16,4096]{2,1,0:T(8,128)(2,1)S(1)}, bf16[1,16,4096]{2,1,0:T(8,128)(2,1)S(1)}, u32[]{:S(2)}, u32[]{:S(2)}) collective-permute-start(bf16[1,16,4096]{2,1,0:T(8,128)(2,1)S(1)} %get-tuple-element.190), channel_id=1, source_target_pairs={{0,24},{2,26},{4,28},{6,30},{8,16},{10,18},{12,20},{14,22},{16,8},... | collective-permute-start | bytes 393224 | tf_op jit(solution)/shard_map/ppermute | solution.py:680
  202.0 11.3 %collective-permute-start.27 = (bf16[8,16,1280]{2,1,0:T(8,128)(2,1)S(1)}, bf16[8,16,1280]{2,1,0:T(8,128)(2,1)S(1)}, u32[]{:S(2)}, u32[]{:S(2)}) collective-permute-start(bf16[8,16,1280]{2,1,0:T(8,128)(2,1)S(1)} %get-tuple-element.189), channel_id=1, source_target_pairs={{0,4},{2,6},{4,0},{6,2},{8,12},{10,14},{12,8},{14,10},{16,20},{18,... | collective-permute-start | bytes 983048 | tf_op jit(solution)/shard_map/ppermute | solution.py:680
  213.2 6.2 %self_grad.1 = (bf16[16,16,1664]{2,1,0:T(8,128)(2,1)S(1)}, bf16[16,16,1664]{2,1,0:T(8,128)(2,1)S(1)}, f32[16,2048]{1,0:T(8,128)}) custom-call(s32[32]{0:T(128)S(1)} %copy-done.5, s32[32]{0:T(128)S(1)} %copy-done.7, bf16[2048,512]{1,0:T(8,128)(2,1)S(1)} %get-tuple-element.156.dq_ref, bf16[2048,512]{1,0:T(8,128)(2,1)S(1)} %get-tuple-element.157.dk_ref, ...), custom_call_target="tpu_custom_call" | custom-call | flops 5000000000 | bytes 1048576 | tf_op jit(solution)/shard_map/self_grad/pallas_call | solution.py:631
  221.1 1.4 collective-permute-start.30
  223.2 2.0 collective-permute-done.29
  225.3 1.2 collective-permute-done.30
  226.9 1.4 collective-permute-start.32
  229.2 2.3 collective-permute-start.39
  231.5 2.0 collective-permute-start.40
  233.6 4.9 %target_grad.1 = bf16[2048,512]{1,0:T(8,128)(2,1)} custom-call(bf16[2048,512]{1,0:T(8,128)(2,1)S(1)} %get-tuple-element.145.h1_ref, bf16[2048,512]{1,0:T(8,128)(2,1)S(1)} %get-tuple-element.156.dq_ref, bf16[2048,512]{1,0:T(8,128)(2,1)S(1)} %get-tuple-element.157.dk_ref, bf16[2048,512]{1,0:T(8,128)(2,1)S(1)} %get-tuple-element.158.dv_ref, ...), custom_call_target="tpu_custom_call" | custom-call | flops 5000000000 | bytes 1048576 | tf_op jit(solution)/shard_map/target_grad/pallas_call | solution.py:651
  238.5 1.3 collective-permute-done.41
  241.8 1.3 collective-permute-start.35
  243.2 2.6 collective-permute-done.34
  245.8 0.9 collective-permute-done.35
  246.8 0.9 collective-permute-start.36
  247.7 1.7 collective-permute-start.38
  249.4 0.9 collective-permute-start.37
  250.3 3.9 %memory_grad.1 = bf16[2048,512]{1,0:T(8,128)(2,1)} custom-call(bf16[2048,512]{1,0:T(8,128)(2,1)S(1)} %copy-done.10, bf16[2048,512]{1,0:T(8,128)(2,1)S(1)} %copy-done.12, bf16[512,2048]{1,0:T(8,128)(2,1)S(1)} %copy-done.8, bf16[4,16,768]{2,1,0:T(8,128)(2,1)S(1)} %slice.322.refs_0_, bf16[4,16,896]{2,1,0:T(8,128)(2,1)S(1)} %slice.324.refs_1_), custom_call_target="tpu_custom_call" | custom-call | flops 4000000000 | bytes 1048576 | tf_op jit(solution)/shard_map/memory_grad/pallas_call | solution.py:561
  (164 shorter events, 18.1 us)
Async XLA Ops:
  7.2 79.2 %all-gather.2.cloned.1.call-start = ((), (), s32[]{:S(2)}) async-start(), calls=%async_computation | async-start | bytes 4866048 | tf_op jit(solution)/shard_map/all_gather | solution.py:763
  9.2 8.3 %collective-permute-start.2 = (bf16[1,16,1664]{2,1,0:T(8,128)(2,1)}, bf16[1,16,1664]{2,1,0:T(8,128)(2,1)S(1)}, u32[]{:S(2)}, u32[]{:S(2)}) collective-permute-start(bf16[1,16,1664]{2,1,0:T(8,128)(2,1)} %get-tuple-element.99), channel_id=1, source_target_pairs={{0,24},{2,26},{4,28},{6,30},{8,16},{10,18},{12,20},{14,22},{16,8},... | collective-permute-start | bytes 159752 | tf_op jit(solution)/shard_map/ppermute | solution.py:680
  14.3 4.4 %collective-permute-start.1 = (bf16[1,16,1664]{2,1,0:T(8,128)(2,1)}, bf16[1,16,1664]{2,1,0:T(8,128)(2,1)S(1)}, u32[]{:S(2)}, u32[]{:S(2)}) collective-permute-start(bf16[1,16,1664]{2,1,0:T(8,128)(2,1)} %get-tuple-element.99), channel_id=1, source_target_pairs={{0,8},{2,10},{4,12},{6,14},{8,0},{10,2},{12,4},{14,6},{16,24},{18,... | collective-permute-start | bytes 159752 | tf_op jit(solution)/shard_map/ppermute | solution.py:680
  14.3 5.6 %collective-permute-start = (bf16[1,16,1664]{2,1,0:T(8,128)(2,1)}, bf16[1,16,1664]{2,1,0:T(8,128)(2,1)S(1)}, u32[]{:S(2)}, u32[]{:S(2)}) collective-permute-start(bf16[1,16,1664]{2,1,0:T(8,128)(2,1)} %get-tuple-element.99), channel_id=1, source_target_pairs={{0,16},{2,18},{4,20},{6,22},{8,24},{10,26},{12,28},{14,30},{16,0},... | collective-permute-start | bytes 159752 | tf_op jit(solution)/shard_map/ppermute | solution.py:680
  16.2 46.1 %copy-start.4 = (s32[32]{0:T(128)}, s32[32]{0:T(128)S(1)}, u32[]{:S(2)}) copy-start(s32[32]{0:T(128)S(1)} %broadcast_xor_fusion.1.index_a.index) | copy-start | bytes 388
  16.9 26.9 %copy-start.6 = (s32[32]{0:T(128)}, s32[32]{0:T(128)S(1)}, u32[]{:S(2)}) copy-start(s32[32]{0:T(128)S(1)} %broadcast_xor_fusion.index_b) | copy-start | bytes 388
  16.9 26.9 %copy-start = (f32[2,1,1024]{2,1,0:T(1,128)}, f32[2,1,1024]{2,1,0:T(1,128)S(1)}, u32[]{:S(2)}) copy-start(f32[2,1,1024]{2,1,0:T(1,128)S(1)} %broadcast_in_dim.58.seg_ref.qseg_ref.kseg_ref) | copy-start | bytes 24580
  20.8 8.4 %collective-permute-start.5 = (bf16[1,16,2048]{2,1,0:T(8,128)(2,1)}, bf16[1,16,2048]{2,1,0:T(8,128)(2,1)S(1)}, u32[]{:S(2)}, u32[]{:S(2)}) collective-permute-start(bf16[1,16,2048]{2,1,0:T(8,128)(2,1)} %get-tuple-element.105), channel_id=1, source_target_pairs={{0,24},{2,26},{4,28},{6,30},{8,16},{10,18},{12,20},{14,22},{16,8},... | collective-permute-start | bytes 196616 | tf_op jit(solution)/shard_map/ppermute | solution.py:680
  22.5 6.7 %collective-permute-start.4 = (bf16[1,16,2048]{2,1,0:T(8,128)(2,1)}, bf16[1,16,2048]{2,1,0:T(8,128)(2,1)S(1)}, u32[]{:S(2)}, u32[]{:S(2)}) collective-permute-start(bf16[1,16,2048]{2,1,0:T(8,128)(2,1)} %get-tuple-element.105), channel_id=1, source_target_pairs={{0,8},{2,10},{4,12},{6,14},{8,0},{10,2},{12,4},{14,6},{16,24},{18,... | collective-permute-start | bytes 196616 | tf_op jit(solution)/shard_map/ppermute | solution.py:680
  22.8 7.7 %collective-permute-start.3 = (bf16[1,16,2048]{2,1,0:T(8,128)(2,1)}, bf16[1,16,2048]{2,1,0:T(8,128)(2,1)S(1)}, u32[]{:S(2)}, u32[]{:S(2)}) collective-permute-start(bf16[1,16,2048]{2,1,0:T(8,128)(2,1)} %get-tuple-element.105), channel_id=1, source_target_pairs={{0,16},{2,18},{4,20},{6,22},{8,24},{10,26},{12,28},{14,30},{16,0},... | collective-permute-start | bytes 196616 | tf_op jit(solution)/shard_map/ppermute | solution.py:680
  26.1 8.8 %collective-permute-start.12 = (bf16[4,16,768]{2,1,0:T(8,128)(2,1)S(1)}, bf16[4,16,768]{2,1,0:T(8,128)(2,1)S(1)}, u32[]{:S(2)}, u32[]{:S(2)}) collective-permute-start(bf16[4,16,768]{2,1,0:T(8,128)(2,1)S(1)} %slice.238), channel_id=1, source_target_pairs={{0,4},{2,6},{4,0},{6,2},{8,12},{10,14},{12,8},{14,10},{16,20},{18,... | collective-permute-start | bytes 294920 | tf_op jit(solution)/shard_map/ppermute | solution.py:680
  27.7 6.1 %collective-permute-start.8 = (bf16[4,16,896]{2,1,0:T(8,128)(2,1)S(1)}, bf16[4,16,896]{2,1,0:T(8,128)(2,1)S(1)}, u32[]{:S(2)}, u32[]{:S(2)}) collective-permute-start(bf16[4,16,896]{2,1,0:T(8,128)(2,1)S(1)} %slice.237), channel_id=1, source_target_pairs={{0,1},{1,0},{2,3},{3,2},{4,5},{5,4},{6,7},{7,6},{8,9},{9,8},{10,11... | collective-permute-start | bytes 344072 | tf_op jit(solution)/shard_map/ppermute | solution.py:675
  31.3 9.9 %collective-permute-start.6 = (bf16[4,16,2048]{2,1,0:T(8,128)(2,1)S(1)}, bf16[4,16,2048]{2,1,0:T(8,128)(2,1)S(1)}, u32[]{:S(2)}, u32[]{:S(2)}) collective-permute-start(bf16[4,16,2048]{2,1,0:T(8,128)(2,1)S(1)} %pad_maximum_fusion.3), channel_id=1, source_target_pairs={{0,1},{1,0},{2,3},{3,2},{4,5},{5,4},{6,7},{7,6},{8,9},{9,8},{10,11... | collective-permute-start | bytes 786440 | tf_op jit(solution)/shard_map/ppermute | solution.py:675
  33.8 6.9 %collective-permute-start.9 = (bf16[8,16,896]{2,1,0:T(8,128)(2,1)S(1)}, bf16[8,16,896]{2,1,0:T(8,128)(2,1)S(1)}, u32[]{:S(2)}, u32[]{:S(2)}) collective-permute-start(bf16[8,16,896]{2,1,0:T(8,128)(2,1)S(1)} %pad_maximum_fusion.4.refs_0_), channel_id=1, source_target_pairs={{0,4},{2,6},{4,0},{6,2},{8,12},{10,14},{12,8},{14,10},{16,20},{18,... | collective-permute-start | bytes 688136 | tf_op jit(solution)/shard_map/ppermute | solution.py:680
  35.0 5.7 %collective-permute-start.13 = (bf16[8,16,768]{2,1,0:T(8,128)(2,1)S(1)}, bf16[8,16,768]{2,1,0:T(8,128)(2,1)S(1)}, u32[]{:S(2)}, u32[]{:S(2)}) collective-permute-start(bf16[8,16,768]{2,1,0:T(8,128)(2,1)S(1)} %pad_maximum_fusion.6.refs_4_), channel_id=1, source_target_pairs={{0,1},{1,0},{2,3},{3,2},{4,5},{5,4},{6,7},{7,6},{8,9},{9,8},{10,11... | collective-permute-start | bytes 589832 | tf_op jit(solution)/shard_map/ppermute | solution.py:675
  35.9 6.6 %collective-permute-start.14 = (bf16[8,16,768]{2,1,0:T(8,128)(2,1)S(1)}, bf16[8,16,768]{2,1,0:T(8,128)(2,1)S(1)}, u32[]{:S(2)}, u32[]{:S(2)}) collective-permute-start(bf16[8,16,768]{2,1,0:T(8,128)(2,1)S(1)} %pad_maximum_fusion.6.refs_4_), channel_id=1, source_target_pairs={{0,2},{2,0},{4,6},{6,4},{8,10},{10,8},{12,14},{14,12},{16,18},{18,... | collective-permute-start | bytes 589832 | tf_op jit(solution)/shard_map/ppermute | solution.py:680
  35.9 6.6 %collective-permute-start.10 = (bf16[8,16,896]{2,1,0:T(8,128)(2,1)S(1)}, bf16[8,16,896]{2,1,0:T(8,128)(2,1)S(1)}, u32[]{:S(2)}, u32[]{:S(2)}) collective-permute-start(bf16[8,16,896]{2,1,0:T(8,128)(2,1)S(1)} %pad_maximum_fusion.4.refs_0_), channel_id=1, source_target_pairs={{0,2},{2,0},{4,6},{6,4},{8,10},{10,8},{12,14},{14,12},{16,18},{18,... | collective-permute-start | bytes 688136 | tf_op jit(solution)/shard_map/ppermute | solution.py:680
  40.7 1.8 collective-permute-start.15
  40.7 1.8 collective-permute-start.11
  41.3 17.4 %collective-permute-start.7 = (bf16[8,16,2048]{2,1,0:T(8,128)(2,1)S(1)}, bf16[8,16,2048]{2,1,0:T(8,128)(2,1)S(1)}, u32[]{:S(2)}, u32[]{:S(2)}) collective-permute-start(bf16[8,16,2048]{2,1,0:T(8,128)(2,1)S(1)} %constant_dynamic-update-slice_fusion.refs_0_), channel_id=1, source_target_pairs={{0,4},{2,6},{4,0},{6,2},{8,12},{10,14},{12,8},{14,10},{16,20},{18,... | collective-permute-start | bytes 1572872 | tf_op jit(solution)/shard_map/ppermute | solution.py:680
  58.7 2.7 %collective-permute-start.16 = (bf16[8,16,2048]{2,1,0:T(8,128)(2,1)S(1)}, bf16[8,16,2048]{2,1,0:T(8,128)(2,1)S(1)}, u32[]{:S(2)}, u32[]{:S(2)}) collective-permute-start(bf16[8,16,2048]{2,1,0:T(8,128)(2,1)S(1)} %constant_dynamic-update-slice_fusion.refs_0_), channel_id=1, source_target_pairs={{0,2},{2,0},{4,6},{6,4},{8,10},{10,8},{12,14},{14,12},{16,18},{18,... | collective-permute-start | bytes 1572872 | tf_op jit(solution)/shard_map/ppermute | solution.py:680
  59.0 3.4 %collective-permute-start.17 = (bf16[8,16,2048]{2,1,0:T(8,128)(2,1)S(1)}, bf16[8,16,2048]{2,1,0:T(8,128)(2,1)S(1)}, u32[]{:S(2)}, u32[]{:S(2)}) collective-permute-start(bf16[8,16,2048]{2,1,0:T(8,128)(2,1)S(1)} %collective-permute-done.7.refs_1_), channel_id=1, source_target_pairs={{0,2},{2,0},{4,6},{6,4},{8,10},{10,8},{12,14},{14,12},{16,18},{18,... | collective-permute-start | bytes 1572872 | tf_op jit(solution)/shard_map/ppermute | solution.py:680
  130.2 21.9 %collective-permute-start.18 = (bf16[16,16,4096]{2,1,0:T(8,128)(2,1)}, bf16[16,16,4096]{2,1,0:T(8,128)(2,1)S(1)}, u32[]{:S(2)}, u32[]{:S(2)}) collective-permute-start(bf16[16,16,4096]{2,1,0:T(8,128)(2,1)} %get-tuple-element.124.refs_0_), channel_id=1, source_target_pairs={{0,2},{2,0},{4,6},{6,4},{8,10},{10,8},{12,14},{14,12},{16,18},{18,... | collective-permute-start | bytes 6291464 | tf_op jit(solution)/shard_map/ppermute | solution.py:680
  130.2 21.9 %copy-start.18 = (bf16[16,16,4096]{2,1,0:T(8,128)(2,1)S(1)}, bf16[16,16,4096]{2,1,0:T(8,128)(2,1)}, u32[]{:S(2)}) copy-start(bf16[16,16,4096]{2,1,0:T(8,128)(2,1)} %get-tuple-element.123) | copy-start | bytes 6291460
  153.1 17.3 %collective-permute-start.20 = (bf16[8,16,2048]{2,1,0:T(8,128)(2,1)S(1)}, bf16[8,16,2048]{2,1,0:T(8,128)(2,1)S(1)}, u32[]{:S(2)}, u32[]{:S(2)}) collective-permute-start(bf16[8,16,2048]{2,1,0:T(8,128)(2,1)S(1)} %get-tuple-element.184), channel_id=1, source_target_pairs={{0,1},{1,0},{2,3},{3,2},{4,5},{5,4},{6,7},{7,6},{8,9},{9,8},{10,11... | collective-permute-start | bytes 1572872 | tf_op jit(solution)/shard_map/ppermute | solution.py:675
  156.3 14.0 %collective-permute-start.19 = (bf16[8,16,2048]{2,1,0:T(8,128)(2,1)S(1)}, bf16[8,16,2048]{2,1,0:T(8,128)(2,1)S(1)}, u32[]{:S(2)}, u32[]{:S(2)}) collective-permute-start(bf16[8,16,2048]{2,1,0:T(8,128)(2,1)S(1)} %get-tuple-element.185), channel_id=1, source_target_pairs={{0,4},{2,6},{4,0},{6,2},{8,12},{10,14},{12,8},{14,10},{16,20},{18,... | collective-permute-start | bytes 1572872 | tf_op jit(solution)/shard_map/ppermute | solution.py:680
  170.8 20.3 %collective-permute-start.21 = (bf16[4,16,2048]{2,1,0:T(8,128)(2,1)S(1)}, bf16[4,16,2048]{2,1,0:T(8,128)(2,1)S(1)}, u32[]{:S(2)}, u32[]{:S(2)}) collective-permute-start(bf16[4,16,2048]{2,1,0:T(8,128)(2,1)S(1)} %slice.298.refs_0_), channel_id=1, source_target_pairs={{0,1},{1,0},{2,3},{3,2},{4,5},{5,4},{6,7},{7,6},{8,9},{9,8},{10,11... | collective-permute-start | bytes 786440 | tf_op jit(solution)/shard_map/ppermute | solution.py:675
  172.3 18.8 %collective-permute-start.22 = (bf16[4,16,2048]{2,1,0:T(8,128)(2,1)S(1)}, bf16[4,16,2048]{2,1,0:T(8,128)(2,1)S(1)}, u32[]{:S(2)}, u32[]{:S(2)}) collective-permute-start(bf16[4,16,2048]{2,1,0:T(8,128)(2,1)S(1)} %slice.300.refs_1_), channel_id=1, source_target_pairs={{0,4},{2,6},{4,0},{6,2},{8,12},{10,14},{12,8},{14,10},{16,20},{18,... | collective-permute-start | bytes 786440 | tf_op jit(solution)/shard_map/ppermute | solution.py:680
  173.2 17.9 %collective-permute-start.23 = (bf16[16,16,2560]{2,1,0:T(8,128)(2,1)S(1)}, bf16[16,16,2560]{2,1,0:T(8,128)(2,1)S(1)}, u32[]{:S(2)}, u32[]{:S(2)}) collective-permute-start(bf16[16,16,2560]{2,1,0:T(8,128)(2,1)S(1)} %get-tuple-element.148.refs_2_), channel_id=1, source_target_pairs={{0,2},{2,0},{4,6},{6,4},{8,10},{10,8},{12,14},{14,12},{16,18},{18,... | collective-permute-start | bytes 3932168 | tf_op jit(solution)/shard_map/ppermute | solution.py:680
  191.4 28.1 %collective-permute-start.26 = (bf16[1,16,4096]{2,1,0:T(8,128)(2,1)S(1)}, bf16[1,16,4096]{2,1,0:T(8,128)(2,1)S(1)}, u32[]{:S(2)}, u32[]{:S(2)}) collective-permute-start(bf16[1,16,4096]{2,1,0:T(8,128)(2,1)S(1)} %get-tuple-element.190), channel_id=1, source_target_pairs={{0,24},{2,26},{4,28},{6,30},{8,16},{10,18},{12,20},{14,22},{16,8},... | collective-permute-start | bytes 393224 | tf_op jit(solution)/shard_map/ppermute | solution.py:680
  200.7 18.8 %collective-permute-start.25 = (bf16[1,16,4096]{2,1,0:T(8,128)(2,1)S(1)}, bf16[1,16,4096]{2,1,0:T(8,128)(2,1)S(1)}, u32[]{:S(2)}, u32[]{:S(2)}) collective-permute-start(bf16[1,16,4096]{2,1,0:T(8,128)(2,1)S(1)} %get-tuple-element.191), channel_id=1, source_target_pairs={{0,8},{2,10},{4,12},{6,14},{8,0},{10,2},{12,4},{14,6},{16,24},{18,... | collective-permute-start | bytes 393224 | tf_op jit(solution)/shard_map/ppermute | solution.py:680
  200.7 18.8 %collective-permute-start.24 = (bf16[1,16,4096]{2,1,0:T(8,128)(2,1)S(1)}, bf16[1,16,4096]{2,1,0:T(8,128)(2,1)S(1)}, u32[]{:S(2)}, u32[]{:S(2)}) collective-permute-start(bf16[1,16,4096]{2,1,0:T(8,128)(2,1)S(1)} %get-tuple-element.192), channel_id=1, source_target_pairs={{0,16},{2,18},{4,20},{6,22},{8,24},{10,26},{12,28},{14,30},{16,0},... | collective-permute-start | bytes 393224 | tf_op jit(solution)/shard_map/ppermute | solution.py:680
  201.8 17.6 %collective-permute-start.28 = (bf16[8,16,1280]{2,1,0:T(8,128)(2,1)S(1)}, bf16[8,16,1280]{2,1,0:T(8,128)(2,1)S(1)}, u32[]{:S(2)}, u32[]{:S(2)}) collective-permute-start(bf16[8,16,1280]{2,1,0:T(8,128)(2,1)S(1)} %get-tuple-element.188), channel_id=1, source_target_pairs={{0,1},{1,0},{2,3},{3,2},{4,5},{5,4},{6,7},{7,6},{8,9},{9,8},{10,11... | collective-permute-start | bytes 983048 | tf_op jit(solution)/shard_map/ppermute | solution.py:675
  202.0 17.7 %collective-permute-start.27 = (bf16[8,16,1280]{2,1,0:T(8,128)(2,1)S(1)}, bf16[8,16,1280]{2,1,0:T(8,128)(2,1)S(1)}, u32[]{:S(2)}, u32[]{:S(2)}) collective-permute-start(bf16[8,16,1280]{2,1,0:T(8,128)(2,1)S(1)} %get-tuple-element.189), channel_id=1, source_target_pairs={{0,4},{2,6},{4,0},{6,2},{8,12},{10,14},{12,8},{14,10},{16,20},{18,... | collective-permute-start | bytes 983048 | tf_op jit(solution)/shard_map/ppermute | solution.py:680
  219.9 5.4 %collective-permute-start.29 = (bf16[4,16,1280]{2,1,0:T(8,128)(2,1)S(1)}, bf16[4,16,1280]{2,1,0:T(8,128)(2,1)S(1)}, u32[]{:S(2)}, u32[]{:S(2)}) collective-permute-start(bf16[4,16,1280]{2,1,0:T(8,128)(2,1)S(1)} %slice.310), channel_id=1, source_target_pairs={{0,1},{1,0},{2,3},{3,2},{4,5},{5,4},{6,7},{7,6},{8,9},{9,8},{10,11... | collective-permute-start | bytes 491528 | tf_op jit(solution)/shard_map/ppermute | solution.py:675
  221.1 5.4 %collective-permute-start.30 = (bf16[4,16,1280]{2,1,0:T(8,128)(2,1)S(1)}, bf16[4,16,1280]{2,1,0:T(8,128)(2,1)S(1)}, u32[]{:S(2)}, u32[]{:S(2)}) collective-permute-start(bf16[4,16,1280]{2,1,0:T(8,128)(2,1)S(1)} %slice.313), channel_id=1, source_target_pairs={{0,4},{2,6},{4,0},{6,2},{8,12},{10,14},{12,8},{14,10},{16,20},{18,... | collective-permute-start | bytes 491528 | tf_op jit(solution)/shard_map/ppermute | solution.py:680
  222.6 4.1 %collective-permute-start.31 = (bf16[16,16,1664]{2,1,0:T(8,128)(2,1)S(1)}, bf16[16,16,1664]{2,1,0:T(8,128)(2,1)S(1)}, u32[]{:S(2)}, u32[]{:S(2)}) collective-permute-start(bf16[16,16,1664]{2,1,0:T(8,128)(2,1)S(1)} %get-tuple-element.170), channel_id=1, source_target_pairs={{0,2},{2,0},{4,6},{6,4},{8,10},{10,8},{12,14},{14,12},{16,18},{18,... | collective-permute-start | bytes 2555912 | tf_op jit(solution)/shard_map/ppermute | solution.py:680
  226.9 14.1 %collective-permute-start.32 = (bf16[8,16,768]{2,1,0:T(8,128)(2,1)S(1)}, bf16[8,16,768]{2,1,0:T(8,128)(2,1)S(1)}, u32[]{:S(2)}, u32[]{:S(2)}) collective-permute-start(bf16[8,16,768]{2,1,0:T(8,128)(2,1)S(1)} %slice.319.refs_3_), channel_id=1, source_target_pairs={{0,4},{2,6},{4,0},{6,2},{8,12},{10,14},{12,8},{14,10},{16,20},{18,... | collective-permute-start | bytes 589832 | tf_op jit(solution)/shard_map/ppermute | solution.py:680
  228.4 13.4 %collective-permute-start.33 = (bf16[8,16,896]{2,1,0:T(8,128)(2,1)S(1)}, bf16[8,16,896]{2,1,0:T(8,128)(2,1)S(1)}, u32[]{:S(2)}, u32[]{:S(2)}) collective-permute-start(bf16[8,16,896]{2,1,0:T(8,128)(2,1)S(1)} %slice.320.refs_4_), channel_id=1, source_target_pairs={{0,1},{1,0},{2,3},{3,2},{4,5},{5,4},{6,7},{7,6},{8,9},{9,8},{10,11... | collective-permute-start | bytes 688136 | tf_op jit(solution)/shard_map/ppermute | solution.py:675
  229.2 9.3 %collective-permute-start.39 = (bf16[1,16,2560]{2,1,0:T(8,128)(2,1)S(1)}, bf16[1,16,2560]{2,1,0:T(8,128)(2,1)S(1)}, u32[]{:S(2)}, u32[]{:S(2)}) collective-permute-start(bf16[1,16,2560]{2,1,0:T(8,128)(2,1)S(1)} %get-tuple-element.171.refs_0_), channel_id=1, source_target_pairs={{0,16},{2,18},{4,20},{6,22},{8,24},{10,26},{12,28},{14,30},{16,0},... | collective-permute-start | bytes 245768 | tf_op jit(solution)/shard_map/ppermute | solution.py:680
  231.5 7.0 %collective-permute-start.40 = (bf16[1,16,2560]{2,1,0:T(8,128)(2,1)S(1)}, bf16[1,16,2560]{2,1,0:T(8,128)(2,1)S(1)}, u32[]{:S(2)}, u32[]{:S(2)}) collective-permute-start(bf16[1,16,2560]{2,1,0:T(8,128)(2,1)S(1)} %get-tuple-element.172.refs_1_), channel_id=1, source_target_pairs={{0,8},{2,10},{4,12},{6,14},{8,0},{10,2},{12,4},{14,6},{16,24},{18,... | collective-permute-start | bytes 245768 | tf_op jit(solution)/shard_map/ppermute | solution.py:680
  233.5 6.2 %collective-permute-start.41 = (bf16[1,16,2560]{2,1,0:T(8,128)(2,1)S(1)}, bf16[1,16,2560]{2,1,0:T(8,128)(2,1)S(1)}, u32[]{:S(2)}, u32[]{:S(2)}) collective-permute-start(bf16[1,16,2560]{2,1,0:T(8,128)(2,1)S(1)} %get-tuple-element.173.refs_2_), channel_id=1, source_target_pairs={{0,24},{2,26},{4,28},{6,30},{8,16},{10,18},{12,20},{14,22},{16,8},... | collective-permute-start | bytes 245768 | tf_op jit(solution)/shard_map/ppermute | solution.py:680
  233.6 16.8 %copy-start.12 = (bf16[2048,512]{1,0:T(8,128)(2,1)S(1)}, bf16[2048,512]{1,0:T(8,128)(2,1)}, u32[]{:S(2)}) copy-start(bf16[2048,512]{1,0:T(8,128)(2,1)} %get-tuple-element.136.cv_ref) | copy-start | bytes 6291460
  241.1 4.7 %collective-permute-start.34 = (bf16[4,16,768]{2,1,0:T(8,128)(2,1)S(1)}, bf16[4,16,768]{2,1,0:T(8,128)(2,1)S(1)}, u32[]{:S(2)}, u32[]{:S(2)}) collective-permute-start(bf16[4,16,768]{2,1,0:T(8,128)(2,1)S(1)} %slice.322.refs_0_), channel_id=1, source_target_pairs={{0,1},{1,0},{2,3},{3,2},{4,5},{5,4},{6,7},{7,6},{8,9},{9,8},{10,11... | collective-permute-start | bytes 294920 | tf_op jit(solution)/shard_map/ppermute | solution.py:675
  241.8 4.9 %collective-permute-start.35 = (bf16[4,16,896]{2,1,0:T(8,128)(2,1)S(1)}, bf16[4,16,896]{2,1,0:T(8,128)(2,1)S(1)}, u32[]{:S(2)}, u32[]{:S(2)}) collective-permute-start(bf16[4,16,896]{2,1,0:T(8,128)(2,1)S(1)} %slice.324.refs_1_), channel_id=1, source_target_pairs={{0,4},{2,6},{4,0},{6,2},{8,12},{10,14},{12,8},{14,10},{16,20},{18,... | collective-permute-start | bytes 344072 | tf_op jit(solution)/shard_map/ppermute | solution.py:680
  246.8 7.5 %collective-permute-start.36 = (bf16[1,16,1664]{2,1,0:T(8,128)(2,1)S(1)}, bf16[1,16,1664]{2,1,0:T(8,128)(2,1)S(1)}, u32[]{:S(2)}, u32[]{:S(2)}) collective-permute-start(bf16[1,16,1664]{2,1,0:T(8,128)(2,1)S(1)} %get-tuple-element.200), channel_id=1, source_target_pairs={{0,16},{2,18},{4,20},{6,22},{8,24},{10,26},{12,28},{14,30},{16,0},... | collective-permute-start | bytes 159752 | tf_op jit(solution)/shard_map/ppermute | solution.py:680
  247.7 6.6 %collective-permute-start.38 = (bf16[1,16,1664]{2,1,0:T(8,128)(2,1)S(1)}, bf16[1,16,1664]{2,1,0:T(8,128)(2,1)S(1)}, u32[]{:S(2)}, u32[]{:S(2)}) collective-permute-start(bf16[1,16,1664]{2,1,0:T(8,128)(2,1)S(1)} %get-tuple-element.201), channel_id=1, source_target_pairs={{0,24},{2,26},{4,28},{6,30},{8,16},{10,18},{12,20},{14,22},{16,8},... | collective-permute-start | bytes 159752 | tf_op jit(solution)/shard_map/ppermute | solution.py:680
  249.4 4.9 %collective-permute-start.37 = (bf16[1,16,1664]{2,1,0:T(8,128)(2,1)S(1)}, bf16[1,16,1664]{2,1,0:T(8,128)(2,1)S(1)}, u32[]{:S(2)}, u32[]{:S(2)}) collective-permute-start(bf16[1,16,1664]{2,1,0:T(8,128)(2,1)S(1)} %get-tuple-element.202), channel_id=1, source_target_pairs={{0,8},{2,10},{4,12},{6,14},{8,0},{10,2},{12,4},{14,6},{16,24},{18,... | collective-permute-start | bytes 159752 | tf_op jit(solution)/shard_map/ppermute | solution.py:680
  (18 other events, 138.3 us)
Sparse Core Ops, SparseCore 0:
  11.5 67.7 all-gather.1

commit v3 on v2

--- a/solution.py
+++ b/solution.py
@@ -798,8 +798,8 @@
 
 
 class Reduction:
-    def __init__(self, net, keep, send, cut):
-        self.net, self.cut = net, cut
+    def __init__(self, net, keep, send, cut, direct=True):
+        self.net, self.cut, self.direct = net, cut, direct
         self.keep, self.send = [keep], [send]
         self.stage = 0
         self.sums = None
@@ -810,7 +810,7 @@
     def start(self):
         if self.sums is not None:
             return
-        if self.stage < self.net.near:
+        if self.stage < self.net.near or not self.direct:
             self.got = [self.net.exchange(x, order[self.stage]) for x, order in zip(self.send, self.net.orders)]
         else:
             far = self.net.far_masks(self.net.orders[0][:self.net.near - 1:-1])
@@ -820,12 +820,17 @@
         if self.sums is not None:
             return
         self.stage += 1
-        if self.stage > self.net.near:
+        if self.direct and self.stage > self.net.near:
             self.sums = sum((wide(got[0]) for got in self.got), self.keep[0][0])
             return
         sums = [wide(k) + wide(g) for k, g in zip(self.keep, self.got)]
+        if self.stage == self.net.bits:
+            self.sums = sums[0][0]
+            return
         if self.stage == 1:
             sums = [sums[0][:, :, :self.cut], sums[0][:, :, self.cut:]]
+        elif self.stage == self.net.near and not self.direct:
+            sums = [jnp.concatenate(sums, axis=2)]
         elif self.stage == self.net.near:
             total = jnp.concatenate(sums, axis=2)
             self.keep = [total[:1]]
@@ -909,7 +914,7 @@
     for group in groups:
         group.add()
     if fast:
-        groups.append(Reduction(net, cross_keep, cross_send, 1280))
+        groups.append(Reduction(net, cross_keep, cross_send, 1280, direct=False))
     self_grads = backward(True, self_plan, (qkv, 0), (qkv, 1), (qkv, 2), self_delta, self_mg, self_lse, tseg)
     for group in groups:
         group.start()

time: 266 us -> 266 us (level)
  waiting for transfers between devices: 20.2 us -> 26.2 us
  Pallas kernels: 153 us -> 150 us
    ppermute x33 -> x32, starting transfers between devices: 51.5 us -> 37.9 us  [across(): return lax.ppermute(x, 'wide', [(i, i ^ mask) for i in range(self.wide)])]
    ppermute x9, starting transfers between devices: 10.9 us -> 23.2 us  [exchange(): lax.ppermute(x, 'narrow', [(i, i ^ 1 << bit) for i in range(self.narrow)])]
    ppermute x33 -> x32, waiting for transfers between devices: 10.3 us -> 20.1 us  [across(): return lax.ppermute(x, 'wide', [(i, i ^ mask) for i in range(self.wide)])]
    ppermute x9, waiting for transfers between devices: 9.83 us -> 5.99 us  [exchange(): lax.ppermute(x, 'narrow', [(i, i ^ 1 << bit) for i in range(self.narrow)])]
  transfers between devices with their start and end apart: 43 -> 42, of which waited for: 13 -> 15; matrix products, arithmetic and copies ran while one was open for 3% -> 3% of each run, Pallas kernels for 41% -> 39%
where the time goes in v3:
time: 266 us; the launch traced here: 265 us
  Pallas kernels  150 us (56%)
  starting transfers between devices  61.1 us (23%)
  waiting for transfers between devices  26.2 us (10%)
  between operations  15 us (6%)
  local copies, waits for them, and re-layouts  7.12 us (3%)
  other arithmetic  5.84 us (2%)
    pallas_call x1, Pallas kernels, middle(): pl.pallas_call(mid_kernel, grid=(total // t,), in_specs=[smem(), smem(),...  43.8 us
    ppermute x32, starting transfers between devices, across(): return lax.ppermute(x, 'wide', [(i, i ^ mask) for i in range(self.wide)])  37.9 us
    pallas_call x2, Pallas kernels, attend_back(): pl.pallas_call(functools.partial(back_kernel, causal), grid=(rows,), in_s...  37.6 us
    ppermute x9, starting transfers between devices, exchange(): lax.ppermute(x, 'narrow', [(i, i ^ 1 << bit) for i in range(self.narrow)])  23.2 us
    pallas_call x1, Pallas kernels, cross_forward(): pl.pallas_call(cross_kernel, grid=(rows,), in_specs=[smem(), smem(), tile...  20.6 us
    ppermute x32, waiting for transfers between devices, across(): return lax.ppermute(x, 'wide', [(i, i ^ mask) for i in range(self.wide)])  20.1 us
    pallas_call x1, Pallas kernels, self_forward(): pl.pallas_call(self_kernel, grid=(rows,), in_specs=[smem(), smem(), tiled...  14.8 us
    pallas_call x1, Pallas kernels, cross_dense(): pl.pallas_call(cross_dense_kernel, grid=(total // t,), in_specs=[smem(),...  13 us
  transfers between devices with their start and end apart: 42, of which 15 were waited for; matrix products, arithmetic and copies ran while one was open for 3% of the time, Pallas kernels for 39%

profile of v3, /device:TPU:0, one launch (start us, length us, event | category | flops | bytes accessed | tf_op | source)
XLA Modules:
  0.0 265.2 jit_solution(11088887495081263538)
XLA Ops:
  7.3 1.9 pack.1
  9.2 5.1 %collective-permute-start.2 = (bf16[1,16,1664]{2,1,0:T(8,128)(2,1)}, bf16[1,16,1664]{2,1,0:T(8,128)(2,1)S(1)}, u32[]{:S(2)}, u32[]{:S(2)}) collective-permute-start(bf16[1,16,1664]{2,1,0:T(8,128)(2,1)} %get-tuple-element.99), channel_id=1, source_target_pairs={{0,24},{2,26},{4,28},{6,30},{8,16},{10,18},{12,20},{14,22},{16,8},... | collective-permute-start | bytes 159752 | tf_op jit(solution)/shard_map/ppermute | solution.py:680
  15.2 0.8 slice.235
  17.5 1.2 collective-permute-done.1
  18.7 1.2 collective-permute-done
  19.9 0.8 pad_maximum_fusion.4
  20.8 1.8 collective-permute-start.5
  22.8 2.4 collective-permute-start.3
  25.2 0.9 constant_dynamic-update-slice_fusion.4
  26.1 1.6 collective-permute-start.12
  27.7 1.5 collective-permute-start.8
  29.2 1.2 collective-permute-done.3
  30.4 0.9 pad_maximum_fusion.2
  31.3 1.6 collective-permute-start.6
  32.9 0.9 collective-permute-done.8
  33.8 1.1 collective-permute-start.9
  35.0 0.9 collective-permute-start.13
  36.4 4.3 %collective-permute-done.13.refs_5_ = bf16[8,16,768]{2,1,0:T(8,128)(2,1)S(1)} collective-permute-done((bf16[8,16,768]{2,1,0:T(8,128)(2,1)S(1)}, bf16[8,16,768]{2,1,0:T(8,128)(2,1)S(1)}, u32[]{:S(2)}, u32[]{:S(2)}) %collective-permute-start.13) | collective-permute-done | bytes 196640 | tf_op jit(solution)/shard_map/ppermute | solution.py:675
  41.3 1.2 collective-permute-start.7
  42.5 1.3 unpack.1
  43.8 14.8 %self_forward.1 = (bf16[2048,1536]{1,0:T(8,128)(2,1)}, bf16[2048,512]{1,0:T(8,128)(2,1)}, f32[2,8,1024]{2,1,0:T(8,128)S(1)}) custom-call(s32[2,8]{1,0:T(2,128)S(1)} %broadcast.63.first_ref, s32[2,8]{1,0:T(2,128)S(1)} %and_select_fusion.2.extra_ref, bf16[2048,512]{1,0:T(8,128)(2,1)S(1)} %copy-done.2, bf16[512,1536]{1,0:T(8,128)(2,1)S(1)} %get-tuple-element.109.w_ref, ...), custom_call_target="tpu_custom_call" | custom-call | flops 20000000000 | bytes 1048576 | tf_op jit(solution)/shard_map/self_forward/pallas_call | solution.py:253
  59.3 2.1 collective-permute-done.16.refs_2_
  61.4 0.9 collective-permute-done.17.refs_3_
  62.3 2.0 place.1.wo_ref.wq_ref.wkv_ref.w_ref
  64.3 20.6 %cross_forward.1 = (bf16[2048,512]{1,0:T(8,128)(2,1)}, bf16[2048,512]{1,0:T(8,128)(2,1)}, bf16[2048,1024]{1,0:T(8,128)(2,1)}, bf16[2048,512]{1,0:T(8,128)(2,1)}, f32[2,8,1024]{2,1,0:T(8,128)}) custom-call(s32[2,8]{1,0:T(2,128)} %get-tuple-element.103.first_ref, s32[2,8]{1,0:T(2,128)} %get-tuple-element.104.extra_ref, bf16[2048,512]{1,0:T(8,128)(2,1)} %x_ref.5, ...), custom_call_target="tpu_custom_call" | custom-call | flops 24999999488 | bytes 1048576 | tf_op jit(solution)/shard_map/cross_forward/pallas_call | solution.py:282
  84.9 43.8 %middle.1 = (bf16[2048,512]{1,0:T(8,128)(2,1)}, bf16[2048,512]{1,0:T(8,128)(2,1)}, bf16[2048,512]{1,0:T(8,128)(2,1)}, f32[2,8,1024]{2,1,0:T(8,128)}, bf16[16,16,...) custom-call(s32[32]{0:T(128)} %copy-done.4, s32[32]{0:T(128)} %copy-done.6, ...), custom_call_target="tpu_custom_call" | custom-call | flops 40000000000 | bytes 1048576 | tf_op jit(solution)/shard_map/middle/pallas_call | solution.py:482
  129.0 20.1 %cross_back.1 = (bf16[2048,512]{1,0:T(8,128)(2,1)}, bf16[2048,512]{1,0:T(8,128)(2,1)}, bf16[2048,512]{1,0:T(8,128)(2,1)}) custom-call(s32[2,8]{1,0:T(2,128)} %get-tuple-element.103.first_ref, s32[2,8]{1,0:T(2,128)} %get-tuple-element.104.extra_ref, bf16[2048,512]{1,0:T(8,128)(2,1)} %get-tuple-element.125.q_ref, ...), custom_call_target="tpu_custom_call" | custom-call | flops 20000000000 | bytes 1048576 | tf_op jit(solution)/shard_map/cross_back/pallas_call | solution.py:365
  150.0 4.8 %collective-permute-start.20 = (bf16[8,16,2048]{2,1,0:T(8,128)(2,1)S(1)}, bf16[8,16,2048]{2,1,0:T(8,128)(2,1)S(1)}, u32[]{:S(2)}, u32[]{:S(2)}) collective-permute-start(bf16[8,16,2048]{2,1,0:T(8,128)(2,1)S(1)} %get-tuple-element.184), channel_id=1, source_target_pairs={{0,1},{1,0},{2,3},{3,2},{4,5},{5,4},{6,7},{7,6},{8,9},{9,8},{10,11... | collective-permute-start | bytes 1572872 | tf_op jit(solution)/shard_map/ppermute | solution.py:675
  154.9 13.0 %cross_dense.1 = (bf16[2048,512]{1,0:T(8,128)(2,1)S(1)}, bf16[2048,512]{1,0:T(8,128)(2,1)S(1)}, f32[2,8,1024]{2,1,0:T(8,128)S(1)}, bf16[16,16,2560]{2,1,0:T(8,12...) custom-call(s32[32]{0:T(128)S(1)} %copy-done.5, s32[32]{0:T(128)S(1)} %copy-done.7, ...), custom_call_target="tpu_custom_call" | custom-call | flops 12000000000 | bytes 1048576 | tf_op jit(solution)/shard_map/cross_dense/pallas_call | solution.py:543
  168.4 2.4 collective-permute-start.21
  170.8 17.5 %self_back.1 = (bf16[2048,512]{1,0:T(8,128)(2,1)S(1)}, bf16[2048,512]{1,0:T(8,128)(2,1)S(1)}, bf16[2048,512]{1,0:T(8,128)(2,1)S(1)}) custom-call(s32[2,8]{1,0:T(2,128)S(1)} %broadcast.63.first_ref, s32[2,8]{1,0:T(2,128)S(1)} %and_select_fusion.2.extra_ref, bf16[2048,1536]{1,0:T(8,128)(2,1)} %get-tuple-element.149.q_ref.k_ref.v_ref, ...), custom_call_target="tpu_custom_call" | custom-call | flops 20000000000 | bytes 1048576 | tf_op jit(solution)/shard_map/self_back/pallas_call | solution.py:365
  188.6 11.1 %collective-permute-start.26 = (bf16[1,16,4096]{2,1,0:T(8,128)(2,1)S(1)}, bf16[1,16,4096]{2,1,0:T(8,128)(2,1)S(1)}, u32[]{:S(2)}, u32[]{:S(2)}) collective-permute-start(bf16[1,16,4096]{2,1,0:T(8,128)(2,1)S(1)} %get-tuple-element.190), channel_id=1, source_target_pairs={{0,24},{2,26},{4,28},{6,30},{8,16},{10,18},{12,20},{14,22},{16,8},... | collective-permute-start | bytes 393224 | tf_op jit(solution)/shard_map/ppermute | solution.py:680
  200.8 9.8 %collective-permute-start.28 = (bf16[8,16,1280]{2,1,0:T(8,128)(2,1)S(1)}, bf16[8,16,1280]{2,1,0:T(8,128)(2,1)S(1)}, u32[]{:S(2)}, u32[]{:S(2)}) collective-permute-start(bf16[8,16,1280]{2,1,0:T(8,128)(2,1)S(1)} %get-tuple-element.188), channel_id=1, source_target_pairs={{0,1},{1,0},{2,3},{3,2},{4,5},{5,4},{6,7},{7,6},{8,9},{9,8},{10,11... | collective-permute-start | bytes 983048 | tf_op jit(solution)/shard_map/ppermute | solution.py:675
  210.6 6.3 %self_grad.1 = (bf16[16,16,1664]{2,1,0:T(8,128)(2,1)S(1)}, bf16[16,16,1664]{2,1,0:T(8,128)(2,1)S(1)}, f32[16,2048]{1,0:T(8,128)}) custom-call(s32[32]{0:T(128)S(1)} %copy-done.5, s32[32]{0:T(128)S(1)} %copy-done.7, bf16[2048,512]{1,0:T(8,128)(2,1)S(1)} %get-tuple-element.156.dq_ref, bf16[2048,512]{1,0:T(8,128)(2,1)S(1)} %get-tuple-element.157.dk_ref, ...), custom_call_target="tpu_custom_call" | custom-call | flops 5000000000 | bytes 1048576 | tf_op jit(solution)/shard_map/self_grad/pallas_call | solution.py:631
  216.9 2.5 collective-permute-done.27
  221.2 3.7 %collective-permute-done.30 = bf16[4,16,1280]{2,1,0:T(8,128)(2,1)S(1)} collective-permute-done((bf16[4,16,1280]{2,1,0:T(8,128)(2,1)S(1)}, bf16[4,16,1280]{2,1,0:T(8,128)(2,1)S(1)}, u32[]{:S(2)}, u32[]{:S(2)}) %collective-permute-start.30) | collective-permute-done | bytes 163872 | tf_op jit(solution)/shard_map/ppermute | solution.py:680
  225.0 0.8 collective-permute-done.29
  226.2 2.1 collective-permute-start.33
  228.3 1.4 collective-permute-start.32
  229.7 4.9 %target_grad.1 = bf16[2048,512]{1,0:T(8,128)(2,1)} custom-call(bf16[2048,512]{1,0:T(8,128)(2,1)S(1)} %get-tuple-element.145.h1_ref, bf16[2048,512]{1,0:T(8,128)(2,1)S(1)} %get-tuple-element.156.dq_ref, bf16[2048,512]{1,0:T(8,128)(2,1)S(1)} %get-tuple-element.157.dk_ref, bf16[2048,512]{1,0:T(8,128)(2,1)S(1)} %get-tuple-element.158.dv_ref, ...), custom_call_target="tpu_custom_call" | custom-call | flops 5000000000 | bytes 1048576 | tf_op jit(solution)/shard_map/target_grad/pallas_call | solution.py:651
  234.7 2.0 collective-permute-start.35
  236.9 3.9 %memory_grad.1 = bf16[2048,512]{1,0:T(8,128)(2,1)} custom-call(bf16[2048,512]{1,0:T(8,128)(2,1)S(1)} %copy-done.10, bf16[2048,512]{1,0:T(8,128)(2,1)S(1)} %copy-done.12, bf16[512,2048]{1,0:T(8,128)(2,1)S(1)} %copy-done.8, bf16[1,16,2560]{2,1,0:T(8,128)(2,1)S(1)} %get-tuple-element.173.refs_0_, bf16[4,16,768]{2,1,0:T(8,128)(2,1)S(1)} %slice.322.refs_1_, ...), custom_call_target="tpu_custom_call" | custom-call | flops 4000000000 | bytes 1048576 | tf_op jit(solution)/shard_map/memory_grad/pallas_call | solution.py:561
  240.8 2.9 %collective-permute-start.40 = (bf16[1,16,2560]{2,1,0:T(8,128)(2,1)S(1)}, bf16[1,16,2560]{2,1,0:T(8,128)(2,1)S(1)}, u32[]{:S(2)}, u32[]{:S(2)}) collective-permute-start(bf16[1,16,2560]{2,1,0:T(8,128)(2,1)S(1)} %get-tuple-element.173.refs_0_), channel_id=1, source_target_pairs={{0,16},{2,18},{4,20},{6,22},{8,24},{10,26},{12,28},{14,30},{16,0},... | collective-permute-start | bytes 245768 | tf_op jit(solution)/shard_map/ppermute | solution.py:680
  243.8 3.2 %collective-permute-done.40 = bf16[1,16,2560]{2,1,0:T(8,128)(2,1)S(1)} collective-permute-done((bf16[1,16,2560]{2,1,0:T(8,128)(2,1)S(1)}, bf16[1,16,2560]{2,1,0:T(8,128)(2,1)S(1)}, u32[]{:S(2)}, u32[]{:S(2)}) %collective-permute-start.40) | collective-permute-done | bytes 81952 | tf_op jit(solution)/shard_map/ppermute | solution.py:680
  247.1 1.5 collective-permute-done.36
  248.6 0.8 collective-permute-start.37
  249.4 2.1 collective-permute-start.39
  254.2 1.2 collective-permute-done.39
  (163 shorter events, 15.4 us)
Async XLA Ops:
  7.2 77.7 %all-gather.2.cloned.1.call-start = ((), (), s32[]{:S(2)}) async-start(), calls=%async_computation | async-start | bytes 4866048 | tf_op jit(solution)/shard_map/all_gather | solution.py:763
  9.2 8.3 %collective-permute-start.2 = (bf16[1,16,1664]{2,1,0:T(8,128)(2,1)}, bf16[1,16,1664]{2,1,0:T(8,128)(2,1)S(1)}, u32[]{:S(2)}, u32[]{:S(2)}) collective-permute-start(bf16[1,16,1664]{2,1,0:T(8,128)(2,1)} %get-tuple-element.99), channel_id=1, source_target_pairs={{0,24},{2,26},{4,28},{6,30},{8,16},{10,18},{12,20},{14,22},{16,8},... | collective-permute-start | bytes 159752 | tf_op jit(solution)/shard_map/ppermute | solution.py:680
  14.3 4.4 %collective-permute-start.1 = (bf16[1,16,1664]{2,1,0:T(8,128)(2,1)}, bf16[1,16,1664]{2,1,0:T(8,128)(2,1)S(1)}, u32[]{:S(2)}, u32[]{:S(2)}) collective-permute-start(bf16[1,16,1664]{2,1,0:T(8,128)(2,1)} %get-tuple-element.99), channel_id=1, source_target_pairs={{0,8},{2,10},{4,12},{6,14},{8,0},{10,2},{12,4},{14,6},{16,24},{18,... | collective-permute-start | bytes 159752 | tf_op jit(solution)/shard_map/ppermute | solution.py:680
  14.3 5.6 %collective-permute-start = (bf16[1,16,1664]{2,1,0:T(8,128)(2,1)}, bf16[1,16,1664]{2,1,0:T(8,128)(2,1)S(1)}, u32[]{:S(2)}, u32[]{:S(2)}) collective-permute-start(bf16[1,16,1664]{2,1,0:T(8,128)(2,1)} %get-tuple-element.99), channel_id=1, source_target_pairs={{0,16},{2,18},{4,20},{6,22},{8,24},{10,26},{12,28},{14,30},{16,0},... | collective-permute-start | bytes 159752 | tf_op jit(solution)/shard_map/ppermute | solution.py:680
  16.2 46.1 %copy-start.4 = (s32[32]{0:T(128)}, s32[32]{0:T(128)S(1)}, u32[]{:S(2)}) copy-start(s32[32]{0:T(128)S(1)} %broadcast_xor_fusion.1.index_a.index) | copy-start | bytes 388
  16.9 26.9 %copy-start.6 = (s32[32]{0:T(128)}, s32[32]{0:T(128)S(1)}, u32[]{:S(2)}) copy-start(s32[32]{0:T(128)S(1)} %broadcast_xor_fusion.index_b) | copy-start | bytes 388
  16.9 26.9 %copy-start = (f32[2,1,1024]{2,1,0:T(1,128)}, f32[2,1,1024]{2,1,0:T(1,128)S(1)}, u32[]{:S(2)}) copy-start(f32[2,1,1024]{2,1,0:T(1,128)S(1)} %broadcast_in_dim.58.seg_ref.qseg_ref.kseg_ref) | copy-start | bytes 24580
  20.8 8.4 %collective-permute-start.5 = (bf16[1,16,2048]{2,1,0:T(8,128)(2,1)}, bf16[1,16,2048]{2,1,0:T(8,128)(2,1)S(1)}, u32[]{:S(2)}, u32[]{:S(2)}) collective-permute-start(bf16[1,16,2048]{2,1,0:T(8,128)(2,1)} %get-tuple-element.105), channel_id=1, source_target_pairs={{0,24},{2,26},{4,28},{6,30},{8,16},{10,18},{12,20},{14,22},{16,8},... | collective-permute-start | bytes 196616 | tf_op jit(solution)/shard_map/ppermute | solution.py:680
  22.5 6.7 %collective-permute-start.4 = (bf16[1,16,2048]{2,1,0:T(8,128)(2,1)}, bf16[1,16,2048]{2,1,0:T(8,128)(2,1)S(1)}, u32[]{:S(2)}, u32[]{:S(2)}) collective-permute-start(bf16[1,16,2048]{2,1,0:T(8,128)(2,1)} %get-tuple-element.105), channel_id=1, source_target_pairs={{0,8},{2,10},{4,12},{6,14},{8,0},{10,2},{12,4},{14,6},{16,24},{18,... | collective-permute-start | bytes 196616 | tf_op jit(solution)/shard_map/ppermute | solution.py:680
  22.8 7.7 %collective-permute-start.3 = (bf16[1,16,2048]{2,1,0:T(8,128)(2,1)}, bf16[1,16,2048]{2,1,0:T(8,128)(2,1)S(1)}, u32[]{:S(2)}, u32[]{:S(2)}) collective-permute-start(bf16[1,16,2048]{2,1,0:T(8,128)(2,1)} %get-tuple-element.105), channel_id=1, source_target_pairs={{0,16},{2,18},{4,20},{6,22},{8,24},{10,26},{12,28},{14,30},{16,0},... | collective-permute-start | bytes 196616 | tf_op jit(solution)/shard_map/ppermute | solution.py:680
  26.1 8.8 %collective-permute-start.12 = (bf16[4,16,768]{2,1,0:T(8,128)(2,1)S(1)}, bf16[4,16,768]{2,1,0:T(8,128)(2,1)S(1)}, u32[]{:S(2)}, u32[]{:S(2)}) collective-permute-start(bf16[4,16,768]{2,1,0:T(8,128)(2,1)S(1)} %slice.239), channel_id=1, source_target_pairs={{0,4},{2,6},{4,0},{6,2},{8,12},{10,14},{12,8},{14,10},{16,20},{18,... | collective-permute-start | bytes 294920 | tf_op jit(solution)/shard_map/ppermute | solution.py:680
  27.7 6.1 %collective-permute-start.8 = (bf16[4,16,896]{2,1,0:T(8,128)(2,1)S(1)}, bf16[4,16,896]{2,1,0:T(8,128)(2,1)S(1)}, u32[]{:S(2)}, u32[]{:S(2)}) collective-permute-start(bf16[4,16,896]{2,1,0:T(8,128)(2,1)S(1)} %slice.238), channel_id=1, source_target_pairs={{0,1},{1,0},{2,3},{3,2},{4,5},{5,4},{6,7},{7,6},{8,9},{9,8},{10,11... | collective-permute-start | bytes 344072 | tf_op jit(solution)/shard_map/ppermute | solution.py:675
  31.3 9.9 %collective-permute-start.6 = (bf16[4,16,2048]{2,1,0:T(8,128)(2,1)S(1)}, bf16[4,16,2048]{2,1,0:T(8,128)(2,1)S(1)}, u32[]{:S(2)}, u32[]{:S(2)}) collective-permute-start(bf16[4,16,2048]{2,1,0:T(8,128)(2,1)S(1)} %pad_maximum_fusion.2), channel_id=1, source_target_pairs={{0,1},{1,0},{2,3},{3,2},{4,5},{5,4},{6,7},{7,6},{8,9},{9,8},{10,11... | collective-permute-start | bytes 786440 | tf_op jit(solution)/shard_map/ppermute | solution.py:675
  33.8 6.9 %collective-permute-start.9 = (bf16[8,16,896]{2,1,0:T(8,128)(2,1)S(1)}, bf16[8,16,896]{2,1,0:T(8,128)(2,1)S(1)}, u32[]{:S(2)}, u32[]{:S(2)}) collective-permute-start(bf16[8,16,896]{2,1,0:T(8,128)(2,1)S(1)} %pad_maximum_fusion.3.refs_0_), channel_id=1, source_target_pairs={{0,4},{2,6},{4,0},{6,2},{8,12},{10,14},{12,8},{14,10},{16,20},{18,... | collective-permute-start | bytes 688136 | tf_op jit(solution)/shard_map/ppermute | solution.py:680
  35.0 5.7 %collective-permute-start.13 = (bf16[8,16,768]{2,1,0:T(8,128)(2,1)S(1)}, bf16[8,16,768]{2,1,0:T(8,128)(2,1)S(1)}, u32[]{:S(2)}, u32[]{:S(2)}) collective-permute-start(bf16[8,16,768]{2,1,0:T(8,128)(2,1)S(1)} %pad_maximum_fusion.5.refs_4_), channel_id=1, source_target_pairs={{0,1},{1,0},{2,3},{3,2},{4,5},{5,4},{6,7},{7,6},{8,9},{9,8},{10,11... | collective-permute-start | bytes 589832 | tf_op jit(solution)/shard_map/ppermute | solution.py:675
  35.9 6.6 %collective-permute-start.14 = (bf16[8,16,768]{2,1,0:T(8,128)(2,1)S(1)}, bf16[8,16,768]{2,1,0:T(8,128)(2,1)S(1)}, u32[]{:S(2)}, u32[]{:S(2)}) collective-permute-start(bf16[8,16,768]{2,1,0:T(8,128)(2,1)S(1)} %pad_maximum_fusion.5.refs_4_), channel_id=1, source_target_pairs={{0,2},{2,0},{4,6},{6,4},{8,10},{10,8},{12,14},{14,12},{16,18},{18,... | collective-permute-start | bytes 589832 | tf_op jit(solution)/shard_map/ppermute | solution.py:680
  35.9 6.6 %collective-permute-start.10 = (bf16[8,16,896]{2,1,0:T(8,128)(2,1)S(1)}, bf16[8,16,896]{2,1,0:T(8,128)(2,1)S(1)}, u32[]{:S(2)}, u32[]{:S(2)}) collective-permute-start(bf16[8,16,896]{2,1,0:T(8,128)(2,1)S(1)} %pad_maximum_fusion.3.refs_0_), channel_id=1, source_target_pairs={{0,2},{2,0},{4,6},{6,4},{8,10},{10,8},{12,14},{14,12},{16,18},{18,... | collective-permute-start | bytes 688136 | tf_op jit(solution)/shard_map/ppermute | solution.py:680
  40.7 1.8 collective-permute-start.15
  40.7 1.8 collective-permute-start.11
  41.3 17.4 %collective-permute-start.7 = (bf16[8,16,2048]{2,1,0:T(8,128)(2,1)S(1)}, bf16[8,16,2048]{2,1,0:T(8,128)(2,1)S(1)}, u32[]{:S(2)}, u32[]{:S(2)}) collective-permute-start(bf16[8,16,2048]{2,1,0:T(8,128)(2,1)S(1)} %constant_dynamic-update-slice_fusion.refs_0_), channel_id=1, source_target_pairs={{0,4},{2,6},{4,0},{6,2},{8,12},{10,14},{12,8},{14,10},{16,20},{18,... | collective-permute-start | bytes 1572872 | tf_op jit(solution)/shard_map/ppermute | solution.py:680
  43.8 14.9 %copy-start.13 = (f32[16,2048]{1,0:T(8,128)}, f32[16,2048]{1,0:T(8,128)S(1)}, u32[]{:S(2)}) copy-start(f32[16,2048]{1,0:T(8,128)S(1)} %get-tuple-element.110.vec_ref) | copy-start | bytes 393220
  58.7 2.7 %collective-permute-start.16 = (bf16[8,16,2048]{2,1,0:T(8,128)(2,1)S(1)}, bf16[8,16,2048]{2,1,0:T(8,128)(2,1)S(1)}, u32[]{:S(2)}, u32[]{:S(2)}) collective-permute-start(bf16[8,16,2048]{2,1,0:T(8,128)(2,1)S(1)} %constant_dynamic-update-slice_fusion.refs_0_), channel_id=1, source_target_pairs={{0,2},{2,0},{4,6},{6,4},{8,10},{10,8},{12,14},{14,12},{16,18},{18,... | collective-permute-start | bytes 1572872 | tf_op jit(solution)/shard_map/ppermute | solution.py:680
  59.0 3.4 %collective-permute-start.17 = (bf16[8,16,2048]{2,1,0:T(8,128)(2,1)S(1)}, bf16[8,16,2048]{2,1,0:T(8,128)(2,1)S(1)}, u32[]{:S(2)}, u32[]{:S(2)}) collective-permute-start(bf16[8,16,2048]{2,1,0:T(8,128)(2,1)S(1)} %collective-permute-done.7.refs_1_), channel_id=1, source_target_pairs={{0,2},{2,0},{4,6},{6,4},{8,10},{10,8},{12,14},{14,12},{16,18},{18,... | collective-permute-start | bytes 1572872 | tf_op jit(solution)/shard_map/ppermute | solution.py:680
  128.7 20.4 %collective-permute-start.18 = (bf16[16,16,4096]{2,1,0:T(8,128)(2,1)}, bf16[16,16,4096]{2,1,0:T(8,128)(2,1)S(1)}, u32[]{:S(2)}, u32[]{:S(2)}) collective-permute-start(bf16[16,16,4096]{2,1,0:T(8,128)(2,1)} %get-tuple-element.124.refs_0_), channel_id=1, source_target_pairs={{0,2},{2,0},{4,6},{6,4},{8,10},{10,8},{12,14},{14,12},{16,18},{18,... | collective-permute-start | bytes 6291464 | tf_op jit(solution)/shard_map/ppermute | solution.py:680
  129.0 20.1 %copy-start.18 = (bf16[16,16,4096]{2,1,0:T(8,128)(2,1)S(1)}, bf16[16,16,4096]{2,1,0:T(8,128)(2,1)}, u32[]{:S(2)}) copy-start(bf16[16,16,4096]{2,1,0:T(8,128)(2,1)} %get-tuple-element.123) | copy-start | bytes 6291460
  150.0 17.9 %collective-permute-start.20 = (bf16[8,16,2048]{2,1,0:T(8,128)(2,1)S(1)}, bf16[8,16,2048]{2,1,0:T(8,128)(2,1)S(1)}, u32[]{:S(2)}, u32[]{:S(2)}) collective-permute-start(bf16[8,16,2048]{2,1,0:T(8,128)(2,1)S(1)} %get-tuple-element.184), channel_id=1, source_target_pairs={{0,1},{1,0},{2,3},{3,2},{4,5},{5,4},{6,7},{7,6},{8,9},{9,8},{10,11... | collective-permute-start | bytes 1572872 | tf_op jit(solution)/shard_map/ppermute | solution.py:675
  154.8 13.1 %collective-permute-start.19 = (bf16[8,16,2048]{2,1,0:T(8,128)(2,1)S(1)}, bf16[8,16,2048]{2,1,0:T(8,128)(2,1)S(1)}, u32[]{:S(2)}, u32[]{:S(2)}) collective-permute-start(bf16[8,16,2048]{2,1,0:T(8,128)(2,1)S(1)} %get-tuple-element.185), channel_id=1, source_target_pairs={{0,4},{2,6},{4,0},{6,2},{8,12},{10,14},{12,8},{14,10},{16,20},{18,... | collective-permute-start | bytes 1572872 | tf_op jit(solution)/shard_map/ppermute | solution.py:680
  168.4 19.9 %collective-permute-start.21 = (bf16[4,16,2048]{2,1,0:T(8,128)(2,1)S(1)}, bf16[4,16,2048]{2,1,0:T(8,128)(2,1)S(1)}, u32[]{:S(2)}, u32[]{:S(2)}) collective-permute-start(bf16[4,16,2048]{2,1,0:T(8,128)(2,1)S(1)} %slice.299.refs_0_), channel_id=1, source_target_pairs={{0,1},{1,0},{2,3},{3,2},{4,5},{5,4},{6,7},{7,6},{8,9},{9,8},{10,11... | collective-permute-start | bytes 786440 | tf_op jit(solution)/shard_map/ppermute | solution.py:675
  170.8 17.5 %collective-permute-start.22 = (bf16[4,16,2048]{2,1,0:T(8,128)(2,1)S(1)}, bf16[4,16,2048]{2,1,0:T(8,128)(2,1)S(1)}, u32[]{:S(2)}, u32[]{:S(2)}) collective-permute-start(bf16[4,16,2048]{2,1,0:T(8,128)(2,1)S(1)} %slice.301.refs_1_), channel_id=1, source_target_pairs={{0,4},{2,6},{4,0},{6,2},{8,12},{10,14},{12,8},{14,10},{16,20},{18,... | collective-permute-start | bytes 786440 | tf_op jit(solution)/shard_map/ppermute | solution.py:680
  170.8 17.5 %collective-permute-start.23 = (bf16[16,16,2560]{2,1,0:T(8,128)(2,1)S(1)}, bf16[16,16,2560]{2,1,0:T(8,128)(2,1)S(1)}, u32[]{:S(2)}, u32[]{:S(2)}) collective-permute-start(bf16[16,16,2560]{2,1,0:T(8,128)(2,1)S(1)} %get-tuple-element.148.refs_2_), channel_id=1, source_target_pairs={{0,2},{2,0},{4,6},{6,4},{8,10},{10,8},{12,14},{14,12},{16,18},{18,... | collective-permute-start | bytes 3932168 | tf_op jit(solution)/shard_map/ppermute | solution.py:680
  188.6 28.3 %collective-permute-start.26 = (bf16[1,16,4096]{2,1,0:T(8,128)(2,1)S(1)}, bf16[1,16,4096]{2,1,0:T(8,128)(2,1)S(1)}, u32[]{:S(2)}, u32[]{:S(2)}) collective-permute-start(bf16[1,16,4096]{2,1,0:T(8,128)(2,1)S(1)} %get-tuple-element.190), channel_id=1, source_target_pairs={{0,24},{2,26},{4,28},{6,30},{8,16},{10,18},{12,20},{14,22},{16,8},... | collective-permute-start | bytes 393224 | tf_op jit(solution)/shard_map/ppermute | solution.py:680
  199.7 17.2 %collective-permute-start.25 = (bf16[1,16,4096]{2,1,0:T(8,128)(2,1)S(1)}, bf16[1,16,4096]{2,1,0:T(8,128)(2,1)S(1)}, u32[]{:S(2)}, u32[]{:S(2)}) collective-permute-start(bf16[1,16,4096]{2,1,0:T(8,128)(2,1)S(1)} %get-tuple-element.191), channel_id=1, source_target_pairs={{0,8},{2,10},{4,12},{6,14},{8,0},{10,2},{12,4},{14,6},{16,24},{18,... | collective-permute-start | bytes 393224 | tf_op jit(solution)/shard_map/ppermute | solution.py:680
  199.7 10.9 %copy-start.17 = (f32[8,2048]{1,0:T(8,128)S(1)}, f32[8,2048]{1,0:T(8,128)}, u32[]{:S(2)}) copy-start(f32[8,2048]{1,0:T(8,128)} %get-tuple-element.163.mid_ref) | copy-start | bytes 196612
  199.7 17.2 %collective-permute-start.24 = (bf16[1,16,4096]{2,1,0:T(8,128)(2,1)S(1)}, bf16[1,16,4096]{2,1,0:T(8,128)(2,1)S(1)}, u32[]{:S(2)}, u32[]{:S(2)}) collective-permute-start(bf16[1,16,4096]{2,1,0:T(8,128)(2,1)S(1)} %get-tuple-element.192), channel_id=1, source_target_pairs={{0,16},{2,18},{4,20},{6,22},{8,24},{10,26},{12,28},{14,30},{16,0},... | collective-permute-start | bytes 393224 | tf_op jit(solution)/shard_map/ppermute | solution.py:680
  200.8 16.1 %collective-permute-start.28 = (bf16[8,16,1280]{2,1,0:T(8,128)(2,1)S(1)}, bf16[8,16,1280]{2,1,0:T(8,128)(2,1)S(1)}, u32[]{:S(2)}, u32[]{:S(2)}) collective-permute-start(bf16[8,16,1280]{2,1,0:T(8,128)(2,1)S(1)} %get-tuple-element.188), channel_id=1, source_target_pairs={{0,1},{1,0},{2,3},{3,2},{4,5},{5,4},{6,7},{7,6},{8,9},{9,8},{10,11... | collective-permute-start | bytes 983048 | tf_op jit(solution)/shard_map/ppermute | solution.py:675
  210.6 8.8 %collective-permute-start.27 = (bf16[8,16,1280]{2,1,0:T(8,128)(2,1)S(1)}, bf16[8,16,1280]{2,1,0:T(8,128)(2,1)S(1)}, u32[]{:S(2)}, u32[]{:S(2)}) collective-permute-start(bf16[8,16,1280]{2,1,0:T(8,128)(2,1)S(1)} %get-tuple-element.189), channel_id=1, source_target_pairs={{0,4},{2,6},{4,0},{6,2},{8,12},{10,14},{12,8},{14,10},{16,20},{18,... | collective-permute-start | bytes 983048 | tf_op jit(solution)/shard_map/ppermute | solution.py:680
  219.6 5.4 %collective-permute-start.30 = (bf16[4,16,1280]{2,1,0:T(8,128)(2,1)S(1)}, bf16[4,16,1280]{2,1,0:T(8,128)(2,1)S(1)}, u32[]{:S(2)}, u32[]{:S(2)}) collective-permute-start(bf16[4,16,1280]{2,1,0:T(8,128)(2,1)S(1)} %slice.314), channel_id=1, source_target_pairs={{0,4},{2,6},{4,0},{6,2},{8,12},{10,14},{12,8},{14,10},{16,20},{18,... | collective-permute-start | bytes 491528 | tf_op jit(solution)/shard_map/ppermute | solution.py:680
  220.4 5.4 %collective-permute-start.29 = (bf16[4,16,1280]{2,1,0:T(8,128)(2,1)S(1)}, bf16[4,16,1280]{2,1,0:T(8,128)(2,1)S(1)}, u32[]{:S(2)}, u32[]{:S(2)}) collective-permute-start(bf16[4,16,1280]{2,1,0:T(8,128)(2,1)S(1)} %slice.311), channel_id=1, source_target_pairs={{0,1},{1,0},{2,3},{3,2},{4,5},{5,4},{6,7},{7,6},{8,9},{9,8},{10,11... | collective-permute-start | bytes 491528 | tf_op jit(solution)/shard_map/ppermute | solution.py:675
  220.6 5.4 %collective-permute-start.31 = (bf16[16,16,1664]{2,1,0:T(8,128)(2,1)S(1)}, bf16[16,16,1664]{2,1,0:T(8,128)(2,1)S(1)}, u32[]{:S(2)}, u32[]{:S(2)}) collective-permute-start(bf16[16,16,1664]{2,1,0:T(8,128)(2,1)S(1)} %get-tuple-element.170), channel_id=1, source_target_pairs={{0,2},{2,0},{4,6},{6,4},{8,10},{10,8},{12,14},{14,12},{16,18},{18,... | collective-permute-start | bytes 2555912 | tf_op jit(solution)/shard_map/ppermute | solution.py:680
  226.2 8.5 %collective-permute-start.33 = (bf16[8,16,768]{2,1,0:T(8,128)(2,1)S(1)}, bf16[8,16,768]{2,1,0:T(8,128)(2,1)S(1)}, u32[]{:S(2)}, u32[]{:S(2)}) collective-permute-start(bf16[8,16,768]{2,1,0:T(8,128)(2,1)S(1)} %slice.317.refs_1_), channel_id=1, source_target_pairs={{0,4},{2,6},{4,0},{6,2},{8,12},{10,14},{12,8},{14,10},{16,20},{18,... | collective-permute-start | bytes 589832 | tf_op jit(solution)/shard_map/ppermute | solution.py:680
  228.3 8.5 %collective-permute-start.34 = (bf16[8,16,896]{2,1,0:T(8,128)(2,1)S(1)}, bf16[8,16,896]{2,1,0:T(8,128)(2,1)S(1)}, u32[]{:S(2)}, u32[]{:S(2)}) collective-permute-start(bf16[8,16,896]{2,1,0:T(8,128)(2,1)S(1)} %slice.318.refs_2_), channel_id=1, source_target_pairs={{0,1},{1,0},{2,3},{3,2},{4,5},{5,4},{6,7},{7,6},{8,9},{9,8},{10,11... | collective-permute-start | bytes 688136 | tf_op jit(solution)/shard_map/ppermute | solution.py:675
  228.3 6.3 %collective-permute-start.32 = (bf16[2,16,2560]{2,1,0:T(8,128)(2,1)S(1)}, bf16[2,16,2560]{2,1,0:T(8,128)(2,1)S(1)}, u32[]{:S(2)}, u32[]{:S(2)}) collective-permute-start(bf16[2,16,2560]{2,1,0:T(8,128)(2,1)S(1)} %get-tuple-element.171.refs_0_), channel_id=1, source_target_pairs={{0,8},{2,10},{4,12},{6,14},{8,0},{10,2},{12,4},{14,6},{16,24},{18,... | collective-permute-start | bytes 491528 | tf_op jit(solution)/shard_map/ppermute | solution.py:680
  234.7 9.1 %collective-permute-start.35 = (bf16[4,16,768]{2,1,0:T(8,128)(2,1)S(1)}, bf16[4,16,768]{2,1,0:T(8,128)(2,1)S(1)}, u32[]{:S(2)}, u32[]{:S(2)}) collective-permute-start(bf16[4,16,768]{2,1,0:T(8,128)(2,1)S(1)} %slice.322.refs_1_), channel_id=1, source_target_pairs={{0,1},{1,0},{2,3},{3,2},{4,5},{5,4},{6,7},{7,6},{8,9},{9,8},{10,11... | collective-permute-start | bytes 294920 | tf_op jit(solution)/shard_map/ppermute | solution.py:675
  240.8 6.2 %collective-permute-start.40 = (bf16[1,16,2560]{2,1,0:T(8,128)(2,1)S(1)}, bf16[1,16,2560]{2,1,0:T(8,128)(2,1)S(1)}, u32[]{:S(2)}, u32[]{:S(2)}) collective-permute-start(bf16[1,16,2560]{2,1,0:T(8,128)(2,1)S(1)} %get-tuple-element.173.refs_0_), channel_id=1, source_target_pairs={{0,16},{2,18},{4,20},{6,22},{8,24},{10,26},{12,28},{14,30},{16,0},... | collective-permute-start | bytes 245768 | tf_op jit(solution)/shard_map/ppermute | solution.py:680
  243.7 4.8 %collective-permute-start.36 = (bf16[4,16,896]{2,1,0:T(8,128)(2,1)S(1)}, bf16[4,16,896]{2,1,0:T(8,128)(2,1)S(1)}, u32[]{:S(2)}, u32[]{:S(2)}) collective-permute-start(bf16[4,16,896]{2,1,0:T(8,128)(2,1)S(1)} %slice.324.refs_2_), channel_id=1, source_target_pairs={{0,4},{2,6},{4,0},{6,2},{8,12},{10,14},{12,8},{14,10},{16,20},{18,... | collective-permute-start | bytes 344072 | tf_op jit(solution)/shard_map/ppermute | solution.py:680
  248.6 5.5 %collective-permute-start.37 = (bf16[1,16,1664]{2,1,0:T(8,128)(2,1)S(1)}, bf16[1,16,1664]{2,1,0:T(8,128)(2,1)S(1)}, u32[]{:S(2)}, u32[]{:S(2)}) collective-permute-start(bf16[1,16,1664]{2,1,0:T(8,128)(2,1)S(1)} %get-tuple-element.199), channel_id=1, source_target_pairs={{0,16},{2,18},{4,20},{6,22},{8,24},{10,26},{12,28},{14,30},{16,0},... | collective-permute-start | bytes 159752 | tf_op jit(solution)/shard_map/ppermute | solution.py:680
  249.4 6.0 %collective-permute-start.39 = (bf16[1,16,1664]{2,1,0:T(8,128)(2,1)S(1)}, bf16[1,16,1664]{2,1,0:T(8,128)(2,1)S(1)}, u32[]{:S(2)}, u32[]{:S(2)}) collective-permute-start(bf16[1,16,1664]{2,1,0:T(8,128)(2,1)S(1)} %get-tuple-element.200), channel_id=1, source_target_pairs={{0,24},{2,26},{4,28},{6,30},{8,16},{10,18},{12,20},{14,22},{16,8},... | collective-permute-start | bytes 159752 | tf_op jit(solution)/shard_map/ppermute | solution.py:680
  251.5 4.4 %collective-permute-start.38 = (bf16[1,16,1664]{2,1,0:T(8,128)(2,1)S(1)}, bf16[1,16,1664]{2,1,0:T(8,128)(2,1)S(1)}, u32[]{:S(2)}, u32[]{:S(2)}) collective-permute-start(bf16[1,16,1664]{2,1,0:T(8,128)(2,1)S(1)} %get-tuple-element.201), channel_id=1, source_target_pairs={{0,8},{2,10},{4,12},{6,14},{8,0},{10,2},{12,4},{14,6},{16,24},{18,... | collective-permute-start | bytes 159752 | tf_op jit(solution)/shard_map/ppermute | solution.py:680
  (17 other events, 105.7 us)
Sparse Core Ops, SparseCore 0:
  11.5 67.7 all-gather.1
